TPU v7x, 32 devices: a whole 2x2x4 slice. The times are simulated.
32 devices in a mesh: grp: 2 (over x), row: 16 (over z, y, core).
Axes of the slice: x: 2, y: 2, z: 4, core: 2. Of those that a mesh axis runs over, the one named last changes fastest.
Arguments:
- tile_blocks: bfloat16 [576, 128, 128], P(('grp', 'row')), parts along dimension 0, may hold values from 0 to 1
- q_block: bfloat16 [8192, 128], P(('grp', 'row')), parts along dimension 0, may hold values from -6 to 6
- tile_index: int32 [576, 2], P(('grp', 'row')), parts along dimension 0, may hold values from 0 to 31, as said below
- tile_count: int32 [64], P(('grp', 'row')), parts along dimension 0, may hold values from 1 to 9, as said below
Outputs:
- product: float32 [8192, 128], P(('grp', 'row')), parts along dimension 0
There are 2 independent parts, one for each index of `grp`. A program takes and returns all parts, laid end to end along the dimension named above; each array names one. Nothing has to cross between parts.
Inputs may be any that keep to these rules, and one draw needn't show every extreme that they name: `tile_index`: block rows of a device are 2 d and 2 d + 1; its live slots come first, those of its first block row before those of its second; every live slot has i equal to one of the device's block rows and j >= i, and the live (i, j) of a block row are distinct and include (i, i). Dead slots hold indices of the same form. Device 0 has all 18 slots live. `tile_count`: the sum over a device's 2 block rows is at most 18; block row i has at most 32 - i tiles.
All inputs are finite; a program needn't handle non-finite values.
Results may differ from a plain program's by a relative error of at most 0.0003.
Values may be sent and summed in bfloat16 or wider, within the bound.
No kernel may reach another device: no remote copies, remote signals or barrier semaphores. Data moves between devices by JAX's collectives and lax.ppermute only.
A program may use at most 128 MiB of HBM per device.

v0:
```python
import math

import jax
import jax.numpy as jnp
from jax import lax
from jax.sharding import PartitionSpec as P


def on_device(tile_blocks, q_block, tile_index, tile_count):
    slot_total = tile_blocks.shape[0]
    tile_size = tile_blocks.shape[1]
    row_count = q_block.shape[0]
    columns = q_block.shape[1]
    local_blocks = row_count // tile_size
    gathered = lax.all_gather(q_block, "row", axis=0, tiled=True)
    node_total = gathered.shape[0]
    block_total = node_total // tile_size
    remote_basis = gathered.reshape(block_total, tile_size, columns)
    own_basis = q_block.reshape(local_blocks, tile_size, columns)
    live_total = jnp.sum(tile_count)
    row_local = tile_index[:, 0] % local_blocks
    col_block = tile_index[:, 1]
    live_mask = (jnp.arange(slot_total) < live_total).astype(jnp.float32)[:, None, None]
    group_size = -(-slot_total // 8)
    own_sum = jnp.zeros((local_blocks, tile_size, columns), jnp.float32)
    mirror_parts = []
    for group_start in range(0, slot_total, group_size):
        group_end = min(group_start + group_size, slot_total)
        blocks = tile_blocks[group_start:group_end]
        rows_here = row_local[group_start:group_end]
        cols_here = col_block[group_start:group_end]
        weights = live_mask[group_start:group_end]
        direct = (
            jnp.einsum(
                "sab,sbk->sak",
                blocks,
                jnp.take(remote_basis, cols_here, axis=0),
                preferred_element_type=jnp.float32,
            )
            * weights
        )
        mirrored = (
            jnp.einsum(
                "sab,sak->sbk",
                blocks,
                jnp.take(own_basis, rows_here, axis=0),
                preferred_element_type=jnp.float32,
            )
            * weights
        )
        direct_sum, mirrored = (
            jax.ops.segment_sum(direct, rows_here, num_segments=local_blocks),
            mirrored,
        )
        own_sum = own_sum + direct_sum
        mirror_parts.append(mirrored)
    mirrored_all = jnp.concatenate(mirror_parts, axis=0)
    partial_rows = jax.ops.segment_sum(mirrored_all, col_block, num_segments=block_total)
    flat_rows = partial_rows.reshape(node_total, columns)
    mirror_rows = lax.psum_scatter(flat_rows, "row", scatter_dimension=0, tiled=True)
    return (own_sum.reshape(row_count, columns) + mirror_rows) * (1.0 / math.sqrt(node_total))


def solution(mesh):
    return jax.shard_map(
        on_device,
        mesh=mesh,
        in_specs=(
            P(("grp", "row"), None, None),
            P(("grp", "row"), None),
            P(("grp", "row"), None),
            P(("grp", "row")),
        ),
        out_specs=P(("grp", "row"), None),
        check_vma=False,
    )
```

profile of v0, /device:TPU:0, one launch (start us, length us, event | category | flops | bytes accessed | tf_op | source)
XLA Modules:
  0.0 122.9 jit_solution(6002067020621339743)
XLA Ops:
  6.5 0.7 all-gather.2.cloned.1.call-update
  7.3 0.7 and_select_fusion
  8.1 1.4 %gather_fusion.6 = bf16[3,128,128]{2,1,0:T(8,128)(2,1)S(1)} fusion(bf16[2,128,128]{2,1,0:T(8,128)(2,1)} %bitcast.66, s32[1024]{0:T(1024)S(1)} %get-tuple-element.68), kind=kCustom, calls=%fused_computation.1.clone | custom fusion | bytes 196620 | tf_op jit(solution)/shard_map/jit(_take)/gather | solution.py:46
  9.5 1.4 %gather_fusion.7 = bf16[3,128,128]{2,1,0:T(8,128)(2,1)S(1)} fusion(bf16[2,128,128]{2,1,0:T(8,128)(2,1)} %bitcast.67, s32[1024]{0:T(1024)S(1)} %get-tuple-element.67), kind=kCustom, calls=%fused_computation.7.clone | custom fusion | bytes 196620 | tf_op jit(solution)/shard_map/jit(_take)/gather | solution.py:46
  11.0 1.4 %gather_fusion.8 = bf16[3,128,128]{2,1,0:T(8,128)(2,1)S(1)} fusion(bf16[2,128,128]{2,1,0:T(8,128)(2,1)} %bitcast.68, s32[1024]{0:T(1024)S(1)} %get-tuple-element.66), kind=kCustom, calls=%fused_computation.8.clone | custom fusion | bytes 196620 | tf_op jit(solution)/shard_map/jit(_take)/gather | solution.py:46
  12.4 1.4 %gather_fusion.9 = bf16[3,128,128]{2,1,0:T(8,128)(2,1)S(1)} fusion(bf16[2,128,128]{2,1,0:T(8,128)(2,1)} %bitcast.69, s32[1024]{0:T(1024)S(1)} %get-tuple-element.65), kind=kCustom, calls=%fused_computation.9.clone | custom fusion | bytes 196620 | tf_op jit(solution)/shard_map/jit(_take)/gather | solution.py:46
  13.8 1.4 %gather_fusion.10 = bf16[3,128,128]{2,1,0:T(8,128)(2,1)S(1)} fusion(bf16[2,128,128]{2,1,0:T(8,128)(2,1)} %bitcast.70, s32[1024]{0:T(1024)S(1)} %get-tuple-element.64), kind=kCustom, calls=%fused_computation.10.clone | custom fusion | bytes 196620 | tf_op jit(solution)/shard_map/jit(_take)/gather | solution.py:46
  15.2 0.6 gather_fusion.11
  15.8 0.6 reduce_sum.9
  16.4 0.6 compare_convert_fusion
  17.5 0.3 fusion.9
  18.7 0.3 fusion.1
  19.0 0.4 copy.29
  19.9 2.8 %scatter_fusion.6 = f32[32,128,128]{2,1,0:T(8,128)S(1)} fusion(f32[32,128,128]{2,1,0:T(8,128)S(1)} %broadcast_in_dim.46, s32[18]{0:T(128)S(1)} %slice_bitcast_fusion, f32[18,128,128]{2,1,0:T(8,128)S(1)} %copy.29), kind=kCustom, calls=%fused_computation.18 | custom fusion | flops 294912 | bytes 3539016 | tf_op jit(solution)/shard_map/scatter-add | solution.py:58
  22.7 1.3 %copy-done = f32[32,128,128]{2,1,0:T(8,128)} copy-done((f32[32,128,128]{2,1,0:T(8,128)}, f32[32,128,128]{2,1,0:T(8,128)S(1)}, u32[]{:S(2)}) %copy-start) | copy-done | bytes 2097176
  24.3 26.0 %all-gather.2.cloned.1.call-done = bf16[4096,128]{1,0:T(8,128)(2,1)} async-done(((bf16[256,128]{1,0:T(8,128)(2,1)}), bf16[4096,128]{1,0:T(8,128)(2,1)}) %all-gather.2.cloned.1.call-update) | async-done | bytes 1048592 | tf_op jit(solution)/shard_map/all_gather | solution.py:15
  50.3 1.8 %gather_fusion = bf16[3,128,128]{2,1,0:T(8,128)(2,1)S(1)} fusion(bf16[32,128,128]{2,1,0:T(8,128)(2,1)} %bitcast.72, s32[1024]{0:T(1024)S(1)} %get-tuple-element.74), kind=kCustom, calls=%fused_computation.clone | custom fusion | bytes 196620 | tf_op jit(solution)/shard_map/jit(_take)/gather | solution.py:37
  52.5 1.8 %gather_fusion.1 = bf16[3,128,128]{2,1,0:T(8,128)(2,1)S(1)} fusion(bf16[32,128,128]{2,1,0:T(8,128)(2,1)} %bitcast.73, s32[1024]{0:T(1024)S(1)} %get-tuple-element.73), kind=kCustom, calls=%fused_computation.2.clone | custom fusion | bytes 196620 | tf_op jit(solution)/shard_map/jit(_take)/gather | solution.py:37
  54.3 0.3 fusion.16
  54.8 1.8 %gather_fusion.2 = bf16[3,128,128]{2,1,0:T(8,128)(2,1)S(1)} fusion(bf16[32,128,128]{2,1,0:T(8,128)(2,1)} %bitcast.74, s32[1024]{0:T(1024)S(1)} %get-tuple-element.72), kind=kCustom, calls=%fused_computation.3.clone | custom fusion | bytes 196620 | tf_op jit(solution)/shard_map/jit(_take)/gather | solution.py:37
  57.0 1.8 %gather_fusion.3 = bf16[3,128,128]{2,1,0:T(8,128)(2,1)S(1)} fusion(bf16[32,128,128]{2,1,0:T(8,128)(2,1)} %bitcast.75, s32[1024]{0:T(1024)S(1)} %get-tuple-element.71), kind=kCustom, calls=%fused_computation.4.clone | custom fusion | bytes 196620 | tf_op jit(solution)/shard_map/jit(_take)/gather | solution.py:37
  59.3 1.8 %gather_fusion.4 = bf16[3,128,128]{2,1,0:T(8,128)(2,1)S(1)} fusion(bf16[32,128,128]{2,1,0:T(8,128)(2,1)} %bitcast.76, s32[1024]{0:T(1024)S(1)} %get-tuple-element.70), kind=kCustom, calls=%fused_computation.5.clone | custom fusion | bytes 196620 | tf_op jit(solution)/shard_map/jit(_take)/gather | solution.py:37
  61.1 0.3 fusion.13
  61.5 1.8 %gather_fusion.5 = bf16[3,128,128]{2,1,0:T(8,128)(2,1)S(1)} fusion(bf16[32,128,128]{2,1,0:T(8,128)(2,1)} %bitcast.77, s32[1024]{0:T(1024)S(1)} %get-tuple-element.69), kind=kCustom, calls=%fused_computation.6.clone | custom fusion | bytes 196620 | tf_op jit(solution)/shard_map/jit(_take)/gather | solution.py:37
  63.8 0.7 scatter_fusion
  64.6 0.7 scatter_fusion.1
  65.3 0.7 scatter_fusion.2
  66.0 0.7 scatter_fusion.3
  66.8 0.7 scatter_fusion.4
  67.5 0.7 scatter_fusion.5
  68.3 46.2 %reduce-scatter.2.cloned.1.call-done = f32[256,128]{1,0:T(8,128)} async-done(((f32[4096,128]{1,0:T(8,128)}), f32[256,128]{1,0:T(8,128)}) %reduce-scatter.2.cloned.1.call-update) | async-done | bytes 131088 | tf_op jit(solution)/shard_map/reduce_scatter | solution.py:60
  114.5 1.6 %fusion.18 = f32[256,128]{1,0:T(8,128)} fusion(f32[256,128]{1,0:T(8,128)} %reduce-scatter.2.cloned.1.call-done, f32[2,128,128]{2,1,0:T(8,128)S(1)} %add.47), kind=kLoop, calls=%fused_computation.50 | loop fusion | flops 65536 | bytes 393216 | tf_op jit(solution)/shard_map/mul | solution.py:61
  (47 shorter events, 4.2 us)
Async XLA Ops:
  6.5 8.7 %copy-start.1 = (bf16[256,128]{1,0:T(8,128)(2,1)S(1)}, bf16[256,128]{1,0:T(8,128)(2,1)}, u32[]{:S(2)}) copy-start(bf16[256,128]{1,0:T(8,128)(2,1)} %param.9) | copy-start | bytes 196612
  6.5 9.2 %copy-start.5 = (s32[2]{0:T(128)S(1)}, s32[2]{0:T(128)}, u32[]{:S(2)}) copy-start(s32[2]{0:T(128)} %param.11) | copy-start | bytes 28
  6.5 10.6 %copy-start.2 = (bf16[18,128,128]{2,1,0:T(8,128)(2,1)S(1)}, bf16[18,128,128]{2,1,0:T(8,128)(2,1)}, u32[]{:S(2)}) copy-start(bf16[18,128,128]{2,1,0:T(8,128)(2,1)} %param.8) | copy-start | bytes 1769476
  6.5 43.7 %all-gather.2.cloned.1.call-start = ((), (), s32[]{:S(2)}) async-start(), calls=%async_computation.1 | async-start | bytes 1114112 | tf_op jit(solution)/shard_map/all_gather | solution.py:15
  7.3 107.2 %reduce-scatter.2.cloned.1.call-start = ((), (), s32[]{:S(2)}) async-start(), calls=%async_computation.2 | async-start | bytes 2228224 | tf_op jit(solution)/shard_map/reduce_scatter | solution.py:60
  19.0 0.7 copy-start.4
  22.7 1.4 %copy-start = (f32[32,128,128]{2,1,0:T(8,128)}, f32[32,128,128]{2,1,0:T(8,128)S(1)}, u32[]{:S(2)}) copy-start(f32[32,128,128]{2,1,0:T(8,128)S(1)} %scatter_fusion.6) | copy-start | bytes 6291460
  22.7 29.4 %copy-start.3 = (bf16[18,128,128]{2,1,0:T(8,128)(2,1)S(1)}, bf16[18,128,128]{2,1,0:T(8,128)(2,1)}, u32[]{:S(2)}) copy-start(bf16[18,128,128]{2,1,0:T(8,128)(2,1)} %param.8) | copy-start | bytes 1769476
Sparse Core Ops, SparseCore 0:
  9.5 40.7 all-gather.1
  54.0 60.4 reduce-scatter.1
where the time goes:
time: 124 us; the launch traced here: 123 us
  waiting for transfers between devices  72.9 us (59%)
  local copies, waits for them, and re-layouts  21.6 us (17%)
  between operations  13.8 us (11%)
  other arithmetic  10.8 us (9%)
  matrix products  3.63 us (3%)
    reduce_scatter x1, waiting for transfers between devices, on_device(): lax.psum_scatter(flat_rows, 'row', scatter_dimension=0, tiled=True)  46.2 us
    all_gather x1, waiting for transfers between devices, on_device(): gathered = lax.all_gather(q_block, 'row', axis=0, tiled=True)  26 us
    gather x6, local copies, waits for them, and re-layouts, on_device(): jnp.take(remote_basis, cols_here, axis=0)  10.8 us
    gather x6, local copies, waits for them, and re-layouts, on_device(): jnp.take(own_basis, rows_here, axis=0)  7.59 us
    scatter-add x6, other arithmetic, on_device(): jax.ops.segment_sum(direct, rows_here, num_segments=local_blocks)  4.27 us
    scatter-add x1, other arithmetic, on_device(): jax.ops.segment_sum(mirrored_all, col_block, num_segments=block_total)  2.77 us
  transfers between devices with their start and end apart: 2, of which 2 were waited for; matrix products, arithmetic and copies ran while one was open for 27% of the time, Pallas kernels for 0%

commit v1 on v0

v1 whole, which is shorter than its diff:
```python
import functools
import math

import jax
import jax.numpy as jnp
from jax import lax
from jax.experimental import pallas as pl
from jax.experimental.pallas import tpu as pltpu
from jax.sharding import PartitionSpec as P

TOP = 32700.0
STEPS = 16.0
LEAST = 1e-30


def place():
    me = lax.axis_index("row")
    return me // 2, me % 2


def scale_of(code):
    return jnp.exp2(code * (1.0 / STEPS))


def encode(x):
    top = jnp.maximum(jnp.max(jnp.abs(x), axis=0, keepdims=True), LEAST)
    code = jnp.ceil(jnp.log2(top) * STEPS)
    values = jnp.round(x * (TOP / scale_of(code)))
    return values.astype(jnp.int32).astype(jnp.int16), code


def pack_kernel(
    own_index, own_count, other_index, other_count, own_tiles, other_tiles,
    own_q, other_q, *outs,
):
    *messages, panels, chip_q, local_rows = outs
    slots = len(messages)
    tile = own_tiles.shape[1]
    rows = own_q.shape[0]
    chip_blocks = 2 * rows // tile
    chip, core = place()

    panels[...] = jnp.zeros_like(panels)
    for index, count, tiles in (
        (own_index, own_count, own_tiles),
        (other_index, other_count, other_tiles),
    ):
        live = count[0]
        for r in range(1, count.shape[0]):
            live = live + count[r]

        def put(s, carry, index=index, tiles=tiles):
            i, j = index[s, 0], index[s, 1]
            cls = chip ^ (j // chip_blocks)

            @pl.when(cls % 2 == core)
            def _():
                panel = (cls // 2) * chip_blocks + j % chip_blocks
                at = pl.multiple_of((i % chip_blocks) * tile, tile)
                panels[panel, pl.ds(at, tile), :] = tiles[s]

            return carry

        lax.fori_loop(0, live, put, 0)

    chip_q[pl.ds(pl.multiple_of(core * rows, rows), rows), :] = own_q[...]
    chip_q[pl.ds(pl.multiple_of((1 - core) * rows, rows), rows), :] = other_q[...]
    q = chip_q[...]
    q_t = q.T
    q_wide = q.astype(jnp.float32)
    for k in reversed(range(slots)):
        up = chip < (chip ^ (2 * k + core))
        codes = []
        for b in range(0, chip_blocks, 2):
            g = k * chip_blocks + b
            pair = jnp.concatenate([panels[g], panels[g + 1]], axis=1)
            sums = jnp.dot(q_t, pair, preferred_element_type=jnp.float32)
            for e in range(2):
                block = sums[:, e * tile:(e + 1) * tile]
                at = (b + e) * tile
                if k == 0:
                    local_rows[at:at + tile, :] = block
                x = jnp.where(up, block, q_wide[at:at + tile, :])
                values, code = encode(x)
                messages[k][at:at + tile, :] = values
                codes.append(code)
        which = lax.broadcasted_iota(jnp.int32, (16, tile), 0)
        tail = jnp.zeros((16, tile), jnp.float32)
        for b, code in enumerate(codes):
            tail = jnp.where(which == b, code, tail)
        messages[k][chip_blocks * tile:, :] = tail.astype(jnp.int32).astype(jnp.int16)


def local_kernel(panels, chip_q, local_rows, base):
    chip_blocks, rows, tile = panels.shape
    _, core = place()
    mine = core == 0
    total = jnp.zeros((rows, tile), jnp.float32)
    for b in range(0, chip_blocks, 2):
        pair = jnp.concatenate([panels[b], panels[b + 1]], axis=1)
        total += jnp.dot(
            pair, chip_q[b * tile:(b + 2) * tile, :], preferred_element_type=jnp.float32
        )
    for b in range(chip_blocks):
        at = slice(b * tile, (b + 1) * tile)
        base[at, :] = jnp.where(mine, total[at, :] + local_rows[at, :].T, 0.0)


def unpack_kernel(base, panels, *refs):
    *received, keep, send, result = refs
    tile = panels.shape[2]
    chip_rows = panels.shape[1]
    chip_blocks = chip_rows // tile
    rows = chip_rows // 2
    chip, core = place()
    total = base[...]
    mirrored = [jnp.zeros((tile, tile), jnp.float32) for _ in range(chip_blocks)]
    for k in reversed(range(len(received))):
        message = received[k]
        low = (chip ^ (2 * k + core)) < chip
        tail = message[chip_rows:, :].astype(jnp.int32).astype(jnp.float32)
        scales = scale_of(tail) * (1.0 / TOP)
        for b in range(0, chip_blocks, 2):
            parts = []
            for e in (b, b + 1):
                values = message[e * tile:(e + 1) * tile, :]
                x = values.astype(jnp.int32).astype(jnp.float32) * scales[e:e + 1, :]
                mirrored[e] += jnp.where(low, x, 0.0)
                parts.append(x.astype(jnp.bfloat16))
            g = k * chip_blocks + b
            pair = jnp.concatenate([panels[g], panels[g + 1]], axis=1)
            total += jnp.dot(
                pair, jnp.concatenate(parts, axis=0), preferred_element_type=jnp.float32
            )
    for b in range(chip_blocks):
        at = slice(b * tile, (b + 1) * tile)
        result[at, :] = total[at, :] + mirrored[b].T
    keep[...] = result[pl.ds(pl.multiple_of(core * rows, rows), rows), :]
    send[...] = result[pl.ds(pl.multiple_of((1 - core) * rows, rows), rows), :]


VMEM = functools.partial(pl.BlockSpec, memory_space=pltpu.VMEM)
SMEM = functools.partial(pl.BlockSpec, memory_space=pltpu.SMEM)


def on_device(devices, tile_blocks, q_block, tile_index, tile_count):
    tile = tile_blocks.shape[1]
    rows, columns = q_block.shape
    chips = devices // 2
    slots = chips // 2
    chip_rows = 2 * rows
    chip_blocks = chip_rows // tile
    wide = jnp.float32
    other_core = [(d, d ^ 1) for d in range(devices)]

    def swap(x):
        return lax.ppermute(x, "row", other_core)

    other_tiles = swap(tile_blocks)
    other_q = swap(q_block)
    other_index = swap(tile_index)
    other_count = swap(tile_count)

    message = jax.ShapeDtypeStruct((chip_rows + 16, columns), jnp.int16)
    *messages, panels, chip_q, local_rows = pl.pallas_call(
        pack_kernel,
        out_shape=[message] * slots + [
            jax.ShapeDtypeStruct((slots * chip_blocks, chip_rows, tile), jnp.bfloat16),
            jax.ShapeDtypeStruct((chip_rows, columns), jnp.bfloat16),
            jax.ShapeDtypeStruct((chip_rows, columns), wide),
        ],
        in_specs=[SMEM()] * 4 + [VMEM()] * 4,
        out_specs=[VMEM()] * (slots + 3),
        compiler_params=pltpu.CompilerParams(vmem_limit_bytes=48 * 2**20),
        name="pack",
    )(tile_index, tile_count, other_index, other_count, tile_blocks, other_tiles,
      q_block, other_q)

    received = [None] * slots
    for k in reversed(range(slots)):
        pairs = [
            (d, d ^ (2 * (2 * k + d % 2))) for d in range(devices) if 2 * k + d % 2
        ]
        received[k] = lax.ppermute(messages[k], "row", pairs)

    base = pl.pallas_call(
        local_kernel,
        out_shape=jax.ShapeDtypeStruct((chip_rows, columns), wide),
        in_specs=[VMEM()] * 3,
        out_specs=VMEM(),
        compiler_params=pltpu.CompilerParams(vmem_limit_bytes=32 * 2**20),
        name="local",
    )(panels[:chip_blocks], chip_q, local_rows)

    keep, send = pl.pallas_call(
        unpack_kernel,
        out_shape=[jax.ShapeDtypeStruct((rows, columns), wide)] * 2,
        in_specs=[VMEM()] * (2 + slots),
        out_specs=[VMEM()] * 2,
        scratch_shapes=[pltpu.VMEM((chip_rows, columns), wide)],
        compiler_params=pltpu.CompilerParams(vmem_limit_bytes=48 * 2**20),
        name="unpack",
    )(base, panels, *received)
    return (keep + swap(send)) * (1.0 / math.sqrt(rows * devices))


def solution(mesh):
    return jax.shard_map(
        functools.partial(on_device, mesh.shape["row"]),
        mesh=mesh,
        in_specs=(
            P(("grp", "row"), None, None),
            P(("grp", "row"), None),
            P(("grp", "row"), None),
            P(("grp", "row")),
        ),
        out_specs=P(("grp", "row"), None),
        check_vma=False,
    )
```

time: 124 us -> 28.9 us (0.23)
  waiting for transfers between devices: 72.9 us -> 10.1 us
  local copies, waits for them, and re-layouts: 21.6 us -> 3.36 us
  between operations: 13.8 us -> 0.06 us
  starting transfers between devices: 0.04 us -> 10.9 us
  other arithmetic: 10.8 us -> 0.68 us
  matrix products: 3.63 us -> 0 us
  Pallas kernels: 0 us -> 3.63 us
    reduce_scatter x1 -> x0, waiting for transfers between devices: 46.2 us -> none  [on_device(): lax.psum_scatter(flat_rows, 'row', scatter_dimension=0, tiled=True)]
    all_gather x1 -> x0, waiting for transfers between devices: 26 us -> none  [on_device(): gathered = lax.all_gather(q_block, 'row', axis=0, tiled=True)]
    gather x12 -> x0, local copies, waits for them, and re-layouts: 18.4 us -> none  [the longest x6 10.8 us: on_device(): jnp.take(remote_basis, cols_here, axis=0)]
    ppermute x0 -> x9, starting transfers between devices: none -> 10.9 us  [the longest x4 5.63 us: on_device(): received[k] = lax.ppermute(messages[k], 'row', pairs)]
    ppermute x0 -> x9, waiting for transfers between devices: none -> 10.1 us  [the longest x4 7.92 us: on_device(): received[k] = lax.ppermute(messages[k], 'row', pairs)]
    scatter-add x7 -> x0, other arithmetic: 7.04 us -> none  [the longest x6 4.27 us: on_device(): jax.ops.segment_sum(direct, rows_here, num_segments=local_blocks)]
    pallas_call x0 -> x3, Pallas kernels: none -> 3.63 us  [the longest x1 2.55 us: on_device(): pl.pallas_call(pack_kernel, out_shape=[message] * slots + [jax.ShapeDtype...]
    dot_general x12 -> x0, matrix products: 3.63 us -> none  [the longest x6 1.81 us: on_device(): jnp.einsum('sab,sak->sbk', blocks, jnp.take(own_basis, rows_here, axis=0)...]
  transfers between devices with their start and end apart: 2 -> 9, of which waited for: 2 -> 5; matrix products, arithmetic and copies ran while one was open for 27% -> 3% of each run, Pallas kernels for 0% -> 1%
where the time goes in v1:
time: 28.9 us; the launch traced here: 28.7 us
  starting transfers between devices  10.9 us (38%)
  waiting for transfers between devices  10.1 us (35%)
  Pallas kernels  3.63 us (13%)
  local copies, waits for them, and re-layouts  3.36 us (12%)
  other arithmetic  0.68 us (2%)
    ppermute x4, waiting for transfers between devices, on_device(): received[k] = lax.ppermute(messages[k], 'row', pairs)  7.92 us
    ppermute x4, starting transfers between devices, on_device(): received[k] = lax.ppermute(messages[k], 'row', pairs)  5.63 us
    ppermute x5, starting transfers between devices, swap(): return lax.ppermute(x, 'row', other_core)  5.24 us
    unnamed x7, local copies, waits for them, and re-layouts  3.32 us
    pallas_call x1, Pallas kernels, on_device(): pl.pallas_call(pack_kernel, out_shape=[message] * slots + [jax.ShapeDtype...  2.55 us
    ppermute x5, waiting for transfers between devices, swap(): return lax.ppermute(x, 'row', other_core)  2.19 us
    pallas_call x1, Pallas kernels, on_device(): pl.pallas_call(unpack_kernel, out_shape=[jax.ShapeDtypeStruct((rows, colu...  0.78 us
    mul x1, other arithmetic, on_device(): return (keep + swap(send)) * (1.0 / math.sqrt(rows * devices))  0.68 us
  transfers between devices with their start and end apart: 9, of which 5 were waited for; matrix products, arithmetic and copies ran while one was open for 3% of the time, Pallas kernels for 1%

profile of v1, /device:TPU:0, one launch (start us, length us, event | category | flops | bytes accessed | tf_op | source)
XLA Modules:
  0.0 28.7 jit_solution(4753194228076103917)
XLA Ops:
  0.0 0.5 %collective-permute-start.2 = (bf16[18,128,128]{2,1,0:T(8,128)(2,1)}, bf16[18,128,128]{2,1,0:T(8,128)(2,1)S(1)}, u32[]{:S(2)}, u32[]{:S(2)}) collective-permute-start(bf16[18,128,128]{2,1,0:T(8,128)(2,1)} %own_tiles.1), channel_id=1, source_target_pairs={{0,1},{1,0},{2,3},{3,2},{4,5},{5,4},{6,7},{7,6},{8,9},{9,8},{10,11... | collective-permute-start | bytes 1769480 | tf_op jit(solution)/shard_map/ppermute | solution.py:157
  0.5 0.1 collective-permute-start.3
  0.5 0.8 %copy.6.own_index = s32[18,2]{1,0:T(8,128)S(1)} copy(s32[18,2]{0,1:T(2,128)} %param.6) | data formatting | bytes 288 | tf_op args[2]
  1.3 0.5 %collective-permute-start = (s32[18,2]{1,0:T(8,128)S(1)}, s32[18,2]{1,0:T(8,128)S(1)}, u32[]{:S(2)}, u32[]{:S(2)}) collective-permute-start(s32[18,2]{1,0:T(8,128)S(1)} %copy.6.own_index), channel_id=1, source_target_pairs={{0,1},{1,0},{2,3},{3,2},{4,5},{5,4},{6,7},{7,6},{8,9},{9,8},{10,11... | collective-permute-start | bytes 440 | tf_op jit(solution)/shard_map/ppermute | solution.py:157
  1.7 0.1 collective-permute-start.1
  1.8 1.2 %collective-permute-done.1.other_count = s32[2]{0:T(128)S(1)} collective-permute-done((s32[2]{0:T(128)}, s32[2]{0:T(128)S(1)}, u32[]{:S(2)}, u32[]{:S(2)}) %collective-permute-start.1) | collective-permute-done | bytes 40 | tf_op jit(solution)/shard_map/ppermute | solution.py:157
  3.0 0.0 collective-permute-done.other_index
  3.0 0.0 collective-permute-done.3.other_q
  3.0 0.0 collective-permute-done.2.other_tiles
  3.0 0.0 copy-start
  3.0 1.1 %copy-done = bf16[18,128,128]{2,1,0:T(8,128)(2,1)S(1)} copy-done((bf16[18,128,128]{2,1,0:T(8,128)(2,1)S(1)}, bf16[18,128,128]{2,1,0:T(8,128)(2,1)}, u32[]{:S(2)}) %copy-start) | copy-done | bytes 589848
  4.1 0.0 copy-start.1
  4.1 0.8 %copy-done.1 = bf16[256,128]{1,0:T(8,128)(2,1)S(1)} copy-done((bf16[256,128]{1,0:T(8,128)(2,1)S(1)}, bf16[256,128]{1,0:T(8,128)(2,1)}, u32[]{:S(2)}) %copy-start.1) | copy-done | bytes 65560
  4.9 0.0 copy-start.2
  4.9 0.7 %copy-done.2 = s32[2]{0:T(128)S(1)} copy-done((s32[2]{0:T(128)S(1)}, s32[2]{0:T(128)}, u32[]{:S(2)}) %copy-start.2) | copy-done | bytes 32
  5.6 2.6 %pack.1 = (s16[528,128]{1,0:T(8,128)(2,1)S(1)}, s16[528,128]{1,0:T(8,128)(2,1)S(1)}, s16[528,128]{1,0:T(8,128)(2,1)S(1)}, s16[528,128]{1,0:T(8,128)(2,1)S(1)}, b...) custom-call(s32[18,2]{1,0:T(8,128)S(1)} %copy.6.own_index, s32[2]{0:T(128)S(1)} %copy-done.2, ...), custom_call_target="tpu_custom_call" | custom-call | tf_op jit(solution)/shard_map/pack/pallas_call | solution.py:165
  8.1 0.7 %collective-permute-start.4 = (s16[528,128]{1,0:T(8,128)(2,1)S(1)}, s16[528,128]{1,0:T(8,128)(2,1)S(1)}, u32[]{:S(2)}, u32[]{:S(2)}) collective-permute-start(s16[528,128]{1,0:T(8,128)(2,1)S(1)} %get-tuple-element.17), channel_id=1, source_target_pairs={{1,3},{3,1},{5,7},{7,5},{9,11},{11,9},{13,15},{15,13},{17,19},{19,... | collective-permute-start | bytes 405512 | tf_op jit(solution)/shard_map/ppermute | solution.py:184
  8.8 2.5 %collective-permute-start.5 = (s16[528,128]{1,0:T(8,128)(2,1)S(1)}, s16[528,128]{1,0:T(8,128)(2,1)S(1)}, u32[]{:S(2)}, u32[]{:S(2)}) collective-permute-start(s16[528,128]{1,0:T(8,128)(2,1)S(1)} %get-tuple-element.18), channel_id=1, source_target_pairs={{0,4},{1,7},{2,6},{3,5},{4,0},{5,3},{6,2},{7,1},{8,12},{9,15},{10,... | collective-permute-start | bytes 405512 | tf_op jit(solution)/shard_map/ppermute | solution.py:184
  11.3 2.3 %collective-permute-start.6 = (s16[528,128]{1,0:T(8,128)(2,1)S(1)}, s16[528,128]{1,0:T(8,128)(2,1)S(1)}, u32[]{:S(2)}, u32[]{:S(2)}) collective-permute-start(s16[528,128]{1,0:T(8,128)(2,1)S(1)} %get-tuple-element.19), channel_id=1, source_target_pairs={{0,8},{1,11},{2,10},{3,9},{4,12},{5,15},{6,14},{7,13},{8,0},{9,3},... | collective-permute-start | bytes 405512 | tf_op jit(solution)/shard_map/ppermute | solution.py:184
  13.6 0.2 collective-permute-start.7
  13.8 0.3 %local.1.base = f32[512,128]{1,0:T(8,128)S(1)} custom-call(bf16[4,512,128]{2,1,0:T(8,128)(2,1)S(1)} %slice.3.panels, bf16[512,128]{1,0:T(8,128)(2,1)S(1)} %get-tuple-element.15.chip_q, f32[512,128]{1,0:T(8,128)S(1)} %get-tuple-element.16.local_rows), custom_call_target="tpu_custom_call" | custom-call | tf_op jit(solution)/shard_map/local/pallas_call | solution.py:186
  14.1 0.0 collective-permute-done.4.refs_0_
  14.1 0.2 collective-permute-done.5.refs_1_
  14.3 3.9 %collective-permute-done.6.refs_2_ = s16[528,128]{1,0:T(8,128)(2,1)S(1)} collective-permute-done((s16[528,128]{1,0:T(8,128)(2,1)S(1)}, s16[528,128]{1,0:T(8,128)(2,1)S(1)}, u32[]{:S(2)}, u32[]{:S(2)}) %collective-permute-start.6) | collective-permute-done | bytes 135200 | tf_op jit(solution)/shard_map/ppermute | solution.py:184
  18.2 3.8 %collective-permute-done.7.refs_3_ = s16[528,128]{1,0:T(8,128)(2,1)S(1)} collective-permute-done((s16[528,128]{1,0:T(8,128)(2,1)S(1)}, s16[528,128]{1,0:T(8,128)(2,1)S(1)}, u32[]{:S(2)}, u32[]{:S(2)}) %collective-permute-start.7) | collective-permute-done | bytes 135200 | tf_op jit(solution)/shard_map/ppermute | solution.py:184
  22.0 0.8 %unpack.1 = (f32[256,128]{1,0:T(8,128)S(1)}, f32[256,128]{1,0:T(8,128)S(1)}) custom-call(f32[512,128]{1,0:T(8,128)S(1)} %local.1.base, bf16[16,512,128]{2,1,0:T(8,128)(2,1)S(1)} %get-tuple-element.14.panels, s16[528,128]{1,0:T(8,128)(2,1)S(1)} %collective-permute-done.4.refs_0_, s16[528,128]{1,0:T(8,128)(2,1)S(1)} %collective-permute-done.5.refs_1_, ...), custom_call_target="tpu_custom_call" | custom-call | tf_op jit(solution)/shard_map/unpack/pallas_call | solution.py:195
  22.8 4.2 %collective-permute-start.8 = (f32[256,128]{1,0:T(8,128)S(1)}, f32[256,128]{1,0:T(8,128)S(1)}, u32[]{:S(2)}, u32[]{:S(2)}) collective-permute-start(f32[256,128]{1,0:T(8,128)S(1)} %get-tuple-element.22), channel_id=1, source_target_pairs={{0,1},{1,0},{2,3},{3,2},{4,5},{5,4},{6,7},{7,6},{8,9},{9,8},{10,11... | collective-permute-start | bytes 393224 | tf_op jit(solution)/shard_map/ppermute | solution.py:157
  27.0 1.0 %collective-permute-done.8 = f32[256,128]{1,0:T(8,128)S(1)} collective-permute-done((f32[256,128]{1,0:T(8,128)S(1)}, f32[256,128]{1,0:T(8,128)S(1)}, u32[]{:S(2)}, u32[]{:S(2)}) %collective-permute-start.8) | collective-permute-done | bytes 131104 | tf_op jit(solution)/shard_map/ppermute | solution.py:157
  28.0 0.7 %add_multiply_fusion = f32[256,128]{1,0:T(8,128)} fusion(f32[256,128]{1,0:T(8,128)S(1)} %get-tuple-element.21, f32[256,128]{1,0:T(8,128)S(1)} %collective-permute-done.8), kind=kLoop, calls=%fused_computation | loop fusion | flops 65536 | bytes 393216 | tf_op jit(solution)/shard_map/mul | solution.py:204
  (1 shorter events, 0.0 us)
Async XLA Ops:
  0.0 3.0 %collective-permute-start.2 = (bf16[18,128,128]{2,1,0:T(8,128)(2,1)}, bf16[18,128,128]{2,1,0:T(8,128)(2,1)S(1)}, u32[]{:S(2)}, u32[]{:S(2)}) collective-permute-start(bf16[18,128,128]{2,1,0:T(8,128)(2,1)} %own_tiles.1), channel_id=1, source_target_pairs={{0,1},{1,0},{2,3},{3,2},{4,5},{5,4},{6,7},{7,6},{8,9},{9,8},{10,11... | collective-permute-start | bytes 1769480 | tf_op jit(solution)/shard_map/ppermute | solution.py:157
  0.5 2.5 %collective-permute-start.3 = (bf16[256,128]{1,0:T(8,128)(2,1)}, bf16[256,128]{1,0:T(8,128)(2,1)S(1)}, u32[]{:S(2)}, u32[]{:S(2)}) collective-permute-start(bf16[256,128]{1,0:T(8,128)(2,1)} %own_q.1), channel_id=1, source_target_pairs={{0,1},{1,0},{2,3},{3,2},{4,5},{5,4},{6,7},{7,6},{8,9},{9,8},{10,11... | collective-permute-start | bytes 196616 | tf_op jit(solution)/shard_map/ppermute | solution.py:157
  1.3 1.7 %collective-permute-start = (s32[18,2]{1,0:T(8,128)S(1)}, s32[18,2]{1,0:T(8,128)S(1)}, u32[]{:S(2)}, u32[]{:S(2)}) collective-permute-start(s32[18,2]{1,0:T(8,128)S(1)} %copy.6.own_index), channel_id=1, source_target_pairs={{0,1},{1,0},{2,3},{3,2},{4,5},{5,4},{6,7},{7,6},{8,9},{9,8},{10,11... | collective-permute-start | bytes 440 | tf_op jit(solution)/shard_map/ppermute | solution.py:157
  1.7 1.3 %collective-permute-start.1 = (s32[2]{0:T(128)}, s32[2]{0:T(128)S(1)}, u32[]{:S(2)}, u32[]{:S(2)}) collective-permute-start(s32[2]{0:T(128)} %own_count.1), channel_id=1, source_target_pairs={{0,1},{1,0},{2,3},{3,2},{4,5},{5,4},{6,7},{7,6},{8,9},{9,8},{10,11... | collective-permute-start | bytes 32 | tf_op jit(solution)/shard_map/ppermute | solution.py:157
  3.0 1.1 %copy-start = (bf16[18,128,128]{2,1,0:T(8,128)(2,1)S(1)}, bf16[18,128,128]{2,1,0:T(8,128)(2,1)}, u32[]{:S(2)}) copy-start(bf16[18,128,128]{2,1,0:T(8,128)(2,1)} %own_tiles.1) | copy-start | bytes 1769476
  4.1 0.8 %copy-start.1 = (bf16[256,128]{1,0:T(8,128)(2,1)S(1)}, bf16[256,128]{1,0:T(8,128)(2,1)}, u32[]{:S(2)}) copy-start(bf16[256,128]{1,0:T(8,128)(2,1)} %own_q.1) | copy-start | bytes 196612
  4.9 0.7 %copy-start.2 = (s32[2]{0:T(128)S(1)}, s32[2]{0:T(128)}, u32[]{:S(2)}) copy-start(s32[2]{0:T(128)} %own_count.1) | copy-start | bytes 28
  8.1 6.0 %collective-permute-start.4 = (s16[528,128]{1,0:T(8,128)(2,1)S(1)}, s16[528,128]{1,0:T(8,128)(2,1)S(1)}, u32[]{:S(2)}, u32[]{:S(2)}) collective-permute-start(s16[528,128]{1,0:T(8,128)(2,1)S(1)} %get-tuple-element.17), channel_id=1, source_target_pairs={{1,3},{3,1},{5,7},{7,5},{9,11},{11,9},{13,15},{15,13},{17,19},{19,... | collective-permute-start | bytes 405512 | tf_op jit(solution)/shard_map/ppermute | solution.py:184
  8.8 5.5 %collective-permute-start.5 = (s16[528,128]{1,0:T(8,128)(2,1)S(1)}, s16[528,128]{1,0:T(8,128)(2,1)S(1)}, u32[]{:S(2)}, u32[]{:S(2)}) collective-permute-start(s16[528,128]{1,0:T(8,128)(2,1)S(1)} %get-tuple-element.18), channel_id=1, source_target_pairs={{0,4},{1,7},{2,6},{3,5},{4,0},{5,3},{6,2},{7,1},{8,12},{9,15},{10,... | collective-permute-start | bytes 405512 | tf_op jit(solution)/shard_map/ppermute | solution.py:184
  11.3 6.9 %collective-permute-start.6 = (s16[528,128]{1,0:T(8,128)(2,1)S(1)}, s16[528,128]{1,0:T(8,128)(2,1)S(1)}, u32[]{:S(2)}, u32[]{:S(2)}) collective-permute-start(s16[528,128]{1,0:T(8,128)(2,1)S(1)} %get-tuple-element.19), channel_id=1, source_target_pairs={{0,8},{1,11},{2,10},{3,9},{4,12},{5,15},{6,14},{7,13},{8,0},{9,3},... | collective-permute-start | bytes 405512 | tf_op jit(solution)/shard_map/ppermute | solution.py:184
  13.6 8.4 %collective-permute-start.7 = (s16[528,128]{1,0:T(8,128)(2,1)S(1)}, s16[528,128]{1,0:T(8,128)(2,1)S(1)}, u32[]{:S(2)}, u32[]{:S(2)}) collective-permute-start(s16[528,128]{1,0:T(8,128)(2,1)S(1)} %get-tuple-element.20), channel_id=1, source_target_pairs={{0,12},{1,15},{2,14},{3,13},{4,8},{5,11},{6,10},{7,9},{8,4},{9,7},... | collective-permute-start | bytes 405512 | tf_op jit(solution)/shard_map/ppermute | solution.py:184
  22.8 5.2 %collective-permute-start.8 = (f32[256,128]{1,0:T(8,128)S(1)}, f32[256,128]{1,0:T(8,128)S(1)}, u32[]{:S(2)}, u32[]{:S(2)}) collective-permute-start(f32[256,128]{1,0:T(8,128)S(1)} %get-tuple-element.22), channel_id=1, source_target_pairs={{0,1},{1,0},{2,3},{3,2},{4,5},{5,4},{6,7},{7,6},{8,9},{9,8},{10,11... | collective-permute-start | bytes 393224 | tf_op jit(solution)/shard_map/ppermute | solution.py:157

commit v2 on v1

--- a/solution.py
+++ b/solution.py
@@ -29,46 +29,41 @@
     return values.astype(jnp.int32).astype(jnp.int16), code
 
 
-def pack_kernel(
-    own_index, own_count, other_index, other_count, own_tiles, other_tiles,
-    own_q, other_q, *outs,
-):
-    *messages, panels, chip_q, local_rows = outs
-    slots = len(messages)
-    tile = own_tiles.shape[1]
-    rows = own_q.shape[0]
-    chip_blocks = 2 * rows // tile
+def put_tiles(index, count, tiles, panels, chip_blocks):
     chip, core = place()
-
+    tile = tiles.shape[1]
+    live = count[0]
+    for r in range(1, count.shape[0]):
+        live = live + count[r]
+
+    def put(s, carry):
+        i, j = index[0, s], index[1, s]
+        cls = chip ^ (j // chip_blocks)
+
+        @pl.when(cls % 2 == core)
+        def _():
+            panel = (cls // 2) * chip_blocks + j % chip_blocks
+            at = pl.multiple_of((i % chip_blocks) * tile, tile)
+            panels[panel, pl.ds(at, tile), :] = tiles[s]
+
+        return carry
+
+    lax.fori_loop(0, live, put, 0)
+
+
+def own_kernel(index, count, tiles, panels):
     panels[...] = jnp.zeros_like(panels)
-    for index, count, tiles in (
-        (own_index, own_count, own_tiles),
-        (other_index, other_count, other_tiles),
-    ):
-        live = count[0]
-        for r in range(1, count.shape[0]):
-            live = live + count[r]
-
-        def put(s, carry, index=index, tiles=tiles):
-            i, j = index[s, 0], index[s, 1]
-            cls = chip ^ (j // chip_blocks)
-
-            @pl.when(cls % 2 == core)
-            def _():
-                panel = (cls // 2) * chip_blocks + j % chip_blocks
-                at = pl.multiple_of((i % chip_blocks) * tile, tile)
-                panels[panel, pl.ds(at, tile), :] = tiles[s]
-
-            return carry
-
-        lax.fori_loop(0, live, put, 0)
-
-    chip_q[pl.ds(pl.multiple_of(core * rows, rows), rows), :] = own_q[...]
-    chip_q[pl.ds(pl.multiple_of((1 - core) * rows, rows), rows), :] = other_q[...]
+    put_tiles(index, count, tiles, panels, panels.shape[1] // panels.shape[2])
+
+
+def write_messages(slots, panels, chip_q, messages, local_rows=None):
+    chip_rows, tile = panels.shape[1:]
+    chip_blocks = chip_rows // tile
+    chip, core = place()
     q = chip_q[...]
     q_t = q.T
     q_wide = q.astype(jnp.float32)
-    for k in reversed(range(slots)):
+    for k, message in zip(slots, messages, strict=True):
         up = chip < (chip ^ (2 * k + core))
         codes = []
         for b in range(0, chip_blocks, 2):
@@ -82,13 +77,26 @@
                     local_rows[at:at + tile, :] = block
                 x = jnp.where(up, block, q_wide[at:at + tile, :])
                 values, code = encode(x)
-                messages[k][at:at + tile, :] = values
+                message[at:at + tile, :] = values
                 codes.append(code)
         which = lax.broadcasted_iota(jnp.int32, (16, tile), 0)
         tail = jnp.zeros((16, tile), jnp.float32)
         for b, code in enumerate(codes):
             tail = jnp.where(which == b, code, tail)
-        messages[k][chip_blocks * tile:, :] = tail.astype(jnp.int32).astype(jnp.int16)
+        message[chip_rows:, :] = tail.astype(jnp.int32).astype(jnp.int16)
+
+
+def far_kernel(slots, index, count, tiles, own_q, other_q, _, panels, chip_q, *messages):
+    rows = own_q.shape[0]
+    _, core = place()
+    put_tiles(index, count, tiles, panels, panels.shape[1] // panels.shape[2])
+    chip_q[pl.ds(pl.multiple_of(core * rows, rows), rows), :] = own_q[...]
+    chip_q[pl.ds(pl.multiple_of((1 - core) * rows, rows), rows), :] = other_q[...]
+    write_messages(slots, panels, chip_q, messages)
+
+
+def near_kernel(slots, panels, chip_q, local_rows, *messages):
+    write_messages(slots, panels, chip_q, messages, local_rows)
 
 
 def local_kernel(panels, chip_q, local_rows, base):
@@ -156,25 +164,46 @@
     def swap(x):
         return lax.ppermute(x, "row", other_core)
 
+    index = tile_index.T
     other_tiles = swap(tile_blocks)
     other_q = swap(q_block)
-    other_index = swap(tile_index)
+    other_index = swap(index)
     other_count = swap(tile_count)
 
+    panels_shape = jax.ShapeDtypeStruct(
+        (slots * chip_blocks, chip_rows, tile), jnp.bfloat16
+    )
+    q_shape = jax.ShapeDtypeStruct((chip_rows, columns), jnp.bfloat16)
     message = jax.ShapeDtypeStruct((chip_rows + 16, columns), jnp.int16)
-    *messages, panels, chip_q, local_rows = pl.pallas_call(
-        pack_kernel,
-        out_shape=[message] * slots + [
-            jax.ShapeDtypeStruct((slots * chip_blocks, chip_rows, tile), jnp.bfloat16),
-            jax.ShapeDtypeStruct((chip_rows, columns), jnp.bfloat16),
-            jax.ShapeDtypeStruct((chip_rows, columns), wide),
-        ],
-        in_specs=[SMEM()] * 4 + [VMEM()] * 4,
-        out_specs=[VMEM()] * (slots + 3),
-        compiler_params=pltpu.CompilerParams(vmem_limit_bytes=48 * 2**20),
-        name="pack",
-    )(tile_index, tile_count, other_index, other_count, tile_blocks, other_tiles,
-      q_block, other_q)
+    params = pltpu.CompilerParams(vmem_limit_bytes=48 * 2**20)
+    own_panels = pl.pallas_call(
+        own_kernel,
+        out_shape=panels_shape,
+        in_specs=[SMEM(), SMEM(), pl.BlockSpec()],
+        out_specs=VMEM(),
+        compiler_params=params,
+        name="own_tiles",
+    )(index, tile_count, tile_blocks)
+    near = list(reversed(range(slots // 2)))
+    far = list(reversed(range(slots // 2, slots)))
+    panels, chip_q, *far_messages = pl.pallas_call(
+        functools.partial(far_kernel, far),
+        out_shape=[panels_shape, q_shape] + [message] * len(far),
+        in_specs=[SMEM(), SMEM(), VMEM(), pl.BlockSpec(), VMEM(), VMEM()],
+        out_specs=[VMEM()] * (2 + len(far)),
+        input_output_aliases={5: 0},
+        compiler_params=params,
+        name="pack_far",
+    )(other_index, other_count, other_tiles, q_block, other_q, own_panels)
+    local_rows, *near_messages = pl.pallas_call(
+        functools.partial(near_kernel, near),
+        out_shape=[jax.ShapeDtypeStruct((chip_rows, columns), wide)] + [message] * len(near),
+        in_specs=[VMEM()] * 2,
+        out_specs=[VMEM()] * (1 + len(near)),
+        compiler_params=params,
+        name="pack_near",
+    )(panels, chip_q)
+    messages = dict(zip(far + near, far_messages + near_messages, strict=True))
 
     received = [None] * slots
     for k in reversed(range(slots)):

time: 28.9 us -> 25.7 us (0.89)
  starting transfers between devices: 10.9 us -> 7.05 us
  waiting for transfers between devices: 10.1 us -> 11.2 us
  local copies, waits for them, and re-layouts: 3.36 us -> 2.44 us
  Pallas kernels: 3.63 us -> 4.03 us
    ppermute x5, starting transfers between devices: 5.24 us -> 1.2 us  [swap(): return lax.ppermute(x, 'row', other_core)]
    ppermute x4, waiting for transfers between devices: 7.92 us -> 9.99 us  [on_device(): received[k] = lax.ppermute(messages[k], 'row', pairs)]
    ppermute x5, waiting for transfers between devices: 2.19 us -> 1.24 us  [swap(): return lax.ppermute(x, 'row', other_core)]
    unnamed x7 -> x8, local copies, waits for them, and re-layouts: 3.32 us -> 2.4 us
    pallas_call x1 -> x3, Pallas kernels: 2.55 us -> 2.94 us  [the longest x1 1.38 us: on_device(): pl.pallas_call(own_kernel, out_shape=panels_shape, in_specs=[SMEM(), SMEM...]
  transfers between devices with their start and end apart: 9 -> 9, of which waited for: 5 -> 3; matrix products, arithmetic and copies ran while one was open for 3% -> 0% of each run, Pallas kernels for 1% -> 8%
where the time goes in v2:
time: 25.7 us; the launch traced here: 25.5 us
  waiting for transfers between devices  11.2 us (44%)
  starting transfers between devices  7.05 us (27%)
  Pallas kernels  4.03 us (16%)
  local copies, waits for them, and re-layouts  2.44 us (9%)
  other arithmetic  0.67 us (3%)
    ppermute x4, waiting for transfers between devices, on_device(): received[k] = lax.ppermute(messages[k], 'row', pairs)  9.99 us
    ppermute x4, starting transfers between devices, on_device(): received[k] = lax.ppermute(messages[k], 'row', pairs)  5.84 us
    unnamed x8, local copies, waits for them, and re-layouts  2.4 us
    pallas_call x1, Pallas kernels, on_device(): pl.pallas_call(own_kernel, out_shape=panels_shape, in_specs=[SMEM(), SMEM...  1.38 us
    ppermute x5, waiting for transfers between devices, swap(): return lax.ppermute(x, 'row', other_core)  1.24 us
    ppermute x5, starting transfers between devices, swap(): return lax.ppermute(x, 'row', other_core)  1.2 us
    pallas_call x1, Pallas kernels, on_device(): pl.pallas_call(functools.partial(far_kernel, far), out_shape=[panels_shap...  1.14 us
    pallas_call x1, Pallas kernels, on_device(): pl.pallas_call(unpack_kernel, out_shape=[jax.ShapeDtypeStruct((rows, colu...  0.78 us
  transfers between devices with their start and end apart: 9, of which 3 were waited for; matrix products, arithmetic and copies ran while one was open for 0% of the time, Pallas kernels for 8%

profile of v2, /device:TPU:0, one launch (start us, length us, event | category | flops | bytes accessed | tf_op | source)
XLA Modules:
  0.0 25.5 jit_solution(11949106490019582072)
XLA Ops:
  0.0 0.5 %collective-permute-start.2 = (bf16[18,128,128]{2,1,0:T(8,128)(2,1)}, bf16[18,128,128]{2,1,0:T(8,128)(2,1)S(1)}, u32[]{:S(2)}, u32[]{:S(2)}) collective-permute-start(bf16[18,128,128]{2,1,0:T(8,128)(2,1)} %tiles.1), channel_id=1, source_target_pairs={{0,1},{1,0},{2,3},{3,2},{4,5},{5,4},{6,7},{7,6},{8,9},{9,8},{10,11... | collective-permute-start | bytes 1769480 | tf_op jit(solution)/shard_map/ppermute | solution.py:165
  0.5 0.1 collective-permute-start.3
  0.5 0.5 %collective-permute-start.1 = (s32[2]{0:T(128)}, s32[2]{0:T(128)S(1)}, u32[]{:S(2)}, u32[]{:S(2)}) collective-permute-start(s32[2]{0:T(128)} %count.1), channel_id=1, source_target_pairs={{0,1},{1,0},{2,3},{3,2},{4,5},{5,4},{6,7},{7,6},{8,9},{9,8},{10,11... | collective-permute-start | bytes 32 | tf_op jit(solution)/shard_map/ppermute | solution.py:165
  1.0 0.1 collective-permute-start
  1.0 0.0 copy-start
  1.0 1.1 %copy-done = bf16[18,128,128]{2,1,0:T(8,128)(2,1)S(1)} copy-done((bf16[18,128,128]{2,1,0:T(8,128)(2,1)S(1)}, bf16[18,128,128]{2,1,0:T(8,128)(2,1)}, u32[]{:S(2)}) %copy-start) | copy-done | bytes 589848
  2.1 0.0 copy-start.2
  2.1 0.7 %copy-done.2 = s32[18,2]{0,1:T(2,128)S(1)} copy-done((s32[18,2]{0,1:T(2,128)S(1)}, s32[18,2]{0,1:T(2,128)}, u32[]{:S(2)}) %copy-start.2) | copy-done | bytes 168
  2.8 0.0 copy-start.3
  2.8 0.7 %copy-done.3 = s32[2]{0:T(128)S(1)} copy-done((s32[2]{0:T(128)S(1)}, s32[2]{0:T(128)}, u32[]{:S(2)}) %copy-start.3) | copy-done | bytes 32
  3.4 0.0 copy-start.1
  3.4 1.4 %own_tiles.1._ = bf16[16,512,128]{2,1,0:T(8,128)(2,1)S(1)} custom-call(s32[2,18]{1,0:T(2,128)S(1)} %bitcast.2, s32[2]{0:T(128)S(1)} %copy-done.3, bf16[18,128,128]{2,1,0:T(8,128)(2,1)S(1)} %copy-done), custom_call_target="tpu_custom_call" | custom-call | tf_op jit(solution)/shard_map/own_tiles/pallas_call | solution.py:179
  4.8 0.0 collective-permute-done.1.count
  4.8 0.0 collective-permute-done.index
  4.8 0.0 collective-permute-done.3.other_q
  4.8 0.0 collective-permute-done.2.tiles
  4.9 0.0 copy-done.1
  4.9 1.1 %pack_far.1 = (bf16[16,512,128]{2,1,0:T(8,128)(2,1)S(1)}, bf16[512,128]{1,0:T(8,128)(2,1)S(1)}, s16[528,128]{1,0:T(8,128)(2,1)S(1)}, s16[528,128]{1,0:T(8,128)(2,1)S(1)}) custom-call(s32[2,18]{1,0:T(2,128)S(1)} %collective-permute-done.index, s32[2]{0:T(128)S(1)} %collective-permute-done.1.count, ...), custom_call_target="tpu_custom_call", output_to_operand_aliasing={{0}: (5, {})} | custom-call | tf_op jit(solution)/shard_map/pack_far/pallas_call | solution.py:189
  6.0 3.6 %collective-permute-start.6 = (s16[528,128]{1,0:T(8,128)(2,1)S(1)}, s16[528,128]{1,0:T(8,128)(2,1)S(1)}, u32[]{:S(2)}, u32[]{:S(2)}) collective-permute-start(s16[528,128]{1,0:T(8,128)(2,1)S(1)} %get-tuple-element.19), channel_id=1, source_target_pairs={{0,8},{1,11},{2,10},{3,9},{4,12},{5,15},{6,14},{7,13},{8,0},{9,3},... | collective-permute-start | bytes 405512 | tf_op jit(solution)/shard_map/ppermute | solution.py:213
  9.6 1.5 %collective-permute-start.7 = (s16[528,128]{1,0:T(8,128)(2,1)S(1)}, s16[528,128]{1,0:T(8,128)(2,1)S(1)}, u32[]{:S(2)}, u32[]{:S(2)}) collective-permute-start(s16[528,128]{1,0:T(8,128)(2,1)S(1)} %get-tuple-element.20), channel_id=1, source_target_pairs={{0,12},{1,15},{2,14},{3,13},{4,8},{5,11},{6,10},{7,9},{8,4},{9,7},... | collective-permute-start | bytes 405512 | tf_op jit(solution)/shard_map/ppermute | solution.py:213
  11.1 0.4 %pack_near.1 = (f32[512,128]{1,0:T(8,128)S(1)}, s16[528,128]{1,0:T(8,128)(2,1)S(1)}, s16[528,128]{1,0:T(8,128)(2,1)S(1)}) custom-call(bf16[16,512,128]{2,1,0:T(8,128)(2,1)S(1)} %get-tuple-element.14.panels, bf16[512,128]{1,0:T(8,128)(2,1)S(1)} %get-tuple-element.15.chip_q), custom_call_target="tpu_custom_call" | custom-call | tf_op jit(solution)/shard_map/pack_near/pallas_call | solution.py:198
  11.5 0.7 %collective-permute-start.4 = (s16[528,128]{1,0:T(8,128)(2,1)S(1)}, s16[528,128]{1,0:T(8,128)(2,1)S(1)}, u32[]{:S(2)}, u32[]{:S(2)}) collective-permute-start(s16[528,128]{1,0:T(8,128)(2,1)S(1)} %get-tuple-element.17), channel_id=1, source_target_pairs={{1,3},{3,1},{5,7},{7,5},{9,11},{11,9},{13,15},{15,13},{17,19},{19,... | collective-permute-start | bytes 405512 | tf_op jit(solution)/shard_map/ppermute | solution.py:213
  12.2 0.1 collective-permute-start.5
  12.3 0.3 %local.1.base = f32[512,128]{1,0:T(8,128)S(1)} custom-call(bf16[4,512,128]{2,1,0:T(8,128)(2,1)S(1)} %slice.3.panels, bf16[512,128]{1,0:T(8,128)(2,1)S(1)} %get-tuple-element.15.chip_q, f32[512,128]{1,0:T(8,128)S(1)} %get-tuple-element.16.local_rows), custom_call_target="tpu_custom_call" | custom-call | tf_op jit(solution)/shard_map/local/pallas_call | solution.py:215
  12.7 6.8 %collective-permute-done.6.refs_2_ = s16[528,128]{1,0:T(8,128)(2,1)S(1)} collective-permute-done((s16[528,128]{1,0:T(8,128)(2,1)S(1)}, s16[528,128]{1,0:T(8,128)(2,1)S(1)}, u32[]{:S(2)}, u32[]{:S(2)}) %collective-permute-start.6) | collective-permute-done | bytes 135200 | tf_op jit(solution)/shard_map/ppermute | solution.py:213
  19.5 0.0 collective-permute-done.7.refs_3_
  19.5 0.0 collective-permute-done.4.refs_0_
  19.5 3.1 %collective-permute-done.5.refs_1_ = s16[528,128]{1,0:T(8,128)(2,1)S(1)} collective-permute-done((s16[528,128]{1,0:T(8,128)(2,1)S(1)}, s16[528,128]{1,0:T(8,128)(2,1)S(1)}, u32[]{:S(2)}, u32[]{:S(2)}) %collective-permute-start.5) | collective-permute-done | bytes 135200 | tf_op jit(solution)/shard_map/ppermute | solution.py:213
  22.6 0.8 %unpack.1 = (f32[256,128]{1,0:T(8,128)S(1)}, f32[256,128]{1,0:T(8,128)S(1)}) custom-call(f32[512,128]{1,0:T(8,128)S(1)} %local.1.base, bf16[16,512,128]{2,1,0:T(8,128)(2,1)S(1)} %get-tuple-element.14.panels, s16[528,128]{1,0:T(8,128)(2,1)S(1)} %collective-permute-done.4.refs_0_, s16[528,128]{1,0:T(8,128)(2,1)S(1)} %collective-permute-done.5.refs_1_, ...), custom_call_target="tpu_custom_call" | custom-call | tf_op jit(solution)/shard_map/unpack/pallas_call | solution.py:224
  23.4 0.2 collective-permute-start.8
  23.6 1.2 %collective-permute-done.8 = f32[256,128]{1,0:T(8,128)S(1)} collective-permute-done((f32[256,128]{1,0:T(8,128)S(1)}, f32[256,128]{1,0:T(8,128)S(1)}, u32[]{:S(2)}, u32[]{:S(2)}) %collective-permute-start.8) | collective-permute-done | bytes 131104 | tf_op jit(solution)/shard_map/ppermute | solution.py:165
  24.8 0.7 %add_multiply_fusion = f32[256,128]{1,0:T(8,128)} fusion(f32[256,128]{1,0:T(8,128)S(1)} %get-tuple-element.21, f32[256,128]{1,0:T(8,128)S(1)} %collective-permute-done.8), kind=kLoop, calls=%fused_computation | loop fusion | flops 65536 | bytes 393216 | tf_op jit(solution)/shard_map/mul | solution.py:233
  (1 shorter events, 0.0 us)
Async XLA Ops:
  0.0 4.8 %collective-permute-start.2 = (bf16[18,128,128]{2,1,0:T(8,128)(2,1)}, bf16[18,128,128]{2,1,0:T(8,128)(2,1)S(1)}, u32[]{:S(2)}, u32[]{:S(2)}) collective-permute-start(bf16[18,128,128]{2,1,0:T(8,128)(2,1)} %tiles.1), channel_id=1, source_target_pairs={{0,1},{1,0},{2,3},{3,2},{4,5},{5,4},{6,7},{7,6},{8,9},{9,8},{10,11... | collective-permute-start | bytes 1769480 | tf_op jit(solution)/shard_map/ppermute | solution.py:165
  0.5 4.4 %collective-permute-start.3 = (bf16[256,128]{1,0:T(8,128)(2,1)}, bf16[256,128]{1,0:T(8,128)(2,1)S(1)}, u32[]{:S(2)}, u32[]{:S(2)}) collective-permute-start(bf16[256,128]{1,0:T(8,128)(2,1)} %own_q.1), channel_id=1, source_target_pairs={{0,1},{1,0},{2,3},{3,2},{4,5},{5,4},{6,7},{7,6},{8,9},{9,8},{10,11... | collective-permute-start | bytes 196616 | tf_op jit(solution)/shard_map/ppermute | solution.py:165
  0.5 4.3 %collective-permute-start.1 = (s32[2]{0:T(128)}, s32[2]{0:T(128)S(1)}, u32[]{:S(2)}, u32[]{:S(2)}) collective-permute-start(s32[2]{0:T(128)} %count.1), channel_id=1, source_target_pairs={{0,1},{1,0},{2,3},{3,2},{4,5},{5,4},{6,7},{7,6},{8,9},{9,8},{10,11... | collective-permute-start | bytes 32 | tf_op jit(solution)/shard_map/ppermute | solution.py:165
  1.0 3.9 %collective-permute-start = (s32[2,18]{1,0:T(2,128)}, s32[2,18]{1,0:T(2,128)S(1)}, u32[]{:S(2)}, u32[]{:S(2)}) collective-permute-start(s32[2,18]{1,0:T(2,128)} %bitcast.1), channel_id=1, source_target_pairs={{0,1},{1,0},{2,3},{3,2},{4,5},{5,4},{6,7},{7,6},{8,9},{9,8},{10,11... | collective-permute-start | bytes 440 | tf_op jit(solution)/shard_map/ppermute | solution.py:165
  1.0 1.1 %copy-start = (bf16[18,128,128]{2,1,0:T(8,128)(2,1)S(1)}, bf16[18,128,128]{2,1,0:T(8,128)(2,1)}, u32[]{:S(2)}) copy-start(bf16[18,128,128]{2,1,0:T(8,128)(2,1)} %tiles.1) | copy-start | bytes 1769476
  2.1 0.7 %copy-start.2 = (s32[18,2]{0,1:T(2,128)S(1)}, s32[18,2]{0,1:T(2,128)}, u32[]{:S(2)}) copy-start(s32[18,2]{0,1:T(2,128)} %param.6) | copy-start | bytes 436
  2.8 0.7 %copy-start.3 = (s32[2]{0:T(128)S(1)}, s32[2]{0:T(128)}, u32[]{:S(2)}) copy-start(s32[2]{0:T(128)} %count.1) | copy-start | bytes 28
  3.4 1.4 %copy-start.1 = (bf16[256,128]{1,0:T(8,128)(2,1)S(1)}, bf16[256,128]{1,0:T(8,128)(2,1)}, u32[]{:S(2)}) copy-start(bf16[256,128]{1,0:T(8,128)(2,1)} %own_q.1) | copy-start | bytes 196612
  6.0 13.5 %collective-permute-start.6 = (s16[528,128]{1,0:T(8,128)(2,1)S(1)}, s16[528,128]{1,0:T(8,128)(2,1)S(1)}, u32[]{:S(2)}, u32[]{:S(2)}) collective-permute-start(s16[528,128]{1,0:T(8,128)(2,1)S(1)} %get-tuple-element.19), channel_id=1, source_target_pairs={{0,8},{1,11},{2,10},{3,9},{4,12},{5,15},{6,14},{7,13},{8,0},{9,3},... | collective-permute-start | bytes 405512 | tf_op jit(solution)/shard_map/ppermute | solution.py:213
  9.6 9.9 %collective-permute-start.7 = (s16[528,128]{1,0:T(8,128)(2,1)S(1)}, s16[528,128]{1,0:T(8,128)(2,1)S(1)}, u32[]{:S(2)}, u32[]{:S(2)}) collective-permute-start(s16[528,128]{1,0:T(8,128)(2,1)S(1)} %get-tuple-element.20), channel_id=1, source_target_pairs={{0,12},{1,15},{2,14},{3,13},{4,8},{5,11},{6,10},{7,9},{8,4},{9,7},... | collective-permute-start | bytes 405512 | tf_op jit(solution)/shard_map/ppermute | solution.py:213
  11.5 8.0 %collective-permute-start.4 = (s16[528,128]{1,0:T(8,128)(2,1)S(1)}, s16[528,128]{1,0:T(8,128)(2,1)S(1)}, u32[]{:S(2)}, u32[]{:S(2)}) collective-permute-start(s16[528,128]{1,0:T(8,128)(2,1)S(1)} %get-tuple-element.17), channel_id=1, source_target_pairs={{1,3},{3,1},{5,7},{7,5},{9,11},{11,9},{13,15},{15,13},{17,19},{19,... | collective-permute-start | bytes 405512 | tf_op jit(solution)/shard_map/ppermute | solution.py:213
  12.2 10.5 %collective-permute-start.5 = (s16[528,128]{1,0:T(8,128)(2,1)S(1)}, s16[528,128]{1,0:T(8,128)(2,1)S(1)}, u32[]{:S(2)}, u32[]{:S(2)}) collective-permute-start(s16[528,128]{1,0:T(8,128)(2,1)S(1)} %get-tuple-element.18), channel_id=1, source_target_pairs={{0,4},{1,7},{2,6},{3,5},{4,0},{5,3},{6,2},{7,1},{8,12},{9,15},{10,... | collective-permute-start | bytes 405512 | tf_op jit(solution)/shard_map/ppermute | solution.py:213
  23.4 1.4 %collective-permute-start.8 = (f32[256,128]{1,0:T(8,128)S(1)}, f32[256,128]{1,0:T(8,128)S(1)}, u32[]{:S(2)}, u32[]{:S(2)}) collective-permute-start(f32[256,128]{1,0:T(8,128)S(1)} %get-tuple-element.22), channel_id=1, source_target_pairs={{0,1},{1,0},{2,3},{3,2},{4,5},{5,4},{6,7},{7,6},{8,9},{9,8},{10,11... | collective-permute-start | bytes 393224 | tf_op jit(solution)/shard_map/ppermute | solution.py:165

commit v3 on v2

--- a/solution.py
+++ b/solution.py
@@ -51,8 +51,18 @@
     lax.fori_loop(0, live, put, 0)
 
 
-def own_kernel(index, count, tiles, panels):
+def own_kernel(index_ref, count_ref, tiles_ref, panels, index, count, tiles, sems):
+    copies = [
+        pltpu.make_async_copy(a, b, sems.at[n])
+        for n, (a, b) in enumerate(
+            ((index_ref, index), (count_ref, count), (tiles_ref, tiles))
+        )
+    ]
+    for copy in copies:
+        copy.start()
     panels[...] = jnp.zeros_like(panels)
+    for copy in copies:
+        copy.wait()
     put_tiles(index, count, tiles, panels, panels.shape[1] // panels.shape[2])
 
 
@@ -179,11 +189,17 @@
     own_panels = pl.pallas_call(
         own_kernel,
         out_shape=panels_shape,
-        in_specs=[SMEM(), SMEM(), pl.BlockSpec()],
+        in_specs=[pl.BlockSpec(memory_space=pltpu.HBM)] * 3,
         out_specs=VMEM(),
+        scratch_shapes=[
+            pltpu.SMEM(index.shape, index.dtype),
+            pltpu.SMEM(tile_count.shape, tile_count.dtype),
+            pltpu.VMEM(tile_blocks.shape, tile_blocks.dtype),
+            pltpu.SemaphoreType.DMA((3,)),
+        ],
         compiler_params=params,
         name="own_tiles",
-    )(index, tile_count, tile_blocks)
+    )(*(pltpu.with_memory_space_constraint(a, pltpu.HBM) for a in (index, tile_count, tile_blocks)))
     near = list(reversed(range(slots // 2)))
     far = list(reversed(range(slots // 2, slots)))
     panels, chip_q, *far_messages = pl.pallas_call(

time: 25.7 us -> 23.6 us (0.918)
  local copies, waits for them, and re-layouts: 2.44 us -> 0.04 us
  starting transfers between devices: 7.05 us -> 7.49 us
    unnamed x8 -> x2, local copies, waits for them, and re-layouts: 2.4 us -> 0.01 us
  transfers between devices with their start and end apart: 9 -> 9, of which waited for: 3 -> 3; matrix products, arithmetic and copies ran while one was open for 0% -> 0% of each run, Pallas kernels for 8% -> 9%
where the time goes in v3:
time: 23.6 us; the launch traced here: 23.5 us
  waiting for transfers between devices  11 us (47%)
  starting transfers between devices  7.49 us (32%)
  Pallas kernels  4.14 us (18%)
  other arithmetic  0.67 us (3%)
    ppermute x4, waiting for transfers between devices, on_device(): received[k] = lax.ppermute(messages[k], 'row', pairs)  9.99 us
    ppermute x4, starting transfers between devices, on_device(): received[k] = lax.ppermute(messages[k], 'row', pairs)  6.08 us
    ppermute x5, starting transfers between devices, swap(): return lax.ppermute(x, 'row', other_core)  1.41 us
    pallas_call x1, Pallas kernels, on_device(): pl.pallas_call(own_kernel, out_shape=panels_shape, in_specs=[pl.BlockSpec...  1.4 us
    pallas_call x1, Pallas kernels, on_device(): pl.pallas_call(functools.partial(far_kernel, far), out_shape=[panels_shap...  1.23 us
    ppermute x5, waiting for transfers between devices, swap(): return lax.ppermute(x, 'row', other_core)  1.04 us
    pallas_call x1, Pallas kernels, on_device(): pl.pallas_call(unpack_kernel, out_shape=[jax.ShapeDtypeStruct((rows, colu...  0.78 us
    mul x1, other arithmetic, on_device(): return (keep + swap(send)) * (1.0 / math.sqrt(rows * devices))  0.67 us
  transfers between devices with their start and end apart: 9, of which 3 were waited for; matrix products, arithmetic and copies ran while one was open for 0% of the time, Pallas kernels for 9%

profile of v3, /device:TPU:0, one launch (start us, length us, event | category | flops | bytes accessed | tf_op | source)
XLA Modules:
  0.0 23.5 jit_solution(5570666819196217222)
XLA Ops:
  0.0 0.0 copy-start
  0.0 0.5 %collective-permute-start.2 = (bf16[18,128,128]{2,1,0:T(8,128)(2,1)}, bf16[18,128,128]{2,1,0:T(8,128)(2,1)S(1)}, u32[]{:S(2)}, u32[]{:S(2)}) collective-permute-start(bf16[18,128,128]{2,1,0:T(8,128)(2,1)} %tiles_ref.1), channel_id=1, source_target_pairs={{0,1},{1,0},{2,3},{3,2},{4,5},{5,4},{6,7},{7,6},{8,9},{9,8},{10,11... | collective-permute-start | bytes 1769480 | tf_op jit(solution)/shard_map/ppermute | solution.py:175
  0.5 0.1 collective-permute-start.3
  0.5 0.4 %collective-permute-start.1 = (s32[2]{0:T(128)}, s32[2]{0:T(128)S(1)}, u32[]{:S(2)}, u32[]{:S(2)}) collective-permute-start(s32[2]{0:T(128)} %count_ref.1), channel_id=1, source_target_pairs={{0,1},{1,0},{2,3},{3,2},{4,5},{5,4},{6,7},{7,6},{8,9},{9,8},{10,11... | collective-permute-start | bytes 32 | tf_op jit(solution)/shard_map/ppermute | solution.py:175
  1.0 0.1 collective-permute-start
  1.0 1.4 %own_tiles.1._ = bf16[16,512,128]{2,1,0:T(8,128)(2,1)S(1)} custom-call(s32[2,18]{1,0:T(2,128)} %bitcast.2, s32[2]{0:T(128)} %count_ref.1, bf16[18,128,128]{2,1,0:T(8,128)(2,1)} %tiles_ref.1), custom_call_target="tpu_custom_call" | custom-call | tf_op jit(solution)/shard_map/own_tiles/pallas_call | solution.py:189
  2.4 0.0 collective-permute-done.1.count
  2.5 0.0 collective-permute-done.index
  2.5 0.0 collective-permute-done.3.other_q
  2.5 0.0 collective-permute-done.2.tiles
  2.5 0.0 copy-done
  2.5 1.2 %pack_far.1 = (bf16[16,512,128]{2,1,0:T(8,128)(2,1)S(1)}, bf16[512,128]{1,0:T(8,128)(2,1)S(1)}, s16[528,128]{1,0:T(8,128)(2,1)S(1)}, s16[528,128]{1,0:T(8,128)(2,1)S(1)}) custom-call(s32[2,18]{1,0:T(2,128)S(1)} %collective-permute-done.index, s32[2]{0:T(128)S(1)} %collective-permute-done.1.count, ...), custom_call_target="tpu_custom_call", output_to_operand_aliasing={{0}: (5, {})} | custom-call | tf_op jit(solution)/shard_map/pack_far/pallas_call | solution.py:205
  3.7 3.8 %collective-permute-start.6 = (s16[528,128]{1,0:T(8,128)(2,1)S(1)}, s16[528,128]{1,0:T(8,128)(2,1)S(1)}, u32[]{:S(2)}, u32[]{:S(2)}) collective-permute-start(s16[528,128]{1,0:T(8,128)(2,1)S(1)} %get-tuple-element.19), channel_id=1, source_target_pairs={{0,8},{1,11},{2,10},{3,9},{4,12},{5,15},{6,14},{7,13},{8,0},{9,3},... | collective-permute-start | bytes 405512 | tf_op jit(solution)/shard_map/ppermute | solution.py:229
  7.6 1.4 %collective-permute-start.7 = (s16[528,128]{1,0:T(8,128)(2,1)S(1)}, s16[528,128]{1,0:T(8,128)(2,1)S(1)}, u32[]{:S(2)}, u32[]{:S(2)}) collective-permute-start(s16[528,128]{1,0:T(8,128)(2,1)S(1)} %get-tuple-element.20), channel_id=1, source_target_pairs={{0,12},{1,15},{2,14},{3,13},{4,8},{5,11},{6,10},{7,9},{8,4},{9,7},... | collective-permute-start | bytes 405512 | tf_op jit(solution)/shard_map/ppermute | solution.py:229
  8.9 0.4 %pack_near.1 = (f32[512,128]{1,0:T(8,128)S(1)}, s16[528,128]{1,0:T(8,128)(2,1)S(1)}, s16[528,128]{1,0:T(8,128)(2,1)S(1)}) custom-call(bf16[16,512,128]{2,1,0:T(8,128)(2,1)S(1)} %get-tuple-element.14.panels, bf16[512,128]{1,0:T(8,128)(2,1)S(1)} %get-tuple-element.15.chip_q), custom_call_target="tpu_custom_call" | custom-call | tf_op jit(solution)/shard_map/pack_near/pallas_call | solution.py:214
  9.3 0.7 %collective-permute-start.4 = (s16[528,128]{1,0:T(8,128)(2,1)S(1)}, s16[528,128]{1,0:T(8,128)(2,1)S(1)}, u32[]{:S(2)}, u32[]{:S(2)}) collective-permute-start(s16[528,128]{1,0:T(8,128)(2,1)S(1)} %get-tuple-element.17), channel_id=1, source_target_pairs={{1,3},{3,1},{5,7},{7,5},{9,11},{11,9},{13,15},{15,13},{17,19},{19,... | collective-permute-start | bytes 405512 | tf_op jit(solution)/shard_map/ppermute | solution.py:229
  10.0 0.2 collective-permute-start.5
  10.3 0.3 %local.1.base = f32[512,128]{1,0:T(8,128)S(1)} custom-call(bf16[4,512,128]{2,1,0:T(8,128)(2,1)S(1)} %slice.3.panels, bf16[512,128]{1,0:T(8,128)(2,1)S(1)} %get-tuple-element.15.chip_q, f32[512,128]{1,0:T(8,128)S(1)} %get-tuple-element.16.local_rows), custom_call_target="tpu_custom_call" | custom-call | tf_op jit(solution)/shard_map/local/pallas_call | solution.py:231
  10.6 6.8 %collective-permute-done.6.refs_2_ = s16[528,128]{1,0:T(8,128)(2,1)S(1)} collective-permute-done((s16[528,128]{1,0:T(8,128)(2,1)S(1)}, s16[528,128]{1,0:T(8,128)(2,1)S(1)}, u32[]{:S(2)}, u32[]{:S(2)}) %collective-permute-start.6) | collective-permute-done | bytes 135200 | tf_op jit(solution)/shard_map/ppermute | solution.py:229
  17.4 0.0 collective-permute-done.7.refs_3_
  17.4 0.0 collective-permute-done.4.refs_0_
  17.4 3.1 %collective-permute-done.5.refs_1_ = s16[528,128]{1,0:T(8,128)(2,1)S(1)} collective-permute-done((s16[528,128]{1,0:T(8,128)(2,1)S(1)}, s16[528,128]{1,0:T(8,128)(2,1)S(1)}, u32[]{:S(2)}, u32[]{:S(2)}) %collective-permute-start.5) | collective-permute-done | bytes 135200 | tf_op jit(solution)/shard_map/ppermute | solution.py:229
  20.6 0.8 %unpack.1 = (f32[256,128]{1,0:T(8,128)S(1)}, f32[256,128]{1,0:T(8,128)S(1)}) custom-call(f32[512,128]{1,0:T(8,128)S(1)} %local.1.base, bf16[16,512,128]{2,1,0:T(8,128)(2,1)S(1)} %get-tuple-element.14.panels, s16[528,128]{1,0:T(8,128)(2,1)S(1)} %collective-permute-done.4.refs_0_, s16[528,128]{1,0:T(8,128)(2,1)S(1)} %collective-permute-done.5.refs_1_, ...), custom_call_target="tpu_custom_call" | custom-call | tf_op jit(solution)/shard_map/unpack/pallas_call | solution.py:240
  21.4 0.4 %collective-permute-start.8 = (f32[256,128]{1,0:T(8,128)S(1)}, f32[256,128]{1,0:T(8,128)S(1)}, u32[]{:S(2)}, u32[]{:S(2)}) collective-permute-start(f32[256,128]{1,0:T(8,128)S(1)} %get-tuple-element.22), channel_id=1, source_target_pairs={{0,1},{1,0},{2,3},{3,2},{4,5},{5,4},{6,7},{7,6},{8,9},{9,8},{10,11... | collective-permute-start | bytes 393224 | tf_op jit(solution)/shard_map/ppermute | solution.py:175
  21.8 1.0 %collective-permute-done.8 = f32[256,128]{1,0:T(8,128)S(1)} collective-permute-done((f32[256,128]{1,0:T(8,128)S(1)}, f32[256,128]{1,0:T(8,128)S(1)}, u32[]{:S(2)}, u32[]{:S(2)}) %collective-permute-start.8) | collective-permute-done | bytes 131104 | tf_op jit(solution)/shard_map/ppermute | solution.py:175
  22.8 0.7 %add_multiply_fusion = f32[256,128]{1,0:T(8,128)} fusion(f32[256,128]{1,0:T(8,128)S(1)} %get-tuple-element.21, f32[256,128]{1,0:T(8,128)S(1)} %collective-permute-done.8), kind=kLoop, calls=%fused_computation | loop fusion | flops 65536 | bytes 393216 | tf_op jit(solution)/shard_map/mul | solution.py:249
  (1 shorter events, 0.0 us)
Async XLA Ops:
  0.0 2.5 %copy-start = (bf16[256,128]{1,0:T(8,128)(2,1)S(1)}, bf16[256,128]{1,0:T(8,128)(2,1)}, u32[]{:S(2)}) copy-start(bf16[256,128]{1,0:T(8,128)(2,1)} %own_q.1) | copy-start | bytes 196612
  0.0 2.5 %collective-permute-start.2 = (bf16[18,128,128]{2,1,0:T(8,128)(2,1)}, bf16[18,128,128]{2,1,0:T(8,128)(2,1)S(1)}, u32[]{:S(2)}, u32[]{:S(2)}) collective-permute-start(bf16[18,128,128]{2,1,0:T(8,128)(2,1)} %tiles_ref.1), channel_id=1, source_target_pairs={{0,1},{1,0},{2,3},{3,2},{4,5},{5,4},{6,7},{7,6},{8,9},{9,8},{10,11... | collective-permute-start | bytes 1769480 | tf_op jit(solution)/shard_map/ppermute | solution.py:175
  0.5 2.0 %collective-permute-start.3 = (bf16[256,128]{1,0:T(8,128)(2,1)}, bf16[256,128]{1,0:T(8,128)(2,1)S(1)}, u32[]{:S(2)}, u32[]{:S(2)}) collective-permute-start(bf16[256,128]{1,0:T(8,128)(2,1)} %own_q.1), channel_id=1, source_target_pairs={{0,1},{1,0},{2,3},{3,2},{4,5},{5,4},{6,7},{7,6},{8,9},{9,8},{10,11... | collective-permute-start | bytes 196616 | tf_op jit(solution)/shard_map/ppermute | solution.py:175
  0.5 1.9 %collective-permute-start.1 = (s32[2]{0:T(128)}, s32[2]{0:T(128)S(1)}, u32[]{:S(2)}, u32[]{:S(2)}) collective-permute-start(s32[2]{0:T(128)} %count_ref.1), channel_id=1, source_target_pairs={{0,1},{1,0},{2,3},{3,2},{4,5},{5,4},{6,7},{7,6},{8,9},{9,8},{10,11... | collective-permute-start | bytes 32 | tf_op jit(solution)/shard_map/ppermute | solution.py:175
  1.0 1.5 %collective-permute-start = (s32[2,18]{1,0:T(2,128)}, s32[2,18]{1,0:T(2,128)S(1)}, u32[]{:S(2)}, u32[]{:S(2)}) collective-permute-start(s32[2,18]{1,0:T(2,128)} %bitcast.1), channel_id=1, source_target_pairs={{0,1},{1,0},{2,3},{3,2},{4,5},{5,4},{6,7},{7,6},{8,9},{9,8},{10,11... | collective-permute-start | bytes 440 | tf_op jit(solution)/shard_map/ppermute | solution.py:175
  3.7 13.7 %collective-permute-start.6 = (s16[528,128]{1,0:T(8,128)(2,1)S(1)}, s16[528,128]{1,0:T(8,128)(2,1)S(1)}, u32[]{:S(2)}, u32[]{:S(2)}) collective-permute-start(s16[528,128]{1,0:T(8,128)(2,1)S(1)} %get-tuple-element.19), channel_id=1, source_target_pairs={{0,8},{1,11},{2,10},{3,9},{4,12},{5,15},{6,14},{7,13},{8,0},{9,3},... | collective-permute-start | bytes 405512 | tf_op jit(solution)/shard_map/ppermute | solution.py:229
  7.6 9.9 %collective-permute-start.7 = (s16[528,128]{1,0:T(8,128)(2,1)S(1)}, s16[528,128]{1,0:T(8,128)(2,1)S(1)}, u32[]{:S(2)}, u32[]{:S(2)}) collective-permute-start(s16[528,128]{1,0:T(8,128)(2,1)S(1)} %get-tuple-element.20), channel_id=1, source_target_pairs={{0,12},{1,15},{2,14},{3,13},{4,8},{5,11},{6,10},{7,9},{8,4},{9,7},... | collective-permute-start | bytes 405512 | tf_op jit(solution)/shard_map/ppermute | solution.py:229
  9.3 8.1 %collective-permute-start.4 = (s16[528,128]{1,0:T(8,128)(2,1)S(1)}, s16[528,128]{1,0:T(8,128)(2,1)S(1)}, u32[]{:S(2)}, u32[]{:S(2)}) collective-permute-start(s16[528,128]{1,0:T(8,128)(2,1)S(1)} %get-tuple-element.17), channel_id=1, source_target_pairs={{1,3},{3,1},{5,7},{7,5},{9,11},{11,9},{13,15},{15,13},{17,19},{19,... | collective-permute-start | bytes 405512 | tf_op jit(solution)/shard_map/ppermute | solution.py:229
  10.0 10.6 %collective-permute-start.5 = (s16[528,128]{1,0:T(8,128)(2,1)S(1)}, s16[528,128]{1,0:T(8,128)(2,1)S(1)}, u32[]{:S(2)}, u32[]{:S(2)}) collective-permute-start(s16[528,128]{1,0:T(8,128)(2,1)S(1)} %get-tuple-element.18), channel_id=1, source_target_pairs={{0,4},{1,7},{2,6},{3,5},{4,0},{5,3},{6,2},{7,1},{8,12},{9,15},{10,... | collective-permute-start | bytes 405512 | tf_op jit(solution)/shard_map/ppermute | solution.py:229
  21.4 1.4 %collective-permute-start.8 = (f32[256,128]{1,0:T(8,128)S(1)}, f32[256,128]{1,0:T(8,128)S(1)}, u32[]{:S(2)}, u32[]{:S(2)}) collective-permute-start(f32[256,128]{1,0:T(8,128)S(1)} %get-tuple-element.22), channel_id=1, source_target_pairs={{0,1},{1,0},{2,3},{3,2},{4,5},{5,4},{6,7},{7,6},{8,9},{9,8},{10,11... | collective-permute-start | bytes 393224 | tf_op jit(solution)/shard_map/ppermute | solution.py:175

commit v4 on v3

v4 whole, which is shorter than its diff:
```python
import functools
import math

import jax
import jax.numpy as jnp
from jax import lax
from jax.experimental import pallas as pl
from jax.experimental.pallas import tpu as pltpu
from jax.sharding import PartitionSpec as P

TOP = 32700.0
STEPS = 16.0
LEAST = 1e-30


def place():
    me = lax.axis_index("row")
    return me // 2, me % 2


def scale_of(code):
    return jnp.exp2(code * (1.0 / STEPS))


def encode(x):
    top = jnp.maximum(jnp.max(jnp.abs(x), axis=0, keepdims=True), LEAST)
    code = jnp.ceil(jnp.log2(top) * STEPS)
    values = jnp.round(x * (TOP / scale_of(code)))
    return values.astype(jnp.int32).astype(jnp.int16), code


def put_tiles(index, count, tiles, panels, chip_blocks):
    chip, core = place()
    tile = tiles.shape[1]
    live = count[0]
    for r in range(1, count.shape[0]):
        live = live + count[r]

    def put(s, carry):
        i, j = index[0, s], index[1, s]
        cls = chip ^ (j // chip_blocks)

        @pl.when(cls % 2 == core)
        def _():
            panel = (cls // 2) * chip_blocks + j % chip_blocks
            at = pl.multiple_of((i % chip_blocks) * tile, tile)
            panels[panel, pl.ds(at, tile), :] = tiles[s]

        return carry

    lax.fori_loop(0, live, put, 0)


def own_kernel(index_ref, count_ref, tiles_ref, panels, index, count, tiles, sems):
    copies = [
        pltpu.make_async_copy(a, b, sems.at[n])
        for n, (a, b) in enumerate(
            ((index_ref, index), (count_ref, count), (tiles_ref, tiles))
        )
    ]
    for copy in copies:
        copy.start()
    panels[...] = jnp.zeros_like(panels)
    for copy in copies:
        copy.wait()
    put_tiles(index, count, tiles, panels, panels.shape[1] // panels.shape[2])


def write_message(message, blocks):
    tile = message.shape[1]
    codes = []
    for b, x in enumerate(blocks):
        values, code = encode(x)
        message[b * tile:(b + 1) * tile, :] = values
        codes.append(code)
    which = lax.broadcasted_iota(jnp.int32, (16, tile), 0)
    tail = jnp.zeros((16, tile), jnp.float32)
    for b, code in enumerate(codes):
        tail = jnp.where(which == b, code, tail)
    message[len(blocks) * tile:, :] = tail.astype(jnp.int32).astype(jnp.int16)


def read_message(message):
    tile = message.shape[1]
    blocks = message.shape[0] // tile
    tail = message[blocks * tile:, :].astype(jnp.int32).astype(jnp.float32)
    scales = scale_of(tail) * (1.0 / TOP)
    return [
        message[b * tile:(b + 1) * tile, :].astype(jnp.int32).astype(jnp.float32)
        * scales[b:b + 1, :]
        for b in range(blocks)
    ]


def mirrored_blocks(q_t, panels, slot):
    tile = panels.shape[2]
    chip_blocks = panels.shape[1] // tile
    blocks = []
    for g in range(slot * chip_blocks, (slot + 1) * chip_blocks, 2):
        pair = jnp.concatenate([panels[g], panels[g + 1]], axis=1)
        sums = jnp.dot(q_t, pair, preferred_element_type=jnp.float32)
        blocks += [sums[:, :tile], sums[:, tile:]]
    return blocks


def direct_sum(panels, slot, blocks):
    tile = panels.shape[2]
    chip_blocks = panels.shape[1] // tile
    total = None
    for b in range(0, chip_blocks, 2):
        g = slot * chip_blocks + b
        pair = jnp.concatenate([panels[g], panels[g + 1]], axis=1)
        q = jnp.concatenate(blocks[b:b + 2], axis=0).astype(jnp.bfloat16)
        part = jnp.dot(pair, q, preferred_element_type=jnp.float32)
        total = part if total is None else total + part
    return total


def split(x, tile):
    return [x[at:at + tile, :] for at in range(0, x.shape[0], tile)]


def in_lower_half(chips):
    return place()[0] < chips // 2


def far_kernel(
    chips, slots, index, count, tiles, own_q, other_q, _, panels, chip_q, *messages
):
    rows, tile = own_q.shape[0], panels.shape[2]
    _, core = place()
    chip_q[pl.ds(pl.multiple_of(core * rows, rows), rows), :] = own_q[...]
    chip_q[pl.ds(pl.multiple_of((1 - core) * rows, rows), rows), :] = other_q[...]

    @pl.when(in_lower_half(chips))
    def _():
        put_tiles(index, count, tiles, panels, panels.shape[1] // tile)
        q_t = chip_q[...].T
        for k, message in zip(slots, messages, strict=True):
            write_message(message, mirrored_blocks(q_t, panels, k))

    @pl.when(jnp.logical_not(in_lower_half(chips)))
    def _():
        write_message(messages[0], split(chip_q[...].astype(jnp.float32), tile))
        for message in messages[1:]:
            message[...] = messages[0][...]


def near_kernel(
    chips, slots, index, count, tiles, _, chip_q, panels, local_rows, *messages
):
    tile = panels.shape[2]
    chip, core = place()

    @pl.when(jnp.logical_not(in_lower_half(chips)))
    def _():
        put_tiles(index, count, tiles, panels, panels.shape[1] // tile)

    q = chip_q[...]
    q_t = q.T
    q_wide = q.astype(jnp.float32)
    for k, message in zip(slots, messages, strict=True):
        up = chip < (chip ^ (2 * k + core))
        blocks = mirrored_blocks(q_t, panels, k)
        if k == 0:
            for b, m in enumerate(blocks):
                local_rows[b * tile:(b + 1) * tile, :] = m
        write_message(
            message,
            [
                jnp.where(up, m, own)
                for m, own in zip(blocks, split(q_wide, tile), strict=True)
            ],
        )


def gather_part(slots, base, panels, received):
    tile = panels.shape[2]
    chip, core = place()
    total, mirrored = base
    for k, message in zip(slots, received, strict=True):
        low = (chip ^ (2 * k + core)) < chip
        blocks = read_message(message)
        mirrored = [
            m + jnp.where(low, x, 0.0) for m, x in zip(mirrored, blocks, strict=True)
        ]
        total = total + direct_sum(panels, k, blocks)
    return total, mirrored


def early_kernel(slots, panels, chip_q, local_rows, *refs):
    *received, direct, mirror = refs
    tile = panels.shape[2]
    _, core = place()
    total = direct_sum(panels, 0, split(chip_q[...], tile))
    base = (
        jnp.where(core == 0, total, 0.0),
        [jnp.where(core == 0, m, 0.0) for m in split(local_rows[...], tile)],
    )
    total, mirrored = gather_part(slots, base, panels, received)
    direct[...] = total
    for b, m in enumerate(mirrored):
        mirror[b * tile:(b + 1) * tile, :] = m


def late_kernel(slots, panels, direct, mirror, *refs):
    *received, keep, send, result = refs
    rows, tile = keep.shape[0], panels.shape[2]
    _, core = place()
    total, mirrored = gather_part(
        slots, (direct[...], split(mirror[...], tile)), panels, received
    )
    for b, (block, m) in enumerate(zip(split(total, tile), mirrored, strict=True)):
        result[b * tile:(b + 1) * tile, :] = block + m.T
    keep[...] = result[pl.ds(pl.multiple_of(core * rows, rows), rows), :]
    send[...] = result[pl.ds(pl.multiple_of((1 - core) * rows, rows), rows), :]


VMEM = functools.partial(pl.BlockSpec, memory_space=pltpu.VMEM)
SMEM = functools.partial(pl.BlockSpec, memory_space=pltpu.SMEM)


def on_device(devices, tile_blocks, q_block, tile_index, tile_count):
    tile = tile_blocks.shape[1]
    rows, columns = q_block.shape
    chips = devices // 2
    slots = chips // 2
    chip_rows = 2 * rows
    chip_blocks = chip_rows // tile
    wide = jnp.float32
    other_core = [(d, d ^ 1) for d in range(devices)]

    def swap(x):
        return lax.ppermute(x, "row", other_core)

    index = tile_index.T
    other_tiles = swap(tile_blocks)
    other_q = swap(q_block)
    other_index = swap(index)
    other_count = swap(tile_count)

    panels_shape = jax.ShapeDtypeStruct(
        (slots * chip_blocks, chip_rows, tile), jnp.bfloat16
    )
    q_shape = jax.ShapeDtypeStruct((chip_rows, columns), jnp.bfloat16)
    message = jax.ShapeDtypeStruct((chip_rows + 16, columns), jnp.int16)
    params = pltpu.CompilerParams(vmem_limit_bytes=48 * 2**20)
    own_panels = pl.pallas_call(
        own_kernel,
        out_shape=panels_shape,
        in_specs=[pl.BlockSpec(memory_space=pltpu.HBM)] * 3,
        out_specs=VMEM(),
        scratch_shapes=[
            pltpu.SMEM(index.shape, index.dtype),
            pltpu.SMEM(tile_count.shape, tile_count.dtype),
            pltpu.VMEM(tile_blocks.shape, tile_blocks.dtype),
            pltpu.SemaphoreType.DMA((3,)),
        ],
        compiler_params=params,
        name="own_tiles",
    )(*(pltpu.with_memory_space_constraint(a, pltpu.HBM) for a in (index, tile_count, tile_blocks)))
    far = list(range(slots // 2, slots))
    near = list(reversed(range(slots // 2)))
    wide_shape = jax.ShapeDtypeStruct((chip_rows, columns), wide)
    panels, chip_q, *far_messages = pl.pallas_call(
        functools.partial(far_kernel, chips, far),
        out_shape=[panels_shape, q_shape] + [message] * len(far),
        in_specs=[SMEM(), SMEM(), VMEM(), pl.BlockSpec(), VMEM(), VMEM()],
        out_specs=[VMEM()] * (2 + len(far)),
        input_output_aliases={5: 0},
        compiler_params=params,
        name="pack_far",
    )(other_index, other_count, other_tiles, q_block, other_q, own_panels)
    panels, local_rows, *near_messages = pl.pallas_call(
        functools.partial(near_kernel, chips, near),
        out_shape=[panels_shape, wide_shape] + [message] * len(near),
        in_specs=[SMEM(), SMEM()] + [VMEM()] * 3,
        out_specs=[VMEM()] * (2 + len(near)),
        input_output_aliases={3: 0},
        compiler_params=params,
        name="pack_near",
    )(other_index, other_count, other_tiles, panels, chip_q)
    messages = dict(zip(far + near, far_messages + near_messages, strict=True))
    received = {
        k: lax.ppermute(messages[k], "row", [
            (d, d ^ (2 * (2 * k + d % 2))) for d in range(devices) if 2 * k + d % 2
        ])
        for k in far + near
    }

    early = [far[0]]
    late = [k for k in far + near if k not in early]
    direct, mirror = pl.pallas_call(
        functools.partial(early_kernel, early),
        out_shape=[wide_shape] * 2,
        in_specs=[VMEM()] * (3 + len(early)),
        out_specs=[VMEM()] * 2,
        compiler_params=params,
        name="gather_early",
    )(panels, chip_q, local_rows, *(received[k] for k in early))
    keep, send = pl.pallas_call(
        functools.partial(late_kernel, late),
        out_shape=[jax.ShapeDtypeStruct((rows, columns), wide)] * 2,
        in_specs=[VMEM()] * (3 + len(late)),
        out_specs=[VMEM()] * 2,
        scratch_shapes=[pltpu.VMEM((chip_rows, columns), wide)],
        compiler_params=params,
        name="gather_late",
    )(panels, direct, mirror, *(received[k] for k in late))
    return (keep + swap(send)) * (1.0 / math.sqrt(rows * devices))


def solution(mesh):
    return jax.shard_map(
        functools.partial(on_device, mesh.shape["row"]),
        mesh=mesh,
        in_specs=(
            P(("grp", "row"), None, None),
            P(("grp", "row"), None),
            P(("grp", "row"), None),
            P(("grp", "row")),
        ),
        out_specs=P(("grp", "row"), None),
        check_vma=False,
    )
```

time: 23.6 us -> 22.5 us (0.953)
  waiting for transfers between devices: 11 us -> 7.6 us
  starting transfers between devices: 7.49 us -> 9.26 us
  Pallas kernels: 4.14 us -> 4.75 us
    ppermute x4, waiting for transfers between devices: 9.99 us -> 6.6 us  [on_device(): lax.ppermute(messages[k], 'row', [(d, d ^ 2 * (2 * k + d % 2)) for d in r...]
    ppermute x5, starting transfers between devices: 1.41 us -> 3.27 us  [swap(): return lax.ppermute(x, 'row', other_core)]
    pallas_call x4, Pallas kernels: 2.74 us -> 3.2 us  [the longest x1 1.13 us: on_device(): pl.pallas_call(functools.partial(far_kernel, chips, far), out_shape=[pane...]
  transfers between devices with their start and end apart: 9 -> 9, of which waited for: 3 -> 4; matrix products, arithmetic and copies ran while one was open for 0% -> 0% of each run, Pallas kernels for 9% -> 13%
where the time goes in v4:
time: 22.5 us; the launch traced here: 22.4 us
  starting transfers between devices  9.26 us (41%)
  waiting for transfers between devices  7.6 us (34%)
  Pallas kernels  4.75 us (21%)
  other arithmetic  0.67 us (3%)
    ppermute x4, waiting for transfers between devices, on_device(): lax.ppermute(messages[k], 'row', [(d, d ^ 2 * (2 * k + d % 2)) for d in r...  6.6 us
    ppermute x4, starting transfers between devices, on_device(): lax.ppermute(messages[k], 'row', [(d, d ^ 2 * (2 * k + d % 2)) for d in r...  5.99 us
    ppermute x5, starting transfers between devices, swap(): return lax.ppermute(x, 'row', other_core)  3.27 us
    pallas_call x1, Pallas kernels, on_device(): pl.pallas_call(own_kernel, out_shape=panels_shape, in_specs=[pl.BlockSpec...  1.55 us
    pallas_call x1, Pallas kernels, on_device(): pl.pallas_call(functools.partial(far_kernel, chips, far), out_shape=[pane...  1.13 us
    ppermute x5, waiting for transfers between devices, swap(): return lax.ppermute(x, 'row', other_core)  1 us
    pallas_call x1, Pallas kernels, on_device(): pl.pallas_call(functools.partial(near_kernel, chips, near), out_shape=[pa...  0.98 us
    mul x1, other arithmetic, on_device(): return (keep + swap(send)) * (1.0 / math.sqrt(rows * devices))  0.67 us
  transfers between devices with their start and end apart: 9, of which 4 were waited for; matrix products, arithmetic and copies ran while one was open for 0% of the time, Pallas kernels for 13%

profile of v4, /device:TPU:0, one launch (start us, length us, event | category | flops | bytes accessed | tf_op | source)
XLA Modules:
  0.0 22.4 jit_solution(9827789116737577738)
XLA Ops:
  0.0 0.0 copy-start
  0.0 0.5 %collective-permute-start.2 = (bf16[18,128,128]{2,1,0:T(8,128)(2,1)}, bf16[18,128,128]{2,1,0:T(8,128)(2,1)S(1)}, u32[]{:S(2)}, u32[]{:S(2)}) collective-permute-start(bf16[18,128,128]{2,1,0:T(8,128)(2,1)} %tiles_ref.1), channel_id=1, source_target_pairs={{0,1},{1,0},{2,3},{3,2},{4,5},{5,4},{6,7},{7,6},{8,9},{9,8},{10,11... | collective-permute-start | bytes 1769480 | tf_op jit(solution)/shard_map/ppermute | solution.py:234
  0.5 0.1 collective-permute-start.3
  0.5 0.4 %collective-permute-start.1 = (s32[2]{0:T(128)}, s32[2]{0:T(128)S(1)}, u32[]{:S(2)}, u32[]{:S(2)}) collective-permute-start(s32[2]{0:T(128)} %count_ref.1), channel_id=1, source_target_pairs={{0,1},{1,0},{2,3},{3,2},{4,5},{5,4},{6,7},{7,6},{8,9},{9,8},{10,11... | collective-permute-start | bytes 32 | tf_op jit(solution)/shard_map/ppermute | solution.py:234
  1.0 0.1 collective-permute-start
  1.0 1.5 %own_tiles.1._ = bf16[16,512,128]{2,1,0:T(8,128)(2,1)S(1)} custom-call(s32[2,18]{1,0:T(2,128)} %bitcast.2, s32[2]{0:T(128)} %count_ref.1, bf16[18,128,128]{2,1,0:T(8,128)(2,1)} %tiles_ref.1), custom_call_target="tpu_custom_call" | custom-call | tf_op jit(solution)/shard_map/own_tiles/pallas_call | solution.py:248
  2.6 0.0 collective-permute-done.1.count
  2.6 0.0 collective-permute-done.index
  2.6 0.0 collective-permute-done.3.other_q
  2.6 0.0 collective-permute-done.2.tiles
  2.6 0.0 copy-done
  2.6 1.1 %pack_far.1 = (bf16[16,512,128]{2,1,0:T(8,128)(2,1)S(1)}, bf16[512,128]{1,0:T(8,128)(2,1)S(1)}, s16[528,128]{1,0:T(8,128)(2,1)S(1)}, s16[528,128]{1,0:T(8,128)(2,1)S(1)}) custom-call(s32[2,18]{1,0:T(2,128)S(1)} %collective-permute-done.index, s32[2]{0:T(128)S(1)} %collective-permute-done.1.count, ...), custom_call_target="tpu_custom_call", output_to_operand_aliasing={{0}: (5, {})} | custom-call | tf_op jit(solution)/shard_map/pack_far/pallas_call | solution.py:265
  3.8 3.3 %collective-permute-start.4 = (s16[528,128]{1,0:T(8,128)(2,1)S(1)}, s16[528,128]{1,0:T(8,128)(2,1)S(1)}, u32[]{:S(2)}, u32[]{:S(2)}) collective-permute-start(s16[528,128]{1,0:T(8,128)(2,1)S(1)} %get-tuple-element.21), channel_id=1, source_target_pairs={{0,8},{1,11},{2,10},{3,9},{4,12},{5,15},{6,14},{7,13},{8,0},{9,3},... | collective-permute-start | bytes 405512 | tf_op jit(solution)/shard_map/ppermute | solution.py:285
  7.1 1.0 %pack_near.1 = (bf16[16,512,128]{2,1,0:T(8,128)(2,1)S(1)}, f32[512,128]{1,0:T(8,128)S(1)}, s16[528,128]{1,0:T(8,128)(2,1)S(1)}, s16[528,128]{1,0:T(8,128)(2,1)S(1)}) custom-call(s32[2,18]{1,0:T(2,128)S(1)} %collective-permute-done.index, s32[2]{0:T(128)S(1)} %collective-permute-done.1.count, ...), custom_call_target="tpu_custom_call", output_to_operand_aliasing={{0}: (3, {})} | custom-call | tf_op jit(solution)/shard_map/pack_near/pallas_call | solution.py:274
  8.1 1.6 %collective-permute-start.6 = (s16[528,128]{1,0:T(8,128)(2,1)S(1)}, s16[528,128]{1,0:T(8,128)(2,1)S(1)}, u32[]{:S(2)}, u32[]{:S(2)}) collective-permute-start(s16[528,128]{1,0:T(8,128)(2,1)S(1)} %get-tuple-element.25), channel_id=1, source_target_pairs={{0,4},{1,7},{2,6},{3,5},{4,0},{5,3},{6,2},{7,1},{8,12},{9,15},{10,... | collective-permute-start | bytes 405512 | tf_op jit(solution)/shard_map/ppermute | solution.py:285
  9.7 0.7 %collective-permute-start.7 = (s16[528,128]{1,0:T(8,128)(2,1)S(1)}, s16[528,128]{1,0:T(8,128)(2,1)S(1)}, u32[]{:S(2)}, u32[]{:S(2)}) collective-permute-start(s16[528,128]{1,0:T(8,128)(2,1)S(1)} %get-tuple-element.26), channel_id=1, source_target_pairs={{1,3},{3,1},{5,7},{7,5},{9,11},{11,9},{13,15},{15,13},{17,19},{19,... | collective-permute-start | bytes 405512 | tf_op jit(solution)/shard_map/ppermute | solution.py:285
  10.4 0.4 %collective-permute-start.5 = (s16[528,128]{1,0:T(8,128)(2,1)S(1)}, s16[528,128]{1,0:T(8,128)(2,1)S(1)}, u32[]{:S(2)}, u32[]{:S(2)}) collective-permute-start(s16[528,128]{1,0:T(8,128)(2,1)S(1)} %get-tuple-element.24), channel_id=1, source_target_pairs={{0,12},{1,15},{2,14},{3,13},{4,8},{5,11},{6,10},{7,9},{8,4},{9,7},... | collective-permute-start | bytes 405512 | tf_op jit(solution)/shard_map/ppermute | solution.py:285
  10.8 2.8 %collective-permute-done.4.refs_0_ = s16[528,128]{1,0:T(8,128)(2,1)S(1)} collective-permute-done((s16[528,128]{1,0:T(8,128)(2,1)S(1)}, s16[528,128]{1,0:T(8,128)(2,1)S(1)}, u32[]{:S(2)}, u32[]{:S(2)}) %collective-permute-start.4) | collective-permute-done | bytes 135200 | tf_op jit(solution)/shard_map/ppermute | solution.py:285
  13.6 0.4 %gather_early.1 = (f32[512,128]{1,0:T(8,128)S(1)}, f32[512,128]{1,0:T(8,128)S(1)}) custom-call(bf16[16,512,128]{2,1,0:T(8,128)(2,1)S(1)} %get-tuple-element.19.panels, bf16[512,128]{1,0:T(8,128)(2,1)S(1)} %get-tuple-element.18.chip_q, f32[512,128]{1,0:T(8,128)S(1)} %get-tuple-element.20.local_rows, s16[528,128]{1,0:T(8,128)(2,1)S(1)} %collective-permute-done.4.refs_0_), custom_call_target="tpu_custom_call" | custom-call | tf_op jit(solution)/shard_map/gather_early/pallas_call | solution.py:293
  14.0 1.4 %collective-permute-done.6.refs_1_ = s16[528,128]{1,0:T(8,128)(2,1)S(1)} collective-permute-done((s16[528,128]{1,0:T(8,128)(2,1)S(1)}, s16[528,128]{1,0:T(8,128)(2,1)S(1)}, u32[]{:S(2)}, u32[]{:S(2)}) %collective-permute-start.6) | collective-permute-done | bytes 135200 | tf_op jit(solution)/shard_map/ppermute | solution.py:285
  15.4 0.0 collective-permute-done.7.refs_2_
  15.4 2.4 %collective-permute-done.5.refs_0_ = s16[528,128]{1,0:T(8,128)(2,1)S(1)} collective-permute-done((s16[528,128]{1,0:T(8,128)(2,1)S(1)}, s16[528,128]{1,0:T(8,128)(2,1)S(1)}, u32[]{:S(2)}, u32[]{:S(2)}) %collective-permute-start.5) | collective-permute-done | bytes 135200 | tf_op jit(solution)/shard_map/ppermute | solution.py:285
  17.8 0.6 %gather_late.1 = (f32[256,128]{1,0:T(8,128)S(1)}, f32[256,128]{1,0:T(8,128)S(1)}) custom-call(bf16[16,512,128]{2,1,0:T(8,128)(2,1)S(1)} %get-tuple-element.19.panels, f32[512,128]{1,0:T(8,128)S(1)} %get-tuple-element.22.direct, f32[512,128]{1,0:T(8,128)S(1)} %get-tuple-element.23.mirror, s16[528,128]{1,0:T(8,128)(2,1)S(1)} %collective-permute-done.5.refs_0_, ...), custom_call_target="tpu_custom_call" | custom-call | tf_op jit(solution)/shard_map/gather_late/pallas_call | solution.py:301
  18.5 2.2 %collective-permute-start.8 = (f32[256,128]{1,0:T(8,128)S(1)}, f32[256,128]{1,0:T(8,128)S(1)}, u32[]{:S(2)}, u32[]{:S(2)}) collective-permute-start(f32[256,128]{1,0:T(8,128)S(1)} %get-tuple-element.28), channel_id=1, source_target_pairs={{0,1},{1,0},{2,3},{3,2},{4,5},{5,4},{6,7},{7,6},{8,9},{9,8},{10,11... | collective-permute-start | bytes 393224 | tf_op jit(solution)/shard_map/ppermute | solution.py:234
  20.7 1.0 %collective-permute-done.8 = f32[256,128]{1,0:T(8,128)S(1)} collective-permute-done((f32[256,128]{1,0:T(8,128)S(1)}, f32[256,128]{1,0:T(8,128)S(1)}, u32[]{:S(2)}, u32[]{:S(2)}) %collective-permute-start.8) | collective-permute-done | bytes 131104 | tf_op jit(solution)/shard_map/ppermute | solution.py:234
  21.7 0.7 %add_multiply_fusion = f32[256,128]{1,0:T(8,128)} fusion(f32[256,128]{1,0:T(8,128)S(1)} %get-tuple-element.27, f32[256,128]{1,0:T(8,128)S(1)} %collective-permute-done.8), kind=kLoop, calls=%fused_computation | loop fusion | flops 65536 | bytes 393216 | tf_op jit(solution)/shard_map/mul | solution.py:310
Async XLA Ops:
  0.0 2.6 %copy-start = (bf16[256,128]{1,0:T(8,128)(2,1)S(1)}, bf16[256,128]{1,0:T(8,128)(2,1)}, u32[]{:S(2)}) copy-start(bf16[256,128]{1,0:T(8,128)(2,1)} %own_q.1) | copy-start | bytes 196612
  0.0 2.6 %collective-permute-start.2 = (bf16[18,128,128]{2,1,0:T(8,128)(2,1)}, bf16[18,128,128]{2,1,0:T(8,128)(2,1)S(1)}, u32[]{:S(2)}, u32[]{:S(2)}) collective-permute-start(bf16[18,128,128]{2,1,0:T(8,128)(2,1)} %tiles_ref.1), channel_id=1, source_target_pairs={{0,1},{1,0},{2,3},{3,2},{4,5},{5,4},{6,7},{7,6},{8,9},{9,8},{10,11... | collective-permute-start | bytes 1769480 | tf_op jit(solution)/shard_map/ppermute | solution.py:234
  0.5 2.2 %collective-permute-start.3 = (bf16[256,128]{1,0:T(8,128)(2,1)}, bf16[256,128]{1,0:T(8,128)(2,1)S(1)}, u32[]{:S(2)}, u32[]{:S(2)}) collective-permute-start(bf16[256,128]{1,0:T(8,128)(2,1)} %own_q.1), channel_id=1, source_target_pairs={{0,1},{1,0},{2,3},{3,2},{4,5},{5,4},{6,7},{7,6},{8,9},{9,8},{10,11... | collective-permute-start | bytes 196616 | tf_op jit(solution)/shard_map/ppermute | solution.py:234
  0.5 2.1 %collective-permute-start.1 = (s32[2]{0:T(128)}, s32[2]{0:T(128)S(1)}, u32[]{:S(2)}, u32[]{:S(2)}) collective-permute-start(s32[2]{0:T(128)} %count_ref.1), channel_id=1, source_target_pairs={{0,1},{1,0},{2,3},{3,2},{4,5},{5,4},{6,7},{7,6},{8,9},{9,8},{10,11... | collective-permute-start | bytes 32 | tf_op jit(solution)/shard_map/ppermute | solution.py:234
  1.0 1.6 %collective-permute-start = (s32[2,18]{1,0:T(2,128)}, s32[2,18]{1,0:T(2,128)S(1)}, u32[]{:S(2)}, u32[]{:S(2)}) collective-permute-start(s32[2,18]{1,0:T(2,128)} %bitcast.1), channel_id=1, source_target_pairs={{0,1},{1,0},{2,3},{3,2},{4,5},{5,4},{6,7},{7,6},{8,9},{9,8},{10,11... | collective-permute-start | bytes 440 | tf_op jit(solution)/shard_map/ppermute | solution.py:234
  3.8 9.8 %collective-permute-start.4 = (s16[528,128]{1,0:T(8,128)(2,1)S(1)}, s16[528,128]{1,0:T(8,128)(2,1)S(1)}, u32[]{:S(2)}, u32[]{:S(2)}) collective-permute-start(s16[528,128]{1,0:T(8,128)(2,1)S(1)} %get-tuple-element.21), channel_id=1, source_target_pairs={{0,8},{1,11},{2,10},{3,9},{4,12},{5,15},{6,14},{7,13},{8,0},{9,3},... | collective-permute-start | bytes 405512 | tf_op jit(solution)/shard_map/ppermute | solution.py:285
  8.1 7.3 %collective-permute-start.6 = (s16[528,128]{1,0:T(8,128)(2,1)S(1)}, s16[528,128]{1,0:T(8,128)(2,1)S(1)}, u32[]{:S(2)}, u32[]{:S(2)}) collective-permute-start(s16[528,128]{1,0:T(8,128)(2,1)S(1)} %get-tuple-element.25), channel_id=1, source_target_pairs={{0,4},{1,7},{2,6},{3,5},{4,0},{5,3},{6,2},{7,1},{8,12},{9,15},{10,... | collective-permute-start | bytes 405512 | tf_op jit(solution)/shard_map/ppermute | solution.py:285
  9.7 5.7 %collective-permute-start.7 = (s16[528,128]{1,0:T(8,128)(2,1)S(1)}, s16[528,128]{1,0:T(8,128)(2,1)S(1)}, u32[]{:S(2)}, u32[]{:S(2)}) collective-permute-start(s16[528,128]{1,0:T(8,128)(2,1)S(1)} %get-tuple-element.26), channel_id=1, source_target_pairs={{1,3},{3,1},{5,7},{7,5},{9,11},{11,9},{13,15},{15,13},{17,19},{19,... | collective-permute-start | bytes 405512 | tf_op jit(solution)/shard_map/ppermute | solution.py:285
  10.4 7.4 %collective-permute-start.5 = (s16[528,128]{1,0:T(8,128)(2,1)S(1)}, s16[528,128]{1,0:T(8,128)(2,1)S(1)}, u32[]{:S(2)}, u32[]{:S(2)}) collective-permute-start(s16[528,128]{1,0:T(8,128)(2,1)S(1)} %get-tuple-element.24), channel_id=1, source_target_pairs={{0,12},{1,15},{2,14},{3,13},{4,8},{5,11},{6,10},{7,9},{8,4},{9,7},... | collective-permute-start | bytes 405512 | tf_op jit(solution)/shard_map/ppermute | solution.py:285
  18.5 3.2 %collective-permute-start.8 = (f32[256,128]{1,0:T(8,128)S(1)}, f32[256,128]{1,0:T(8,128)S(1)}, u32[]{:S(2)}, u32[]{:S(2)}) collective-permute-start(f32[256,128]{1,0:T(8,128)S(1)} %get-tuple-element.28), channel_id=1, source_target_pairs={{0,1},{1,0},{2,3},{3,2},{4,5},{5,4},{6,7},{7,6},{8,9},{9,8},{10,11... | collective-permute-start | bytes 393224 | tf_op jit(solution)/shard_map/ppermute | solution.py:234

commit v5 on v4

v5 whole, which is shorter than its diff:
```python
import functools
import math

import jax
import jax.numpy as jnp
from jax import lax
from jax.experimental import pallas as pl
from jax.experimental.pallas import tpu as pltpu
from jax.sharding import PartitionSpec as P

TOP = 32700.0
STEPS = 16.0
LEAST = 1e-30


def place():
    me = lax.axis_index("row")
    return me // 2, me % 2


def scale_of(code):
    return jnp.exp2(code * (1.0 / STEPS))


def encode(x):
    top = jnp.maximum(jnp.max(jnp.abs(x), axis=0, keepdims=True), LEAST)
    code = jnp.ceil(jnp.log2(top) * STEPS)
    values = jnp.round(x * (TOP / scale_of(code)))
    return values.astype(jnp.int32).astype(jnp.int16), code


def live_tiles(count):
    live = count[0]
    for r in range(1, count.shape[0]):
        live = live + count[r]
    return live


def put_tiles(index, count, tiles, panels, chip_blocks):
    chip, core = place()
    tile = tiles.shape[1]
    local = panels.shape[0] // chip_blocks - 1
    live = live_tiles(count)

    def put(s, carry):
        i, j = index[0, s], index[1, s]
        cls = chip ^ (j // chip_blocks)

        @pl.when((cls == 0) | (cls % 2 == core))
        def _():
            slot = jnp.where(cls == 0, local, cls // 2)
            panel = slot * chip_blocks + j % chip_blocks
            at = pl.multiple_of((i % chip_blocks) * tile, tile)
            panels[panel, pl.ds(at, tile), :] = tiles[s]

        return carry

    lax.fori_loop(0, live, put, 0)


def fetch(sems, *pairs):
    copies = [
        pltpu.make_async_copy(a, b, sems.at[n]) for n, (a, b) in enumerate(pairs)
    ]
    for copy in copies:
        copy.start()
    return copies


def own_kernel(index_ref, count_ref, tiles_ref, panels, index, count, tiles, sems):
    copies = fetch(sems, (index_ref, index), (count_ref, count), (tiles_ref, tiles))
    panels[...] = jnp.zeros_like(panels)
    for copy in copies:
        copy.wait()
    put_tiles(index, count, tiles, panels, panels.shape[1] // panels.shape[2])


def direct_kernel(
    index_ref, count_ref, tiles_ref, panels, chip_q, rows_panels, direct, mirror,
    index, count, tiles, sems,
):
    copies = fetch(sems, (index_ref, index), (count_ref, count), (tiles_ref, tiles))
    rows_panels[...] = jnp.zeros_like(rows_panels)
    for copy in copies:
        copy.wait()
    tile = tiles.shape[1]
    rows = rows_panels.shape[1]
    chip_blocks = 2 * rows // tile
    chip, core = place()

    def put(s, carry):
        i, j = index[0, s], index[1, s]
        panel = (chip ^ (j // chip_blocks)) * chip_blocks + j % chip_blocks
        at = pl.multiple_of((i % (rows // tile)) * tile, tile)
        rows_panels[panel, pl.ds(at, tile), :] = tiles[s]
        return carry

    lax.fori_loop(0, live_tiles(count), put, 0)
    direct[...] = direct_sum(rows_panels, 0, split(chip_q[...], tile))
    q_t = chip_q[...].T
    local = panels.shape[0] - chip_blocks + core * (chip_blocks // 2)
    for b in range(rows // tile):
        mirror[b * tile:(b + 1) * tile, :] = jnp.dot(
            q_t, panels[local + b], preferred_element_type=jnp.float32
        )


def write_message(message, blocks):
    tile = message.shape[1]
    codes = []
    for b, x in enumerate(blocks):
        values, code = encode(x)
        message[b * tile:(b + 1) * tile, :] = values
        codes.append(code)
    which = lax.broadcasted_iota(jnp.int32, (16, tile), 0)
    tail = jnp.zeros((16, tile), jnp.float32)
    for b, code in enumerate(codes):
        tail = jnp.where(which == b, code, tail)
    message[len(blocks) * tile:, :] = tail.astype(jnp.int32).astype(jnp.int16)


def read_message(message):
    tile = message.shape[1]
    blocks = message.shape[0] // tile
    tail = message[blocks * tile:, :].astype(jnp.int32).astype(jnp.float32)
    scales = scale_of(tail) * (1.0 / TOP)
    return [
        message[b * tile:(b + 1) * tile, :].astype(jnp.int32).astype(jnp.float32)
        * scales[b:b + 1, :]
        for b in range(blocks)
    ]


def mirrored_blocks(q_t, panels, slot):
    tile = panels.shape[2]
    chip_blocks = panels.shape[1] // tile
    blocks = []
    for g in range(slot * chip_blocks, (slot + 1) * chip_blocks, 2):
        pair = jnp.concatenate([panels[g], panels[g + 1]], axis=1)
        sums = jnp.dot(q_t, pair, preferred_element_type=jnp.float32)
        blocks += [sums[:, :tile], sums[:, tile:]]
    return blocks


def direct_sum(panels, start, blocks):
    total = None
    for b in range(0, len(blocks), 2):
        pair = jnp.concatenate([panels[start + b], panels[start + b + 1]], axis=1)
        q = jnp.concatenate(blocks[b:b + 2], axis=0).astype(jnp.bfloat16)
        part = jnp.dot(pair, q, preferred_element_type=jnp.float32)
        total = part if total is None else total + part
    return total


def split(x, tile):
    return [x[at:at + tile, :] for at in range(0, x.shape[0], tile)]


def in_lower_half(chips):
    return place()[0] < chips // 2


def far_kernel(
    chips, slots, index_ref, count_ref, tiles, own_q, other_q, _, panels, chip_q, *refs
):
    *messages, index, count, sems = refs
    rows, tile = own_q.shape[0], panels.shape[2]
    _, core = place()
    chip_q[pl.ds(pl.multiple_of(core * rows, rows), rows), :] = own_q[...]
    chip_q[pl.ds(pl.multiple_of((1 - core) * rows, rows), rows), :] = other_q[...]

    @pl.when(in_lower_half(chips))
    def _():
        for copy in fetch(sems, (index_ref, index), (count_ref, count)):
            copy.wait()
        put_tiles(index, count, tiles, panels, panels.shape[1] // tile)
        q_t = chip_q[...].T
        for k, message in zip(slots, messages, strict=True):
            write_message(message, mirrored_blocks(q_t, panels, k))

    @pl.when(jnp.logical_not(in_lower_half(chips)))
    def _():
        write_message(messages[0], split(chip_q[...].astype(jnp.float32), tile))
        for message in messages[1:]:
            message[...] = messages[0][...]


def near_kernel(
    chips, slots, index, count, tiles, _, chip_q, panels, *messages
):
    tile = panels.shape[2]
    chip, core = place()

    @pl.when(jnp.logical_not(in_lower_half(chips)))
    def _():
        put_tiles(index, count, tiles, panels, panels.shape[1] // tile)

    q = chip_q[...]
    q_t = q.T
    q_wide = q.astype(jnp.float32)
    for k, message in zip(slots, messages, strict=True):
        up = chip < (chip ^ (2 * k + core))
        blocks = mirrored_blocks(q_t, panels, k)
        write_message(
            message,
            [
                jnp.where(up, m, own)
                for m, own in zip(blocks, split(q_wide, tile), strict=True)
            ],
        )


def gather_part(sources, rows_panels, direct, mirror, messages):
    tile = rows_panels.shape[2]
    chip, core = place()
    total = direct[...]
    mirrored = split(mirror[...], tile)
    half = len(mirrored)
    for (k, mine), message in zip(sources, messages, strict=True):
        cls = 2 * k + (core if mine else 1 - core)
        low = (chip ^ cls) < chip
        blocks = read_message(message)
        total = total + direct_sum(rows_panels, cls * 2 * half, blocks)
        mirrored = [
            m + jnp.where(low, jnp.where(core == 0, a, b), 0.0)
            for m, a, b in zip(mirrored, blocks[:half], blocks[half:], strict=True)
        ]
    return total, mirrored


def gather_kernel(sources, rows_panels, direct, mirror, *refs):
    *messages, direct_out, mirror_out = refs
    tile = rows_panels.shape[2]
    total, mirrored = gather_part(sources, rows_panels, direct, mirror, messages)
    direct_out[...] = total
    for b, m in enumerate(mirrored):
        mirror_out[b * tile:(b + 1) * tile, :] = m


def final_kernel(sources, factor, rows_panels, direct, mirror, *refs):
    *messages, out, result, sems = refs
    tile = rows_panels.shape[2]
    total, mirrored = gather_part(sources, rows_panels, direct, mirror, messages)
    copies = []
    for b, (block, m) in enumerate(zip(split(total, tile), mirrored, strict=True)):
        at = pl.ds(b * tile, tile)
        result[at, :] = (block + m.T) * factor
        copies.append(pltpu.make_async_copy(result.at[at], out.at[at], sems.at[b]))
        copies[-1].start()
    for copy in copies:
        copy.wait()


VMEM = functools.partial(pl.BlockSpec, memory_space=pltpu.VMEM)
SMEM = functools.partial(pl.BlockSpec, memory_space=pltpu.SMEM)


def on_device(devices, tile_blocks, q_block, tile_index, tile_count):
    tile = tile_blocks.shape[1]
    rows, columns = q_block.shape
    chips = devices // 2
    slots = chips // 2
    chip_rows = 2 * rows
    chip_blocks = chip_rows // tile
    wide = jnp.float32
    other_core = [(d, d ^ 1) for d in range(devices)]

    def swap(x):
        return lax.ppermute(x, "row", other_core)

    index = tile_index.T
    other_tiles = swap(tile_blocks)
    other_q = swap(q_block)
    other_index = swap(index)
    other_count = swap(tile_count)

    panels_shape = jax.ShapeDtypeStruct(
        ((slots + 1) * chip_blocks, chip_rows, tile), jnp.bfloat16
    )
    rows_panels_shape = jax.ShapeDtypeStruct(
        (chips * chip_blocks, rows, tile), jnp.bfloat16
    )
    q_shape = jax.ShapeDtypeStruct((chip_rows, columns), jnp.bfloat16)
    message = jax.ShapeDtypeStruct((chip_rows + 16, columns), jnp.int16)
    half_shape = jax.ShapeDtypeStruct((rows, columns), wide)
    params = pltpu.CompilerParams(vmem_limit_bytes=48 * 2**20)
    hbm = pl.BlockSpec(memory_space=pltpu.HBM)
    own = [
        pltpu.with_memory_space_constraint(a, pltpu.HBM)
        for a in (index, tile_count, tile_blocks)
    ]
    own_scratch = [
        pltpu.SMEM(index.shape, index.dtype),
        pltpu.SMEM(tile_count.shape, tile_count.dtype),
        pltpu.VMEM(tile_blocks.shape, tile_blocks.dtype),
        pltpu.SemaphoreType.DMA((3,)),
    ]
    own_panels = pl.pallas_call(
        own_kernel,
        out_shape=panels_shape,
        in_specs=[hbm] * 3,
        out_specs=VMEM(),
        scratch_shapes=own_scratch,
        compiler_params=params,
        name="own_tiles",
    )(*own)
    far = list(range(slots // 2, slots))
    near = list(reversed(range(slots // 2)))
    panels, chip_q, *far_messages = pl.pallas_call(
        functools.partial(far_kernel, chips, far),
        out_shape=[panels_shape, q_shape] + [message] * len(far),
        in_specs=[pl.BlockSpec(memory_space=pl.ANY)] * 2 + [VMEM()] * 4,
        out_specs=[VMEM()] * (2 + len(far)),
        scratch_shapes=own_scratch[:2] + [pltpu.SemaphoreType.DMA((2,))],
        input_output_aliases={5: 0},
        compiler_params=params,
        name="pack_far",
    )(other_index, other_count, other_tiles, q_block, other_q, own_panels)
    panels, *near_messages = pl.pallas_call(
        functools.partial(near_kernel, chips, near),
        out_shape=[panels_shape] + [message] * len(near),
        in_specs=[SMEM(), SMEM()] + [VMEM()] * 3,
        out_specs=[VMEM()] * (1 + len(near)),
        input_output_aliases={3: 0},
        compiler_params=params,
        name="pack_near",
    )(other_index, other_count, other_tiles, panels, chip_q)
    messages = dict(zip(far + near, far_messages + near_messages, strict=True))
    received = {
        k: lax.ppermute(messages[k], "row", [
            (d, d ^ (2 * (2 * k + d % 2))) for d in range(devices) if 2 * k + d % 2
        ])
        for k in far + near
    }

    rows_panels, direct, mirror = pl.pallas_call(
        direct_kernel,
        out_shape=[rows_panels_shape, half_shape, half_shape],
        in_specs=[hbm] * 3 + [VMEM()] * 2,
        out_specs=[VMEM()] * 3,
        scratch_shapes=own_scratch,
        compiler_params=params,
        cost_estimate=pl.CostEstimate(flops=10000000000, bytes_accessed=0, transcendentals=0),
            name="direct_local",
    )(*own, panels, chip_q)

    other = {k: swap(received[k]) for k in received}

    def gather(sources, direct, mirror, name):
        return pl.pallas_call(
            functools.partial(gather_kernel, sources),
            out_shape=[half_shape] * 2,
            in_specs=[VMEM()] * (3 + len(sources)),
            out_specs=[VMEM()] * 2,
            compiler_params=params,
            cost_estimate=pl.CostEstimate(
                flops=10**10, bytes_accessed=0, transcendentals=0
            ),
            name=name,
        )(rows_panels, direct, mirror,
          *((received if mine else other)[k] for k, mine in sources))

    *late, last = near + far[1:]
    sums = gather([(far[0], True), (far[0], False)], direct, mirror, "gather_first")
    sums = gather([(k, mine) for k in late for mine in (True, False)], *sums, "gather_near")
    sums = gather([(last, True)], *sums, "gather_own")
    return pl.pallas_call(
        functools.partial(
            final_kernel, [(last, False)], 1.0 / math.sqrt(rows * devices)
        ),
        out_shape=half_shape,
        in_specs=[VMEM()] * 4,
        out_specs=hbm,
        scratch_shapes=[
            pltpu.VMEM((rows, columns), wide),
            pltpu.SemaphoreType.DMA((rows // tile,)),
        ],
        compiler_params=params,
        name="gather_last",
    )(rows_panels, *sums, other[last])


def solution(mesh):
    return jax.shard_map(
        functools.partial(on_device, mesh.shape["row"]),
        mesh=mesh,
        in_specs=(
            P(("grp", "row"), None, None),
            P(("grp", "row"), None),
            P(("grp", "row"), None),
            P(("grp", "row")),
        ),
        out_specs=P(("grp", "row"), None),
        check_vma=False,
    )
```

time: 22.5 us -> 21.7 us (0.964)
  waiting for transfers between devices: 7.6 us -> 2.32 us
  Pallas kernels: 4.75 us -> 7.28 us
  starting transfers between devices: 9.26 us -> 11.7 us
  other arithmetic: 0.67 us -> 0 us
    ppermute x4, waiting for transfers between devices: 6.6 us -> 2.3 us  [on_device(): lax.ppermute(messages[k], 'row', [(d, d ^ 2 * (2 * k + d % 2)) for d in r...]
    pallas_call x3 -> x6, Pallas kernels: 2.64 us -> 5.07 us  [the longest x1 1.65 us: on_device(): pl.pallas_call(direct_kernel, out_shape=[rows_panels_shape, half_shape, h...]
    ppermute x5 -> x8, starting transfers between devices: 3.27 us -> 5.67 us  [swap(): return lax.ppermute(x, 'row', other_core)]
    ppermute x5 -> x8, waiting for transfers between devices: 1 us -> 0.02 us  [swap(): return lax.ppermute(x, 'row', other_core)]
    mul x1 -> x0, other arithmetic: 0.67 us -> none  [on_device(): return (keep + swap(send)) * (1.0 / math.sqrt(rows * devices))]
  transfers between devices with their start and end apart: 9 -> 12, of which waited for: 4 -> 1; matrix products, arithmetic and copies ran while one was open for 0% -> 0% of each run, Pallas kernels for 13% -> 24%
where the time goes in v5:
time: 21.7 us; the launch traced here: 21.4 us
  starting transfers between devices  11.7 us (54%)
  Pallas kernels  7.28 us (34%)
  waiting for transfers between devices  2.32 us (11%)
    ppermute x4, starting transfers between devices, on_device(): lax.ppermute(messages[k], 'row', [(d, d ^ 2 * (2 * k + d % 2)) for d in r...  6.02 us
    ppermute x8, starting transfers between devices, swap(): return lax.ppermute(x, 'row', other_core)  5.67 us
    ppermute x4, waiting for transfers between devices, on_device(): lax.ppermute(messages[k], 'row', [(d, d ^ 2 * (2 * k + d % 2)) for d in r...  2.3 us
    pallas_call x1, Pallas kernels, on_device(): pl.pallas_call(direct_kernel, out_shape=[rows_panels_shape, half_shape, h...  1.65 us
    pallas_call x1, Pallas kernels, on_device(): pl.pallas_call(own_kernel, out_shape=panels_shape, in_specs=[hbm] * 3, ou...  1.51 us
    pallas_call x1, Pallas kernels, on_device(): pl.pallas_call(functools.partial(far_kernel, chips, far), out_shape=[pane...  1.23 us
    pallas_call x3, Pallas kernels, gather(): pl.pallas_call(functools.partial(gather_kernel, sources), out_shape=[half...  1.03 us
    pallas_call x1, Pallas kernels, on_device(): pl.pallas_call(functools.partial(near_kernel, chips, near), out_shape=[pa...  0.97 us
  transfers between devices with their start and end apart: 12, of which 1 were waited for; matrix products, arithmetic and copies ran while one was open for 0% of the time, Pallas kernels for 24%

profile of v5, /device:TPU:0, one launch (start us, length us, event | category | flops | bytes accessed | tf_op | source)
XLA Modules:
  0.0 21.4 jit_solution(806753049399612951)
XLA Ops:
  0.0 0.5 %collective-permute-start.2 = (bf16[18,128,128]{2,1,0:T(8,128)(2,1)}, bf16[18,128,128]{2,1,0:T(8,128)(2,1)S(1)}, u32[]{:S(2)}, u32[]{:S(2)}) collective-permute-start(bf16[18,128,128]{2,1,0:T(8,128)(2,1)} %tiles_ref.3), channel_id=1, source_target_pairs={{0,1},{1,0},{2,3},{3,2},{4,5},{5,4},{6,7},{7,6},{8,9},{9,8},{10,11... | collective-permute-start | bytes 1769480 | tf_op jit(solution)/shard_map/ppermute | solution.py:269
  0.5 0.1 collective-permute-start.3
  0.5 0.4 %collective-permute-start.1 = (s32[2]{0:T(128)}, s32[2]{0:T(128)S(1)}, u32[]{:S(2)}, u32[]{:S(2)}) collective-permute-start(s32[2]{0:T(128)} %count_ref.3), channel_id=1, source_target_pairs={{0,1},{1,0},{2,3},{3,2},{4,5},{5,4},{6,7},{7,6},{8,9},{9,8},{10,11... | collective-permute-start | bytes 32 | tf_op jit(solution)/shard_map/ppermute | solution.py:269
  1.0 0.1 collective-permute-start
  1.0 1.5 %own_tiles.1._ = bf16[20,512,128]{2,1,0:T(8,128)(2,1)S(1)} custom-call(s32[2,18]{1,0:T(2,128)} %bitcast.2, s32[2]{0:T(128)} %count_ref.3, bf16[18,128,128]{2,1,0:T(8,128)(2,1)} %tiles_ref.3), custom_call_target="tpu_custom_call" | custom-call | tf_op jit(solution)/shard_map/own_tiles/pallas_call | solution.py:298
  2.5 0.0 collective-permute-done.1.count_ref.count
  2.6 0.0 collective-permute-done.index_ref.index
  2.6 0.0 collective-permute-done.3.other_q
  2.6 0.0 collective-permute-done.2.tiles
  2.6 1.2 %pack_far.1 = (bf16[20,512,128]{2,1,0:T(8,128)(2,1)S(1)}, bf16[512,128]{1,0:T(8,128)(2,1)S(1)}, s16[528,128]{1,0:T(8,128)(2,1)S(1)}, s16[528,128]{1,0:T(8,128)(2,1)S(1)}) custom-call(s32[2,18]{1,0:T(2,128)S(1)} %collective-permute-done.index_ref.index, s32[2]{0:T(128)S(1)} %collective-permute-done.1.count_ref.count, ...), custom_call_target="tpu_custom_call", output_to_operand_aliasing={{0}: (5, {})} | custom-call | tf_op jit(solution)/shard_map/pack_far/pallas_call | solution.py:309
  3.8 2.7 %collective-permute-start.4 = (s16[528,128]{1,0:T(8,128)(2,1)S(1)}, s16[528,128]{1,0:T(8,128)(2,1)S(1)}, u32[]{:S(2)}, u32[]{:S(2)}) collective-permute-start(s16[528,128]{1,0:T(8,128)(2,1)S(1)} %get-tuple-element.27), channel_id=1, source_target_pairs={{0,8},{1,11},{2,10},{3,9},{4,12},{5,15},{6,14},{7,13},{8,0},{9,3},... | collective-permute-start | bytes 405512 | tf_op jit(solution)/shard_map/ppermute | solution.py:330
  6.6 1.0 %pack_near.1 = (bf16[20,512,128]{2,1,0:T(8,128)(2,1)S(1)}, s16[528,128]{1,0:T(8,128)(2,1)S(1)}, s16[528,128]{1,0:T(8,128)(2,1)S(1)}) custom-call(s32[2,18]{1,0:T(2,128)S(1)} %collective-permute-done.index_ref.index, s32[2]{0:T(128)S(1)} %collective-permute-done.1.count_ref.count, ...), custom_call_target="tpu_custom_call", output_to_operand_aliasing={{0}: (3, {})} | custom-call | tf_op jit(solution)/shard_map/pack_near/pallas_call | solution.py:319
  7.6 1.6 %collective-permute-start.6 = (s16[528,128]{1,0:T(8,128)(2,1)S(1)}, s16[528,128]{1,0:T(8,128)(2,1)S(1)}, u32[]{:S(2)}, u32[]{:S(2)}) collective-permute-start(s16[528,128]{1,0:T(8,128)(2,1)S(1)} %get-tuple-element.30), channel_id=1, source_target_pairs={{0,4},{1,7},{2,6},{3,5},{4,0},{5,3},{6,2},{7,1},{8,12},{9,15},{10,... | collective-permute-start | bytes 405512 | tf_op jit(solution)/shard_map/ppermute | solution.py:330
  9.2 0.7 %collective-permute-start.8 = (s16[528,128]{1,0:T(8,128)(2,1)S(1)}, s16[528,128]{1,0:T(8,128)(2,1)S(1)}, u32[]{:S(2)}, u32[]{:S(2)}) collective-permute-start(s16[528,128]{1,0:T(8,128)(2,1)S(1)} %get-tuple-element.31), channel_id=1, source_target_pairs={{1,3},{3,1},{5,7},{7,5},{9,11},{11,9},{13,15},{15,13},{17,19},{19,... | collective-permute-start | bytes 405512 | tf_op jit(solution)/shard_map/ppermute | solution.py:330
  9.9 1.0 %collective-permute-start.10 = (s16[528,128]{1,0:T(8,128)(2,1)S(1)}, s16[528,128]{1,0:T(8,128)(2,1)S(1)}, u32[]{:S(2)}, u32[]{:S(2)}) collective-permute-start(s16[528,128]{1,0:T(8,128)(2,1)S(1)} %get-tuple-element.34), channel_id=1, source_target_pairs={{0,12},{1,15},{2,14},{3,13},{4,8},{5,11},{6,10},{7,9},{8,4},{9,7},... | collective-permute-start | bytes 405512 | tf_op jit(solution)/shard_map/ppermute | solution.py:330
  10.8 0.0 collective-permute-done.4.refs_0_
  10.8 3.0 %collective-permute-start.5 = (s16[528,128]{1,0:T(8,128)(2,1)S(1)}, s16[528,128]{1,0:T(8,128)(2,1)S(1)}, u32[]{:S(2)}, u32[]{:S(2)}) collective-permute-start(s16[528,128]{1,0:T(8,128)(2,1)S(1)} %collective-permute-done.4.refs_0_), channel_id=1, source_target_pairs={{0,1},{1,0},{2,3},{3,2},{4,5},{5,4},{6,7},{7,6},{8,9},{9,8},{10,11... | collective-permute-start | bytes 405512 | tf_op jit(solution)/shard_map/ppermute | solution.py:269
  13.9 1.6 %direct_local.1 = (bf16[32,256,128]{2,1,0:T(8,128)(2,1)S(1)}, f32[256,128]{1,0:T(8,128)S(1)}, f32[256,128]{1,0:T(8,128)S(1)}) custom-call(s32[2,18]{1,0:T(2,128)} %bitcast.3, s32[2]{0:T(128)} %count_ref.3, bf16[18,128,128]{2,1,0:T(8,128)(2,1)} %tiles_ref.3, bf16[20,512,128]{2,1,0:T(8,128)(2,1)S(1)} %get-tuple-element.23.panels, ...), custom_call_target="tpu_custom_call" | custom-call | flops 10000000000 | tf_op jit(solution)/shard_map/direct_local/pallas_call | solution.py:336
  15.5 0.0 collective-permute-done.6.refs_0_
  15.5 0.3 %collective-permute-start.7 = (s16[528,128]{1,0:T(8,128)(2,1)S(1)}, s16[528,128]{1,0:T(8,128)(2,1)S(1)}, u32[]{:S(2)}, u32[]{:S(2)}) collective-permute-start(s16[528,128]{1,0:T(8,128)(2,1)S(1)} %collective-permute-done.6.refs_0_), channel_id=1, source_target_pairs={{0,1},{1,0},{2,3},{3,2},{4,5},{5,4},{6,7},{7,6},{8,9},{9,8},{10,11... | collective-permute-start | bytes 405512 | tf_op jit(solution)/shard_map/ppermute | solution.py:269
  15.8 0.0 collective-permute-done.8.refs_2_
  15.8 0.3 %collective-permute-start.9 = (s16[528,128]{1,0:T(8,128)(2,1)S(1)}, s16[528,128]{1,0:T(8,128)(2,1)S(1)}, u32[]{:S(2)}, u32[]{:S(2)}) collective-permute-start(s16[528,128]{1,0:T(8,128)(2,1)S(1)} %collective-permute-done.8.refs_2_), channel_id=1, source_target_pairs={{0,1},{1,0},{2,3},{3,2},{4,5},{5,4},{6,7},{7,6},{8,9},{9,8},{10,11... | collective-permute-start | bytes 405512 | tf_op jit(solution)/shard_map/ppermute | solution.py:269
  16.1 2.3 %collective-permute-done.10.refs_0_ = s16[528,128]{1,0:T(8,128)(2,1)S(1)} collective-permute-done((s16[528,128]{1,0:T(8,128)(2,1)S(1)}, s16[528,128]{1,0:T(8,128)(2,1)S(1)}, u32[]{:S(2)}, u32[]{:S(2)}) %collective-permute-start.10) | collective-permute-done | bytes 135200 | tf_op jit(solution)/shard_map/ppermute | solution.py:330
  18.4 1.1 %collective-permute-start.11 = (s16[528,128]{1,0:T(8,128)(2,1)S(1)}, s16[528,128]{1,0:T(8,128)(2,1)S(1)}, u32[]{:S(2)}, u32[]{:S(2)}) collective-permute-start(s16[528,128]{1,0:T(8,128)(2,1)S(1)} %collective-permute-done.10.refs_0_), channel_id=1, source_target_pairs={{0,1},{1,0},{2,3},{3,2},{4,5},{5,4},{6,7},{7,6},{8,9},{9,8},{10,11... | collective-permute-start | bytes 405512 | tf_op jit(solution)/shard_map/ppermute | solution.py:269
  19.5 0.0 collective-permute-done.5.refs_1_
  19.5 0.3 %gather_first.1 = (f32[256,128]{1,0:T(8,128)S(1)}, f32[256,128]{1,0:T(8,128)S(1)}) custom-call(bf16[32,256,128]{2,1,0:T(8,128)(2,1)S(1)} %get-tuple-element.24.rows_panels, f32[256,128]{1,0:T(8,128)S(1)} %get-tuple-element.25.direct, f32[256,128]{1,0:T(8,128)S(1)} %get-tuple-element.26.mirror, s16[528,128]{1,0:T(8,128)(2,1)S(1)} %collective-permute-done.4.refs_0_, ...), custom_call_target="tpu_custom_call" | custom-call | flops 10000000000 | tf_op jit(solution)/shard_map/gather_first/pallas_call | solution.py:350
  19.8 0.0 collective-permute-done.7.refs_1_
  19.8 0.0 collective-permute-done.9.refs_3_
  19.8 0.5 %gather_near.1 = (f32[256,128]{1,0:T(8,128)S(1)}, f32[256,128]{1,0:T(8,128)S(1)}) custom-call(bf16[32,256,128]{2,1,0:T(8,128)(2,1)S(1)} %get-tuple-element.24.rows_panels, f32[256,128]{1,0:T(8,128)S(1)} %get-tuple-element.28.direct, f32[256,128]{1,0:T(8,128)S(1)} %get-tuple-element.29.mirror, s16[528,128]{1,0:T(8,128)(2,1)S(1)} %collective-permute-done.6.refs_0_, ...), custom_call_target="tpu_custom_call" | custom-call | flops 10000000000 | tf_op jit(solution)/shard_map/gather_near/pallas_call | solution.py:350
  20.3 0.2 %gather_own.1 = (f32[256,128]{1,0:T(8,128)S(1)}, f32[256,128]{1,0:T(8,128)S(1)}) custom-call(bf16[32,256,128]{2,1,0:T(8,128)(2,1)S(1)} %get-tuple-element.24.rows_panels, f32[256,128]{1,0:T(8,128)S(1)} %get-tuple-element.32.direct, f32[256,128]{1,0:T(8,128)S(1)} %get-tuple-element.33.mirror, s16[528,128]{1,0:T(8,128)(2,1)S(1)} %collective-permute-done.10.refs_0_), custom_call_target="tpu_custom_call" | custom-call | flops 10000000000 | tf_op jit(solution)/shard_map/gather_own/pallas_call | solution.py:350
  20.5 0.0 collective-permute-done.11.refs_0_
  20.5 0.9 %gather_last.1 = f32[256,128]{1,0:T(8,128)} custom-call(bf16[32,256,128]{2,1,0:T(8,128)(2,1)S(1)} %get-tuple-element.24.rows_panels, f32[256,128]{1,0:T(8,128)S(1)} %get-tuple-element.35.direct, f32[256,128]{1,0:T(8,128)S(1)} %get-tuple-element.36.mirror, s16[528,128]{1,0:T(8,128)(2,1)S(1)} %collective-permute-done.11.refs_0_), custom_call_target="tpu_custom_call" | custom-call | tf_op jit(solution)/shard_map/gather_last/pallas_call | solution.py:367
  (2 shorter events, 0.0 us)
Async XLA Ops:
  0.0 2.6 %copy-start = (bf16[256,128]{1,0:T(8,128)(2,1)S(1)}, bf16[256,128]{1,0:T(8,128)(2,1)}, u32[]{:S(2)}) copy-start(bf16[256,128]{1,0:T(8,128)(2,1)} %own_q.1) | copy-start | bytes 196612
  0.0 2.6 %collective-permute-start.2 = (bf16[18,128,128]{2,1,0:T(8,128)(2,1)}, bf16[18,128,128]{2,1,0:T(8,128)(2,1)S(1)}, u32[]{:S(2)}, u32[]{:S(2)}) collective-permute-start(bf16[18,128,128]{2,1,0:T(8,128)(2,1)} %tiles_ref.3), channel_id=1, source_target_pairs={{0,1},{1,0},{2,3},{3,2},{4,5},{5,4},{6,7},{7,6},{8,9},{9,8},{10,11... | collective-permute-start | bytes 1769480 | tf_op jit(solution)/shard_map/ppermute | solution.py:269
  0.5 2.1 %collective-permute-start.3 = (bf16[256,128]{1,0:T(8,128)(2,1)}, bf16[256,128]{1,0:T(8,128)(2,1)S(1)}, u32[]{:S(2)}, u32[]{:S(2)}) collective-permute-start(bf16[256,128]{1,0:T(8,128)(2,1)} %own_q.1), channel_id=1, source_target_pairs={{0,1},{1,0},{2,3},{3,2},{4,5},{5,4},{6,7},{7,6},{8,9},{9,8},{10,11... | collective-permute-start | bytes 196616 | tf_op jit(solution)/shard_map/ppermute | solution.py:269
  0.5 2.0 %collective-permute-start.1 = (s32[2]{0:T(128)}, s32[2]{0:T(128)S(1)}, u32[]{:S(2)}, u32[]{:S(2)}) collective-permute-start(s32[2]{0:T(128)} %count_ref.3), channel_id=1, source_target_pairs={{0,1},{1,0},{2,3},{3,2},{4,5},{5,4},{6,7},{7,6},{8,9},{9,8},{10,11... | collective-permute-start | bytes 32 | tf_op jit(solution)/shard_map/ppermute | solution.py:269
  1.0 1.6 %collective-permute-start = (s32[2,18]{1,0:T(2,128)}, s32[2,18]{1,0:T(2,128)S(1)}, u32[]{:S(2)}, u32[]{:S(2)}) collective-permute-start(s32[2,18]{1,0:T(2,128)} %bitcast.1), channel_id=1, source_target_pairs={{0,1},{1,0},{2,3},{3,2},{4,5},{5,4},{6,7},{7,6},{8,9},{9,8},{10,11... | collective-permute-start | bytes 440 | tf_op jit(solution)/shard_map/ppermute | solution.py:269
  3.8 7.0 %collective-permute-start.4 = (s16[528,128]{1,0:T(8,128)(2,1)S(1)}, s16[528,128]{1,0:T(8,128)(2,1)S(1)}, u32[]{:S(2)}, u32[]{:S(2)}) collective-permute-start(s16[528,128]{1,0:T(8,128)(2,1)S(1)} %get-tuple-element.27), channel_id=1, source_target_pairs={{0,8},{1,11},{2,10},{3,9},{4,12},{5,15},{6,14},{7,13},{8,0},{9,3},... | collective-permute-start | bytes 405512 | tf_op jit(solution)/shard_map/ppermute | solution.py:330
  7.6 8.0 %collective-permute-start.6 = (s16[528,128]{1,0:T(8,128)(2,1)S(1)}, s16[528,128]{1,0:T(8,128)(2,1)S(1)}, u32[]{:S(2)}, u32[]{:S(2)}) collective-permute-start(s16[528,128]{1,0:T(8,128)(2,1)S(1)} %get-tuple-element.30), channel_id=1, source_target_pairs={{0,4},{1,7},{2,6},{3,5},{4,0},{5,3},{6,2},{7,1},{8,12},{9,15},{10,... | collective-permute-start | bytes 405512 | tf_op jit(solution)/shard_map/ppermute | solution.py:330
  9.2 6.6 %collective-permute-start.8 = (s16[528,128]{1,0:T(8,128)(2,1)S(1)}, s16[528,128]{1,0:T(8,128)(2,1)S(1)}, u32[]{:S(2)}, u32[]{:S(2)}) collective-permute-start(s16[528,128]{1,0:T(8,128)(2,1)S(1)} %get-tuple-element.31), channel_id=1, source_target_pairs={{1,3},{3,1},{5,7},{7,5},{9,11},{11,9},{13,15},{15,13},{17,19},{19,... | collective-permute-start | bytes 405512 | tf_op jit(solution)/shard_map/ppermute | solution.py:330
  9.9 8.5 %collective-permute-start.10 = (s16[528,128]{1,0:T(8,128)(2,1)S(1)}, s16[528,128]{1,0:T(8,128)(2,1)S(1)}, u32[]{:S(2)}, u32[]{:S(2)}) collective-permute-start(s16[528,128]{1,0:T(8,128)(2,1)S(1)} %get-tuple-element.34), channel_id=1, source_target_pairs={{0,12},{1,15},{2,14},{3,13},{4,8},{5,11},{6,10},{7,9},{8,4},{9,7},... | collective-permute-start | bytes 405512 | tf_op jit(solution)/shard_map/ppermute | solution.py:330
  10.8 8.6 %collective-permute-start.5 = (s16[528,128]{1,0:T(8,128)(2,1)S(1)}, s16[528,128]{1,0:T(8,128)(2,1)S(1)}, u32[]{:S(2)}, u32[]{:S(2)}) collective-permute-start(s16[528,128]{1,0:T(8,128)(2,1)S(1)} %collective-permute-done.4.refs_0_), channel_id=1, source_target_pairs={{0,1},{1,0},{2,3},{3,2},{4,5},{5,4},{6,7},{7,6},{8,9},{9,8},{10,11... | collective-permute-start | bytes 405512 | tf_op jit(solution)/shard_map/ppermute | solution.py:269
  15.5 4.2 %collective-permute-start.7 = (s16[528,128]{1,0:T(8,128)(2,1)S(1)}, s16[528,128]{1,0:T(8,128)(2,1)S(1)}, u32[]{:S(2)}, u32[]{:S(2)}) collective-permute-start(s16[528,128]{1,0:T(8,128)(2,1)S(1)} %collective-permute-done.6.refs_0_), channel_id=1, source_target_pairs={{0,1},{1,0},{2,3},{3,2},{4,5},{5,4},{6,7},{7,6},{8,9},{9,8},{10,11... | collective-permute-start | bytes 405512 | tf_op jit(solution)/shard_map/ppermute | solution.py:269
  15.8 4.0 %collective-permute-start.9 = (s16[528,128]{1,0:T(8,128)(2,1)S(1)}, s16[528,128]{1,0:T(8,128)(2,1)S(1)}, u32[]{:S(2)}, u32[]{:S(2)}) collective-permute-start(s16[528,128]{1,0:T(8,128)(2,1)S(1)} %collective-permute-done.8.refs_2_), channel_id=1, source_target_pairs={{0,1},{1,0},{2,3},{3,2},{4,5},{5,4},{6,7},{7,6},{8,9},{9,8},{10,11... | collective-permute-start | bytes 405512 | tf_op jit(solution)/shard_map/ppermute | solution.py:269
  18.4 2.1 %collective-permute-start.11 = (s16[528,128]{1,0:T(8,128)(2,1)S(1)}, s16[528,128]{1,0:T(8,128)(2,1)S(1)}, u32[]{:S(2)}, u32[]{:S(2)}) collective-permute-start(s16[528,128]{1,0:T(8,128)(2,1)S(1)} %collective-permute-done.10.refs_0_), channel_id=1, source_target_pairs={{0,1},{1,0},{2,3},{3,2},{4,5},{5,4},{6,7},{7,6},{8,9},{9,8},{10,11... | collective-permute-start | bytes 405512 | tf_op jit(solution)/shard_map/ppermute | solution.py:269

commit v6 on v5

--- a/solution.py
+++ b/solution.py
@@ -171,10 +171,11 @@
 
     @pl.when(in_lower_half(chips))
     def _():
-        for copy in fetch(sems, (index_ref, index), (count_ref, count)):
+        copies = fetch(sems, (index_ref, index), (count_ref, count))
+        q_t = chip_q[...].T
+        for copy in copies:
             copy.wait()
         put_tiles(index, count, tiles, panels, panels.shape[1] // tile)
-        q_t = chip_q[...].T
         for k, message in zip(slots, messages, strict=True):
             write_message(message, mirrored_blocks(q_t, panels, k))
 
@@ -186,26 +187,30 @@
 
 
 def near_kernel(
-    chips, slots, index, count, tiles, _, chip_q, panels, *messages
+    chips, slots, index_ref, count_ref, tiles, _, chip_q, panels, *refs
 ):
+    *messages, index, count, sems = refs
     tile = panels.shape[2]
     chip, core = place()
+    q = chip_q[...]
 
     @pl.when(jnp.logical_not(in_lower_half(chips)))
     def _():
+        for copy in fetch(sems, (index_ref, index), (count_ref, count)):
+            copy.wait()
         put_tiles(index, count, tiles, panels, panels.shape[1] // tile)
 
-    q = chip_q[...]
     q_t = q.T
     q_wide = q.astype(jnp.float32)
     for k, message in zip(slots, messages, strict=True):
         up = chip < (chip ^ (2 * k + core))
-        blocks = mirrored_blocks(q_t, panels, k)
         write_message(
             message,
             [
                 jnp.where(up, m, own)
-                for m, own in zip(blocks, split(q_wide, tile), strict=True)
+                for m, own in zip(
+                    mirrored_blocks(q_t, panels, k), split(q_wide, tile), strict=True
+                )
             ],
         )
 
@@ -306,31 +311,34 @@
     )(*own)
     far = list(range(slots // 2, slots))
     near = list(reversed(range(slots // 2)))
+    rest = near + far[1:]
+    first = far[:1]
     panels, chip_q, *far_messages = pl.pallas_call(
-        functools.partial(far_kernel, chips, far),
-        out_shape=[panels_shape, q_shape] + [message] * len(far),
+        functools.partial(far_kernel, chips, first),
+        out_shape=[panels_shape, q_shape] + [message] * len(first),
         in_specs=[pl.BlockSpec(memory_space=pl.ANY)] * 2 + [VMEM()] * 4,
-        out_specs=[VMEM()] * (2 + len(far)),
+        out_specs=[VMEM()] * (2 + len(first)),
         scratch_shapes=own_scratch[:2] + [pltpu.SemaphoreType.DMA((2,))],
         input_output_aliases={5: 0},
         compiler_params=params,
         name="pack_far",
     )(other_index, other_count, other_tiles, q_block, other_q, own_panels)
-    panels, *near_messages = pl.pallas_call(
-        functools.partial(near_kernel, chips, near),
-        out_shape=[panels_shape] + [message] * len(near),
-        in_specs=[SMEM(), SMEM()] + [VMEM()] * 3,
-        out_specs=[VMEM()] * (1 + len(near)),
+    panels, *rest_messages = pl.pallas_call(
+        functools.partial(near_kernel, chips, rest),
+        out_shape=[panels_shape] + [message] * len(rest),
+        in_specs=[pl.BlockSpec(memory_space=pl.ANY)] * 2 + [VMEM()] * 3,
+        out_specs=[VMEM()] * (1 + len(rest)),
+        scratch_shapes=own_scratch[:2] + [pltpu.SemaphoreType.DMA((2,))],
         input_output_aliases={3: 0},
         compiler_params=params,
         name="pack_near",
     )(other_index, other_count, other_tiles, panels, chip_q)
-    messages = dict(zip(far + near, far_messages + near_messages, strict=True))
+    messages = dict(zip(first + rest, far_messages + rest_messages, strict=True))
     received = {
         k: lax.ppermute(messages[k], "row", [
             (d, d ^ (2 * (2 * k + d % 2))) for d in range(devices) if 2 * k + d % 2
         ])
-        for k in far + near
+        for k in first + rest
     }
 
     rows_panels, direct, mirror = pl.pallas_call(

time: 21.7 us -> 21.5 us (level)
  the two profiles are of different devices: /device:TPU:0 before, /device:TPU:11 now
where the time goes in v6:
time: 21.5 us; the launch traced here: 21.4 us
  starting transfers between devices  10.2 us (47%)
  Pallas kernels  6.1 us (28%)
  waiting for transfers between devices  5.01 us (23%)
    ppermute x4, starting transfers between devices, on_device(): lax.ppermute(messages[k], 'row', [(d, d ^ 2 * (2 * k + d % 2)) for d in r...  7.45 us
    ppermute x4, waiting for transfers between devices, on_device(): lax.ppermute(messages[k], 'row', [(d, d ^ 2 * (2 * k + d % 2)) for d in r...  4.84 us
    ppermute x8, starting transfers between devices, swap(): return lax.ppermute(x, 'row', other_core)  2.73 us
    pallas_call x1, Pallas kernels, on_device(): pl.pallas_call(direct_kernel, out_shape=[rows_panels_shape, half_shape, h...  1.44 us
    pallas_call x1, Pallas kernels, on_device(): pl.pallas_call(own_kernel, out_shape=panels_shape, in_specs=[hbm] * 3, ou...  1.2 us
    pallas_call x1, Pallas kernels, on_device(): pl.pallas_call(functools.partial(far_kernel, chips, first), out_shape=[pa...  1.03 us
    pallas_call x3, Pallas kernels, gather(): pl.pallas_call(functools.partial(gather_kernel, sources), out_shape=[half...  1.03 us
    pallas_call x1, Pallas kernels, on_device(): pl.pallas_call(functools.partial(final_kernel, [(last, False)], 1.0 / mat...  0.89 us
  transfers between devices with their start and end apart: 12, of which 3 were waited for; matrix products, arithmetic and copies ran while one was open for 0% of the time, Pallas kernels for 20%

profile of v6, /device:TPU:11, one launch (start us, length us, event | category | flops | bytes accessed | tf_op | source)
XLA Modules:
  0.0 21.4 jit_solution(18432888553561071281)
XLA Ops:
  0.0 0.7 %collective-permute-start.2 = (bf16[18,128,128]{2,1,0:T(8,128)(2,1)}, bf16[18,128,128]{2,1,0:T(8,128)(2,1)S(1)}, u32[]{:S(2)}, u32[]{:S(2)}) collective-permute-start(bf16[18,128,128]{2,1,0:T(8,128)(2,1)} %tiles_ref.3), channel_id=1, source_target_pairs={{0,1},{1,0},{2,3},{3,2},{4,5},{5,4},{6,7},{7,6},{8,9},{9,8},{10,11... | collective-permute-start | bytes 1769480 | tf_op jit(solution)/shard_map/ppermute | solution.py:274
  0.7 0.1 collective-permute-start.3
  0.7 0.4 %collective-permute-start.1 = (s32[2]{0:T(128)}, s32[2]{0:T(128)S(1)}, u32[]{:S(2)}, u32[]{:S(2)}) collective-permute-start(s32[2]{0:T(128)} %count_ref.3), channel_id=1, source_target_pairs={{0,1},{1,0},{2,3},{3,2},{4,5},{5,4},{6,7},{7,6},{8,9},{9,8},{10,11... | collective-permute-start | bytes 32 | tf_op jit(solution)/shard_map/ppermute | solution.py:274
  1.2 0.1 collective-permute-start
  1.3 1.2 %own_tiles.1._ = bf16[20,512,128]{2,1,0:T(8,128)(2,1)S(1)} custom-call(s32[2,18]{1,0:T(2,128)} %bitcast.2, s32[2]{0:T(128)} %count_ref.3, bf16[18,128,128]{2,1,0:T(8,128)(2,1)} %tiles_ref.3), custom_call_target="tpu_custom_call" | custom-call | tf_op jit(solution)/shard_map/own_tiles/pallas_call | solution.py:303
  2.5 0.1 collective-permute-done.1.count_ref
  2.6 0.0 collective-permute-done.index_ref
  2.6 0.0 collective-permute-done.3.other_q
  2.6 0.0 collective-permute-done.2.tiles
  2.6 1.0 %pack_far.1 = (bf16[20,512,128]{2,1,0:T(8,128)(2,1)S(1)}, bf16[512,128]{1,0:T(8,128)(2,1)S(1)}, s16[528,128]{1,0:T(8,128)(2,1)S(1)}) custom-call(s32[2,18]{1,0:T(2,128)S(1)} %collective-permute-done.index_ref, s32[2]{0:T(128)S(1)} %collective-permute-done.1.count_ref, ...), custom_call_target="tpu_custom_call", output_to_operand_aliasing={{0}: (5, {})} | custom-call | tf_op jit(solution)/shard_map/pack_far/pallas_call | solution.py:316
  3.7 2.4 %collective-permute-start.4 = (s16[528,128]{1,0:T(8,128)(2,1)S(1)}, s16[528,128]{1,0:T(8,128)(2,1)S(1)}, u32[]{:S(2)}, u32[]{:S(2)}) collective-permute-start(s16[528,128]{1,0:T(8,128)(2,1)S(1)} %get-tuple-element.27), channel_id=1, source_target_pairs={{0,8},{1,11},{2,10},{3,9},{4,12},{5,15},{6,14},{7,13},{8,0},{9,3},... | collective-permute-start | bytes 405512 | tf_op jit(solution)/shard_map/ppermute | solution.py:338
  6.1 0.5 %pack_near.1 = (bf16[20,512,128]{2,1,0:T(8,128)(2,1)S(1)}, s16[528,128]{1,0:T(8,128)(2,1)S(1)}, s16[528,128]{1,0:T(8,128)(2,1)S(1)}, s16[528,128]{1,0:T(8,128)(2,1)S(1)}) custom-call(s32[2,18]{1,0:T(2,128)S(1)} %collective-permute-done.index_ref, s32[2]{0:T(128)S(1)} %collective-permute-done.1.count_ref, ...), custom_call_target="tpu_custom_call", output_to_operand_aliasing={{0}: (3, {})} | custom-call | tf_op jit(solution)/shard_map/pack_near/pallas_call | solution.py:326
  6.6 0.2 collective-permute-start.6
  6.8 3.1 %collective-permute-start.8 = (s16[528,128]{1,0:T(8,128)(2,1)S(1)}, s16[528,128]{1,0:T(8,128)(2,1)S(1)}, u32[]{:S(2)}, u32[]{:S(2)}) collective-permute-start(s16[528,128]{1,0:T(8,128)(2,1)S(1)} %get-tuple-element.31), channel_id=1, source_target_pairs={{1,3},{3,1},{5,7},{7,5},{9,11},{11,9},{13,15},{15,13},{17,19},{19,... | collective-permute-start | bytes 405512 | tf_op jit(solution)/shard_map/ppermute | solution.py:338
  9.9 1.7 %collective-permute-start.10 = (s16[528,128]{1,0:T(8,128)(2,1)S(1)}, s16[528,128]{1,0:T(8,128)(2,1)S(1)}, u32[]{:S(2)}, u32[]{:S(2)}) collective-permute-start(s16[528,128]{1,0:T(8,128)(2,1)S(1)} %get-tuple-element.34), channel_id=1, source_target_pairs={{0,12},{1,15},{2,14},{3,13},{4,8},{5,11},{6,10},{7,9},{8,4},{9,7},... | collective-permute-start | bytes 405512 | tf_op jit(solution)/shard_map/ppermute | solution.py:338
  11.7 0.6 %collective-permute-done.4.refs_0_ = s16[528,128]{1,0:T(8,128)(2,1)S(1)} collective-permute-done((s16[528,128]{1,0:T(8,128)(2,1)S(1)}, s16[528,128]{1,0:T(8,128)(2,1)S(1)}, u32[]{:S(2)}, u32[]{:S(2)}) %collective-permute-start.4) | collective-permute-done | bytes 135200 | tf_op jit(solution)/shard_map/ppermute | solution.py:338
  12.2 0.5 %collective-permute-start.5 = (s16[528,128]{1,0:T(8,128)(2,1)S(1)}, s16[528,128]{1,0:T(8,128)(2,1)S(1)}, u32[]{:S(2)}, u32[]{:S(2)}) collective-permute-start(s16[528,128]{1,0:T(8,128)(2,1)S(1)} %collective-permute-done.4.refs_0_), channel_id=1, source_target_pairs={{0,1},{1,0},{2,3},{3,2},{4,5},{5,4},{6,7},{7,6},{8,9},{9,8},{10,11... | collective-permute-start | bytes 405512 | tf_op jit(solution)/shard_map/ppermute | solution.py:274
  12.7 1.4 %direct_local.1 = (bf16[32,256,128]{2,1,0:T(8,128)(2,1)S(1)}, f32[256,128]{1,0:T(8,128)S(1)}, f32[256,128]{1,0:T(8,128)S(1)}) custom-call(s32[2,18]{1,0:T(2,128)} %bitcast.3, s32[2]{0:T(128)} %count_ref.3, bf16[18,128,128]{2,1,0:T(8,128)(2,1)} %tiles_ref.3, bf16[20,512,128]{2,1,0:T(8,128)(2,1)S(1)} %get-tuple-element.23.panels, ...), custom_call_target="tpu_custom_call" | custom-call | flops 10000000000 | tf_op jit(solution)/shard_map/direct_local/pallas_call | solution.py:344
  14.1 0.0 collective-permute-done.6.refs_0_
  14.1 0.1 collective-permute-start.7
  14.2 0.0 collective-permute-done.8.refs_2_
  14.2 0.5 %collective-permute-start.9 = (s16[528,128]{1,0:T(8,128)(2,1)S(1)}, s16[528,128]{1,0:T(8,128)(2,1)S(1)}, u32[]{:S(2)}, u32[]{:S(2)}) collective-permute-start(s16[528,128]{1,0:T(8,128)(2,1)S(1)} %collective-permute-done.8.refs_2_), channel_id=1, source_target_pairs={{0,1},{1,0},{2,3},{3,2},{4,5},{5,4},{6,7},{7,6},{8,9},{9,8},{10,11... | collective-permute-start | bytes 405512 | tf_op jit(solution)/shard_map/ppermute | solution.py:274
  14.7 4.3 %collective-permute-done.10.refs_0_ = s16[528,128]{1,0:T(8,128)(2,1)S(1)} collective-permute-done((s16[528,128]{1,0:T(8,128)(2,1)S(1)}, s16[528,128]{1,0:T(8,128)(2,1)S(1)}, u32[]{:S(2)}, u32[]{:S(2)}) %collective-permute-start.10) | collective-permute-done | bytes 135200 | tf_op jit(solution)/shard_map/ppermute | solution.py:338
  19.0 0.4 %collective-permute-start.11 = (s16[528,128]{1,0:T(8,128)(2,1)S(1)}, s16[528,128]{1,0:T(8,128)(2,1)S(1)}, u32[]{:S(2)}, u32[]{:S(2)}) collective-permute-start(s16[528,128]{1,0:T(8,128)(2,1)S(1)} %collective-permute-done.10.refs_0_), channel_id=1, source_target_pairs={{0,1},{1,0},{2,3},{3,2},{4,5},{5,4},{6,7},{7,6},{8,9},{9,8},{10,11... | collective-permute-start | bytes 405512 | tf_op jit(solution)/shard_map/ppermute | solution.py:274
  19.5 0.0 collective-permute-done.5.refs_1_
  19.5 0.3 %gather_first.1 = (f32[256,128]{1,0:T(8,128)S(1)}, f32[256,128]{1,0:T(8,128)S(1)}) custom-call(bf16[32,256,128]{2,1,0:T(8,128)(2,1)S(1)} %get-tuple-element.24.rows_panels, f32[256,128]{1,0:T(8,128)S(1)} %get-tuple-element.25.direct, f32[256,128]{1,0:T(8,128)S(1)} %get-tuple-element.26.mirror, s16[528,128]{1,0:T(8,128)(2,1)S(1)} %collective-permute-done.4.refs_0_, ...), custom_call_target="tpu_custom_call" | custom-call | flops 10000000000 | tf_op jit(solution)/shard_map/gather_first/pallas_call | solution.py:358
  19.8 0.0 collective-permute-done.7.refs_1_
  19.8 0.0 collective-permute-done.9.refs_3_
  19.8 0.5 %gather_near.1 = (f32[256,128]{1,0:T(8,128)S(1)}, f32[256,128]{1,0:T(8,128)S(1)}) custom-call(bf16[32,256,128]{2,1,0:T(8,128)(2,1)S(1)} %get-tuple-element.24.rows_panels, f32[256,128]{1,0:T(8,128)S(1)} %get-tuple-element.28.direct, f32[256,128]{1,0:T(8,128)S(1)} %get-tuple-element.29.mirror, s16[528,128]{1,0:T(8,128)(2,1)S(1)} %collective-permute-done.6.refs_0_, ...), custom_call_target="tpu_custom_call" | custom-call | flops 10000000000 | tf_op jit(solution)/shard_map/gather_near/pallas_call | solution.py:358
  20.3 0.2 %gather_own.1 = (f32[256,128]{1,0:T(8,128)S(1)}, f32[256,128]{1,0:T(8,128)S(1)}) custom-call(bf16[32,256,128]{2,1,0:T(8,128)(2,1)S(1)} %get-tuple-element.24.rows_panels, f32[256,128]{1,0:T(8,128)S(1)} %get-tuple-element.32.direct, f32[256,128]{1,0:T(8,128)S(1)} %get-tuple-element.33.mirror, s16[528,128]{1,0:T(8,128)(2,1)S(1)} %collective-permute-done.10.refs_0_), custom_call_target="tpu_custom_call" | custom-call | flops 10000000000 | tf_op jit(solution)/shard_map/gather_own/pallas_call | solution.py:358
  20.5 0.0 collective-permute-done.11.refs_0_
  20.5 0.9 %gather_last.1 = f32[256,128]{1,0:T(8,128)} custom-call(bf16[32,256,128]{2,1,0:T(8,128)(2,1)S(1)} %get-tuple-element.24.rows_panels, f32[256,128]{1,0:T(8,128)S(1)} %get-tuple-element.35.direct, f32[256,128]{1,0:T(8,128)S(1)} %get-tuple-element.36.mirror, s16[528,128]{1,0:T(8,128)(2,1)S(1)} %collective-permute-done.11.refs_0_), custom_call_target="tpu_custom_call" | custom-call | tf_op jit(solution)/shard_map/gather_last/pallas_call | solution.py:375
  (2 shorter events, 0.0 us)
Async XLA Ops:
  0.0 2.6 %copy-start = (bf16[256,128]{1,0:T(8,128)(2,1)S(1)}, bf16[256,128]{1,0:T(8,128)(2,1)}, u32[]{:S(2)}) copy-start(bf16[256,128]{1,0:T(8,128)(2,1)} %own_q.1) | copy-start | bytes 196612
  0.0 2.6 %collective-permute-start.2 = (bf16[18,128,128]{2,1,0:T(8,128)(2,1)}, bf16[18,128,128]{2,1,0:T(8,128)(2,1)S(1)}, u32[]{:S(2)}, u32[]{:S(2)}) collective-permute-start(bf16[18,128,128]{2,1,0:T(8,128)(2,1)} %tiles_ref.3), channel_id=1, source_target_pairs={{0,1},{1,0},{2,3},{3,2},{4,5},{5,4},{6,7},{7,6},{8,9},{9,8},{10,11... | collective-permute-start | bytes 1769480 | tf_op jit(solution)/shard_map/ppermute | solution.py:274
  0.7 1.9 %collective-permute-start.3 = (bf16[256,128]{1,0:T(8,128)(2,1)}, bf16[256,128]{1,0:T(8,128)(2,1)S(1)}, u32[]{:S(2)}, u32[]{:S(2)}) collective-permute-start(bf16[256,128]{1,0:T(8,128)(2,1)} %own_q.1), channel_id=1, source_target_pairs={{0,1},{1,0},{2,3},{3,2},{4,5},{5,4},{6,7},{7,6},{8,9},{9,8},{10,11... | collective-permute-start | bytes 196616 | tf_op jit(solution)/shard_map/ppermute | solution.py:274
  0.7 1.9 %collective-permute-start.1 = (s32[2]{0:T(128)}, s32[2]{0:T(128)S(1)}, u32[]{:S(2)}, u32[]{:S(2)}) collective-permute-start(s32[2]{0:T(128)} %count_ref.3), channel_id=1, source_target_pairs={{0,1},{1,0},{2,3},{3,2},{4,5},{5,4},{6,7},{7,6},{8,9},{9,8},{10,11... | collective-permute-start | bytes 32 | tf_op jit(solution)/shard_map/ppermute | solution.py:274
  1.2 1.4 %collective-permute-start = (s32[2,18]{1,0:T(2,128)}, s32[2,18]{1,0:T(2,128)S(1)}, u32[]{:S(2)}, u32[]{:S(2)}) collective-permute-start(s32[2,18]{1,0:T(2,128)} %bitcast.1), channel_id=1, source_target_pairs={{0,1},{1,0},{2,3},{3,2},{4,5},{5,4},{6,7},{7,6},{8,9},{9,8},{10,11... | collective-permute-start | bytes 440 | tf_op jit(solution)/shard_map/ppermute | solution.py:274
  3.7 8.5 %collective-permute-start.4 = (s16[528,128]{1,0:T(8,128)(2,1)S(1)}, s16[528,128]{1,0:T(8,128)(2,1)S(1)}, u32[]{:S(2)}, u32[]{:S(2)}) collective-permute-start(s16[528,128]{1,0:T(8,128)(2,1)S(1)} %get-tuple-element.27), channel_id=1, source_target_pairs={{0,8},{1,11},{2,10},{3,9},{4,12},{5,15},{6,14},{7,13},{8,0},{9,3},... | collective-permute-start | bytes 405512 | tf_op jit(solution)/shard_map/ppermute | solution.py:338
  6.6 7.5 %collective-permute-start.6 = (s16[528,128]{1,0:T(8,128)(2,1)S(1)}, s16[528,128]{1,0:T(8,128)(2,1)S(1)}, u32[]{:S(2)}, u32[]{:S(2)}) collective-permute-start(s16[528,128]{1,0:T(8,128)(2,1)S(1)} %get-tuple-element.30), channel_id=1, source_target_pairs={{0,4},{1,7},{2,6},{3,5},{4,0},{5,3},{6,2},{7,1},{8,12},{9,15},{10,... | collective-permute-start | bytes 405512 | tf_op jit(solution)/shard_map/ppermute | solution.py:338
  6.8 7.4 %collective-permute-start.8 = (s16[528,128]{1,0:T(8,128)(2,1)S(1)}, s16[528,128]{1,0:T(8,128)(2,1)S(1)}, u32[]{:S(2)}, u32[]{:S(2)}) collective-permute-start(s16[528,128]{1,0:T(8,128)(2,1)S(1)} %get-tuple-element.31), channel_id=1, source_target_pairs={{1,3},{3,1},{5,7},{7,5},{9,11},{11,9},{13,15},{15,13},{17,19},{19,... | collective-permute-start | bytes 405512 | tf_op jit(solution)/shard_map/ppermute | solution.py:338
  9.9 9.1 %collective-permute-start.10 = (s16[528,128]{1,0:T(8,128)(2,1)S(1)}, s16[528,128]{1,0:T(8,128)(2,1)S(1)}, u32[]{:S(2)}, u32[]{:S(2)}) collective-permute-start(s16[528,128]{1,0:T(8,128)(2,1)S(1)} %get-tuple-element.34), channel_id=1, source_target_pairs={{0,12},{1,15},{2,14},{3,13},{4,8},{5,11},{6,10},{7,9},{8,4},{9,7},... | collective-permute-start | bytes 405512 | tf_op jit(solution)/shard_map/ppermute | solution.py:338
  12.2 7.2 %collective-permute-start.5 = (s16[528,128]{1,0:T(8,128)(2,1)S(1)}, s16[528,128]{1,0:T(8,128)(2,1)S(1)}, u32[]{:S(2)}, u32[]{:S(2)}) collective-permute-start(s16[528,128]{1,0:T(8,128)(2,1)S(1)} %collective-permute-done.4.refs_0_), channel_id=1, source_target_pairs={{0,1},{1,0},{2,3},{3,2},{4,5},{5,4},{6,7},{7,6},{8,9},{9,8},{10,11... | collective-permute-start | bytes 405512 | tf_op jit(solution)/shard_map/ppermute | solution.py:274
  14.1 5.6 %collective-permute-start.7 = (s16[528,128]{1,0:T(8,128)(2,1)S(1)}, s16[528,128]{1,0:T(8,128)(2,1)S(1)}, u32[]{:S(2)}, u32[]{:S(2)}) collective-permute-start(s16[528,128]{1,0:T(8,128)(2,1)S(1)} %collective-permute-done.6.refs_0_), channel_id=1, source_target_pairs={{0,1},{1,0},{2,3},{3,2},{4,5},{5,4},{6,7},{7,6},{8,9},{9,8},{10,11... | collective-permute-start | bytes 405512 | tf_op jit(solution)/shard_map/ppermute | solution.py:274
  14.2 5.6 %collective-permute-start.9 = (s16[528,128]{1,0:T(8,128)(2,1)S(1)}, s16[528,128]{1,0:T(8,128)(2,1)S(1)}, u32[]{:S(2)}, u32[]{:S(2)}) collective-permute-start(s16[528,128]{1,0:T(8,128)(2,1)S(1)} %collective-permute-done.8.refs_2_), channel_id=1, source_target_pairs={{0,1},{1,0},{2,3},{3,2},{4,5},{5,4},{6,7},{7,6},{8,9},{9,8},{10,11... | collective-permute-start | bytes 405512 | tf_op jit(solution)/shard_map/ppermute | solution.py:274
  19.0 1.5 %collective-permute-start.11 = (s16[528,128]{1,0:T(8,128)(2,1)S(1)}, s16[528,128]{1,0:T(8,128)(2,1)S(1)}, u32[]{:S(2)}, u32[]{:S(2)}) collective-permute-start(s16[528,128]{1,0:T(8,128)(2,1)S(1)} %collective-permute-done.10.refs_0_), channel_id=1, source_target_pairs={{0,1},{1,0},{2,3},{3,2},{4,5},{5,4},{6,7},{7,6},{8,9},{9,8},{10,11... | collective-permute-start | bytes 405512 | tf_op jit(solution)/shard_map/ppermute | solution.py:274

commit v7 on v6

--- a/solution.py
+++ b/solution.py
@@ -215,20 +215,31 @@
         )
 
 
+def is_low(k, mine):
+    chip, core = place()
+    cls = 2 * k + (core if mine else 1 - core)
+    return (chip ^ cls) < chip, cls
+
+
+def own_half(blocks):
+    _, core = place()
+    half = len(blocks) // 2
+    return [
+        jnp.where(core == 0, a, b)
+        for a, b in zip(blocks[:half], blocks[half:], strict=True)
+    ]
+
+
 def gather_part(sources, rows_panels, direct, mirror, messages):
-    tile = rows_panels.shape[2]
-    chip, core = place()
     total = direct[...]
-    mirrored = split(mirror[...], tile)
-    half = len(mirrored)
+    mirrored = split(mirror[...], rows_panels.shape[2])
     for (k, mine), message in zip(sources, messages, strict=True):
-        cls = 2 * k + (core if mine else 1 - core)
-        low = (chip ^ cls) < chip
+        low, cls = is_low(k, mine)
         blocks = read_message(message)
-        total = total + direct_sum(rows_panels, cls * 2 * half, blocks)
+        total = total + direct_sum(rows_panels, cls * len(blocks), blocks)
         mirrored = [
-            m + jnp.where(low, jnp.where(core == 0, a, b), 0.0)
-            for m, a, b in zip(mirrored, blocks[:half], blocks[half:], strict=True)
+            m + jnp.where(low, x, 0.0)
+            for m, x in zip(mirrored, own_half(blocks), strict=True)
         ]
     return total, mirrored
 
@@ -242,18 +253,33 @@
         mirror_out[b * tile:(b + 1) * tile, :] = m
 
 
-def final_kernel(sources, factor, rows_panels, direct, mirror, *refs):
-    *messages, out, result, sems = refs
+def join_kernel(sources, rows_panels, direct, mirror, *refs):
+    *messages, base = refs
     tile = rows_panels.shape[2]
     total, mirrored = gather_part(sources, rows_panels, direct, mirror, messages)
-    copies = []
     for b, (block, m) in enumerate(zip(split(total, tile), mirrored, strict=True)):
-        at = pl.ds(b * tile, tile)
-        result[at, :] = (block + m.T) * factor
-        copies.append(pltpu.make_async_copy(result.at[at], out.at[at], sems.at[b]))
-        copies[-1].start()
-    for copy in copies:
-        copy.wait()
+        base[b * tile:(b + 1) * tile, :] = block + m.T
+
+
+def final_kernel(k, factor, rows_panels, base, message, out, result, sem):
+    tile = rows_panels.shape[2]
+    low, cls = is_low(k, False)
+
+    @pl.when(low)
+    def _():
+        for b, x in enumerate(own_half(read_message(message))):
+            at = slice(b * tile, (b + 1) * tile)
+            result[at, :] = (base[at, :] + x.T) * factor
+
+    @pl.when(jnp.logical_not(low))
+    def _():
+        blocks = read_message(message)
+        total = direct_sum(rows_panels, cls * len(blocks), blocks)
+        result[...] = (base[...] + total) * factor
+
+    copy = pltpu.make_async_copy(result, out, sem)
+    copy.start()
+    copy.wait()
 
 
 VMEM = functools.partial(pl.BlockSpec, memory_space=pltpu.VMEM)
@@ -352,40 +378,44 @@
             name="direct_local",
     )(*own, panels, chip_q)
 
-    other = {k: swap(received[k]) for k in received}
-
-    def gather(sources, direct, mirror, name):
+    def gather(kernel, sources, sums, name, outs, passed=()):
+        sums = list(sums)
         return pl.pallas_call(
-            functools.partial(gather_kernel, sources),
-            out_shape=[half_shape] * 2,
-            in_specs=[VMEM()] * (3 + len(sources)),
-            out_specs=[VMEM()] * 2,
+            functools.partial(kernel, sources),
+            out_shape=[half_shape] * outs + [message] * len(passed),
+            in_specs=[VMEM()] * (1 + len(sums) + len(sources) + len(passed)),
+            out_specs=[VMEM()] * (outs + len(passed)),
+            input_output_aliases={
+                1 + len(sums) + len(sources) + n: outs + n for n in range(len(passed))
+            },
             compiler_params=params,
             cost_estimate=pl.CostEstimate(
                 flops=10**10, bytes_accessed=0, transcendentals=0
             ),
             name=name,
-        )(rows_panels, direct, mirror,
-          *((received if mine else other)[k] for k, mine in sources))
+        )(rows_panels, *sums,
+          *((received if mine else other)[k] for k, mine in sources), *passed)
 
     *late, last = near + far[1:]
-    sums = gather([(far[0], True), (far[0], False)], direct, mirror, "gather_first")
-    sums = gather([(k, mine) for k in late for mine in (True, False)], *sums, "gather_near")
-    sums = gather([(last, True)], *sums, "gather_own")
+    other = {k: swap(received[k]) for k in [far[0], *late, last]}
+    direct, mirror = gather(
+        gather_kernel, [(far[0], True), (far[0], False)], (direct, mirror),
+        "gather_first", 2,
+    )
+    (base,) = gather(
+        join_kernel,
+        [(k, mine) for k in late for mine in (True, False)] + [(last, True)],
+        (direct, mirror), "gather_most", 1,
+    )
     return pl.pallas_call(
-        functools.partial(
-            final_kernel, [(last, False)], 1.0 / math.sqrt(rows * devices)
-        ),
+        functools.partial(final_kernel, last, 1.0 / math.sqrt(rows * devices)),
         out_shape=half_shape,
-        in_specs=[VMEM()] * 4,
+        in_specs=[VMEM()] * 3,
         out_specs=hbm,
-        scratch_shapes=[
-            pltpu.VMEM((rows, columns), wide),
-            pltpu.SemaphoreType.DMA((rows // tile,)),
-        ],
+        scratch_shapes=[pltpu.VMEM((rows, columns), wide), pltpu.SemaphoreType.DMA(())],
         compiler_params=params,
         name="gather_last",
-    )(rows_panels, *sums, other[last])
+    )(rows_panels, base, other[last])
 
 
 def solution(mesh):

time: 21.5 us -> 21.4 us (level)
  the two profiles are of different devices: /device:TPU:11 before, /device:TPU:0 now
where the time goes in v7:
time: 21.4 us; the launch traced here: 21 us
  starting transfers between devices  11.7 us (55%)
  Pallas kernels  6.5 us (30%)
  waiting for transfers between devices  2.67 us (12%)
    ppermute x4, starting transfers between devices, on_device(): lax.ppermute(messages[k], 'row', [(d, d ^ 2 * (2 * k + d % 2)) for d in r...  6.58 us
    ppermute x8, starting transfers between devices, swap(): return lax.ppermute(x, 'row', other_core)  5.14 us
    ppermute x4, waiting for transfers between devices, on_device(): lax.ppermute(messages[k], 'row', [(d, d ^ 2 * (2 * k + d % 2)) for d in r...  2.56 us
    pallas_call x1, Pallas kernels, on_device(): pl.pallas_call(direct_kernel, out_shape=[rows_panels_shape, half_shape, h...  1.65 us
    pallas_call x1, Pallas kernels, on_device(): pl.pallas_call(own_kernel, out_shape=panels_shape, in_specs=[hbm] * 3, ou...  1.44 us
    pallas_call x1, Pallas kernels, on_device(): pl.pallas_call(functools.partial(far_kernel, chips, first), out_shape=[pa...  1.14 us
    pallas_call x1, Pallas kernels, on_device(): pl.pallas_call(functools.partial(final_kernel, last, 1.0 / math.sqrt(rows...  0.9 us
    pallas_call x2, Pallas kernels, gather(): pl.pallas_call(functools.partial(kernel, sources), out_shape=[half_shape]...  0.86 us
  transfers between devices with their start and end apart: 12, of which 2 were waited for; matrix products, arithmetic and copies ran while one was open for 0% of the time, Pallas kernels for 21%

profile of v7, /device:TPU:0, one launch (start us, length us, event | category | flops | bytes accessed | tf_op | source)
XLA Modules:
  0.0 21.0 jit_solution(6459562157567900290)
XLA Ops:
  0.0 0.5 %collective-permute-start.2 = (bf16[18,128,128]{2,1,0:T(8,128)(2,1)}, bf16[18,128,128]{2,1,0:T(8,128)(2,1)S(1)}, u32[]{:S(2)}, u32[]{:S(2)}) collective-permute-start(bf16[18,128,128]{2,1,0:T(8,128)(2,1)} %tiles_ref.3), channel_id=1, source_target_pairs={{0,1},{1,0},{2,3},{3,2},{4,5},{5,4},{6,7},{7,6},{8,9},{9,8},{10,11... | collective-permute-start | bytes 1769480 | tf_op jit(solution)/shard_map/ppermute | solution.py:300
  0.5 0.1 collective-permute-start.3
  0.5 0.4 %collective-permute-start.1 = (s32[2]{0:T(128)}, s32[2]{0:T(128)S(1)}, u32[]{:S(2)}, u32[]{:S(2)}) collective-permute-start(s32[2]{0:T(128)} %count_ref.3), channel_id=1, source_target_pairs={{0,1},{1,0},{2,3},{3,2},{4,5},{5,4},{6,7},{7,6},{8,9},{9,8},{10,11... | collective-permute-start | bytes 32 | tf_op jit(solution)/shard_map/ppermute | solution.py:300
  1.0 0.1 collective-permute-start
  1.0 1.4 %own_tiles.1._ = bf16[20,512,128]{2,1,0:T(8,128)(2,1)S(1)} custom-call(s32[2,18]{1,0:T(2,128)} %bitcast.2, s32[2]{0:T(128)} %count_ref.3, bf16[18,128,128]{2,1,0:T(8,128)(2,1)} %tiles_ref.3), custom_call_target="tpu_custom_call" | custom-call | tf_op jit(solution)/shard_map/own_tiles/pallas_call | solution.py:329
  2.5 0.0 collective-permute-done.1.count_ref
  2.5 0.0 collective-permute-done.index_ref
  2.5 0.0 collective-permute-done.3.other_q
  2.5 0.0 collective-permute-done.2.tiles
  2.5 0.0 copy-done
  2.5 1.1 %pack_far.1 = (bf16[20,512,128]{2,1,0:T(8,128)(2,1)S(1)}, bf16[512,128]{1,0:T(8,128)(2,1)S(1)}, s16[528,128]{1,0:T(8,128)(2,1)S(1)}) custom-call(s32[2,18]{1,0:T(2,128)S(1)} %collective-permute-done.index_ref, s32[2]{0:T(128)S(1)} %collective-permute-done.1.count_ref, ...), custom_call_target="tpu_custom_call", output_to_operand_aliasing={{0}: (5, {})} | custom-call | tf_op jit(solution)/shard_map/pack_far/pallas_call | solution.py:342
  3.7 2.9 %collective-permute-start.4 = (s16[528,128]{1,0:T(8,128)(2,1)S(1)}, s16[528,128]{1,0:T(8,128)(2,1)S(1)}, u32[]{:S(2)}, u32[]{:S(2)}) collective-permute-start(s16[528,128]{1,0:T(8,128)(2,1)S(1)} %get-tuple-element.23), channel_id=1, source_target_pairs={{0,8},{1,11},{2,10},{3,9},{4,12},{5,15},{6,14},{7,13},{8,0},{9,3},... | collective-permute-start | bytes 405512 | tf_op jit(solution)/shard_map/ppermute | solution.py:364
  6.6 0.5 %pack_near.1 = (bf16[20,512,128]{2,1,0:T(8,128)(2,1)S(1)}, s16[528,128]{1,0:T(8,128)(2,1)S(1)}, s16[528,128]{1,0:T(8,128)(2,1)S(1)}, s16[528,128]{1,0:T(8,128)(2,1)S(1)}) custom-call(s32[2,18]{1,0:T(2,128)S(1)} %collective-permute-done.index_ref, s32[2]{0:T(128)S(1)} %collective-permute-done.1.count_ref, ...), custom_call_target="tpu_custom_call", output_to_operand_aliasing={{0}: (3, {})} | custom-call | tf_op jit(solution)/shard_map/pack_near/pallas_call | solution.py:352
  7.1 1.6 %collective-permute-start.6 = (s16[528,128]{1,0:T(8,128)(2,1)S(1)}, s16[528,128]{1,0:T(8,128)(2,1)S(1)}, u32[]{:S(2)}, u32[]{:S(2)}) collective-permute-start(s16[528,128]{1,0:T(8,128)(2,1)S(1)} %get-tuple-element.26), channel_id=1, source_target_pairs={{0,4},{1,7},{2,6},{3,5},{4,0},{5,3},{6,2},{7,1},{8,12},{9,15},{10,... | collective-permute-start | bytes 405512 | tf_op jit(solution)/shard_map/ppermute | solution.py:364
  8.7 0.7 %collective-permute-start.8 = (s16[528,128]{1,0:T(8,128)(2,1)S(1)}, s16[528,128]{1,0:T(8,128)(2,1)S(1)}, u32[]{:S(2)}, u32[]{:S(2)}) collective-permute-start(s16[528,128]{1,0:T(8,128)(2,1)S(1)} %get-tuple-element.27), channel_id=1, source_target_pairs={{1,3},{3,1},{5,7},{7,5},{9,11},{11,9},{13,15},{15,13},{17,19},{19,... | collective-permute-start | bytes 405512 | tf_op jit(solution)/shard_map/ppermute | solution.py:364
  9.4 1.4 %collective-permute-start.10 = (s16[528,128]{1,0:T(8,128)(2,1)S(1)}, s16[528,128]{1,0:T(8,128)(2,1)S(1)}, u32[]{:S(2)}, u32[]{:S(2)}) collective-permute-start(s16[528,128]{1,0:T(8,128)(2,1)S(1)} %get-tuple-element.28), channel_id=1, source_target_pairs={{0,12},{1,15},{2,14},{3,13},{4,8},{5,11},{6,10},{7,9},{8,4},{9,7},... | collective-permute-start | bytes 405512 | tf_op jit(solution)/shard_map/ppermute | solution.py:364
  10.8 0.0 collective-permute-done.4.refs_0_
  10.8 3.0 %collective-permute-start.5 = (s16[528,128]{1,0:T(8,128)(2,1)S(1)}, s16[528,128]{1,0:T(8,128)(2,1)S(1)}, u32[]{:S(2)}, u32[]{:S(2)}) collective-permute-start(s16[528,128]{1,0:T(8,128)(2,1)S(1)} %collective-permute-done.4.refs_0_), channel_id=1, source_target_pairs={{0,1},{1,0},{2,3},{3,2},{4,5},{5,4},{6,7},{7,6},{8,9},{9,8},{10,11... | collective-permute-start | bytes 405512 | tf_op jit(solution)/shard_map/ppermute | solution.py:300
  13.8 1.6 %direct_local.1 = (bf16[32,256,128]{2,1,0:T(8,128)(2,1)S(1)}, f32[256,128]{1,0:T(8,128)S(1)}, f32[256,128]{1,0:T(8,128)S(1)}) custom-call(s32[2,18]{1,0:T(2,128)} %bitcast.3, s32[2]{0:T(128)} %count_ref.3, bf16[18,128,128]{2,1,0:T(8,128)(2,1)} %tiles_ref.3, bf16[20,512,128]{2,1,0:T(8,128)(2,1)S(1)} %get-tuple-element.19.panels, ...), custom_call_target="tpu_custom_call" | custom-call | flops 10000000000 | tf_op jit(solution)/shard_map/direct_local/pallas_call | solution.py:370
  15.4 0.0 collective-permute-done.6.refs_0_
  15.4 0.1 collective-permute-start.7
  15.5 0.0 collective-permute-done.8.refs_2_
  15.5 0.5 %collective-permute-start.9 = (s16[528,128]{1,0:T(8,128)(2,1)S(1)}, s16[528,128]{1,0:T(8,128)(2,1)S(1)}, u32[]{:S(2)}, u32[]{:S(2)}) collective-permute-start(s16[528,128]{1,0:T(8,128)(2,1)S(1)} %collective-permute-done.8.refs_2_), channel_id=1, source_target_pairs={{0,1},{1,0},{2,3},{3,2},{4,5},{5,4},{6,7},{7,6},{8,9},{9,8},{10,11... | collective-permute-start | bytes 405512 | tf_op jit(solution)/shard_map/ppermute | solution.py:300
  16.0 2.5 %collective-permute-done.10.refs_4_ = s16[528,128]{1,0:T(8,128)(2,1)S(1)} collective-permute-done((s16[528,128]{1,0:T(8,128)(2,1)S(1)}, s16[528,128]{1,0:T(8,128)(2,1)S(1)}, u32[]{:S(2)}, u32[]{:S(2)}) %collective-permute-start.10) | collective-permute-done | bytes 135200 | tf_op jit(solution)/shard_map/ppermute | solution.py:364
  18.6 0.6 %collective-permute-start.11 = (s16[528,128]{1,0:T(8,128)(2,1)S(1)}, s16[528,128]{1,0:T(8,128)(2,1)S(1)}, u32[]{:S(2)}, u32[]{:S(2)}) collective-permute-start(s16[528,128]{1,0:T(8,128)(2,1)S(1)} %collective-permute-done.10.refs_4_), channel_id=1, source_target_pairs={{0,1},{1,0},{2,3},{3,2},{4,5},{5,4},{6,7},{7,6},{8,9},{9,8},{10,11... | collective-permute-start | bytes 405512 | tf_op jit(solution)/shard_map/ppermute | solution.py:300
  19.1 0.0 collective-permute-done.5.refs_1_
  19.1 0.3 %gather_first.1 = (f32[256,128]{1,0:T(8,128)S(1)}, f32[256,128]{1,0:T(8,128)S(1)}) custom-call(bf16[32,256,128]{2,1,0:T(8,128)(2,1)S(1)} %get-tuple-element.20.rows_panels, f32[256,128]{1,0:T(8,128)S(1)} %get-tuple-element.21.direct, f32[256,128]{1,0:T(8,128)S(1)} %get-tuple-element.22.mirror, s16[528,128]{1,0:T(8,128)(2,1)S(1)} %collective-permute-done.4.refs_0_, ...), custom_call_target="tpu_custom_call" | custom-call | flops 10000000000 | tf_op jit(solution)/shard_map/gather_first/pallas_call | solution.py:383
  19.5 0.0 collective-permute-done.7.refs_1_
  19.5 0.0 collective-permute-done.9.refs_3_
  19.5 0.5 %gather_most.1.base = f32[256,128]{1,0:T(8,128)S(1)} custom-call(bf16[32,256,128]{2,1,0:T(8,128)(2,1)S(1)} %get-tuple-element.20.rows_panels, f32[256,128]{1,0:T(8,128)S(1)} %get-tuple-element.24.direct, f32[256,128]{1,0:T(8,128)S(1)} %get-tuple-element.25.mirror, s16[528,128]{1,0:T(8,128)(2,1)S(1)} %collective-permute-done.6.refs_0_, ...), custom_call_target="tpu_custom_call" | custom-call | flops 10000000000 | tf_op jit(solution)/shard_map/gather_most/pallas_call | solution.py:383
  20.0 0.1 collective-permute-done.11.message
  20.1 0.9 %gather_last.1 = f32[256,128]{1,0:T(8,128)} custom-call(bf16[32,256,128]{2,1,0:T(8,128)(2,1)S(1)} %get-tuple-element.20.rows_panels, f32[256,128]{1,0:T(8,128)S(1)} %gather_most.1.base, s16[528,128]{1,0:T(8,128)(2,1)S(1)} %collective-permute-done.11.message), custom_call_target="tpu_custom_call" | custom-call | tf_op jit(solution)/shard_map/gather_last/pallas_call | solution.py:410
  (1 shorter events, 0.0 us)
Async XLA Ops:
  0.0 2.5 %copy-start = (bf16[256,128]{1,0:T(8,128)(2,1)S(1)}, bf16[256,128]{1,0:T(8,128)(2,1)}, u32[]{:S(2)}) copy-start(bf16[256,128]{1,0:T(8,128)(2,1)} %own_q.1) | copy-start | bytes 196612
  0.0 2.5 %collective-permute-start.2 = (bf16[18,128,128]{2,1,0:T(8,128)(2,1)}, bf16[18,128,128]{2,1,0:T(8,128)(2,1)S(1)}, u32[]{:S(2)}, u32[]{:S(2)}) collective-permute-start(bf16[18,128,128]{2,1,0:T(8,128)(2,1)} %tiles_ref.3), channel_id=1, source_target_pairs={{0,1},{1,0},{2,3},{3,2},{4,5},{5,4},{6,7},{7,6},{8,9},{9,8},{10,11... | collective-permute-start | bytes 1769480 | tf_op jit(solution)/shard_map/ppermute | solution.py:300
  0.5 2.0 %collective-permute-start.3 = (bf16[256,128]{1,0:T(8,128)(2,1)}, bf16[256,128]{1,0:T(8,128)(2,1)S(1)}, u32[]{:S(2)}, u32[]{:S(2)}) collective-permute-start(bf16[256,128]{1,0:T(8,128)(2,1)} %own_q.1), channel_id=1, source_target_pairs={{0,1},{1,0},{2,3},{3,2},{4,5},{5,4},{6,7},{7,6},{8,9},{9,8},{10,11... | collective-permute-start | bytes 196616 | tf_op jit(solution)/shard_map/ppermute | solution.py:300
  0.5 2.0 %collective-permute-start.1 = (s32[2]{0:T(128)}, s32[2]{0:T(128)S(1)}, u32[]{:S(2)}, u32[]{:S(2)}) collective-permute-start(s32[2]{0:T(128)} %count_ref.3), channel_id=1, source_target_pairs={{0,1},{1,0},{2,3},{3,2},{4,5},{5,4},{6,7},{7,6},{8,9},{9,8},{10,11... | collective-permute-start | bytes 32 | tf_op jit(solution)/shard_map/ppermute | solution.py:300
  1.0 1.5 %collective-permute-start = (s32[2,18]{1,0:T(2,128)}, s32[2,18]{1,0:T(2,128)S(1)}, u32[]{:S(2)}, u32[]{:S(2)}) collective-permute-start(s32[2,18]{1,0:T(2,128)} %bitcast.1), channel_id=1, source_target_pairs={{0,1},{1,0},{2,3},{3,2},{4,5},{5,4},{6,7},{7,6},{8,9},{9,8},{10,11... | collective-permute-start | bytes 440 | tf_op jit(solution)/shard_map/ppermute | solution.py:300
  3.7 7.1 %collective-permute-start.4 = (s16[528,128]{1,0:T(8,128)(2,1)S(1)}, s16[528,128]{1,0:T(8,128)(2,1)S(1)}, u32[]{:S(2)}, u32[]{:S(2)}) collective-permute-start(s16[528,128]{1,0:T(8,128)(2,1)S(1)} %get-tuple-element.23), channel_id=1, source_target_pairs={{0,8},{1,11},{2,10},{3,9},{4,12},{5,15},{6,14},{7,13},{8,0},{9,3},... | collective-permute-start | bytes 405512 | tf_op jit(solution)/shard_map/ppermute | solution.py:364
  7.1 8.3 %collective-permute-start.6 = (s16[528,128]{1,0:T(8,128)(2,1)S(1)}, s16[528,128]{1,0:T(8,128)(2,1)S(1)}, u32[]{:S(2)}, u32[]{:S(2)}) collective-permute-start(s16[528,128]{1,0:T(8,128)(2,1)S(1)} %get-tuple-element.26), channel_id=1, source_target_pairs={{0,4},{1,7},{2,6},{3,5},{4,0},{5,3},{6,2},{7,1},{8,12},{9,15},{10,... | collective-permute-start | bytes 405512 | tf_op jit(solution)/shard_map/ppermute | solution.py:364
  8.7 6.8 %collective-permute-start.8 = (s16[528,128]{1,0:T(8,128)(2,1)S(1)}, s16[528,128]{1,0:T(8,128)(2,1)S(1)}, u32[]{:S(2)}, u32[]{:S(2)}) collective-permute-start(s16[528,128]{1,0:T(8,128)(2,1)S(1)} %get-tuple-element.27), channel_id=1, source_target_pairs={{1,3},{3,1},{5,7},{7,5},{9,11},{11,9},{13,15},{15,13},{17,19},{19,... | collective-permute-start | bytes 405512 | tf_op jit(solution)/shard_map/ppermute | solution.py:364
  9.4 9.2 %collective-permute-start.10 = (s16[528,128]{1,0:T(8,128)(2,1)S(1)}, s16[528,128]{1,0:T(8,128)(2,1)S(1)}, u32[]{:S(2)}, u32[]{:S(2)}) collective-permute-start(s16[528,128]{1,0:T(8,128)(2,1)S(1)} %get-tuple-element.28), channel_id=1, source_target_pairs={{0,12},{1,15},{2,14},{3,13},{4,8},{5,11},{6,10},{7,9},{8,4},{9,7},... | collective-permute-start | bytes 405512 | tf_op jit(solution)/shard_map/ppermute | solution.py:364
  10.8 8.4 %collective-permute-start.5 = (s16[528,128]{1,0:T(8,128)(2,1)S(1)}, s16[528,128]{1,0:T(8,128)(2,1)S(1)}, u32[]{:S(2)}, u32[]{:S(2)}) collective-permute-start(s16[528,128]{1,0:T(8,128)(2,1)S(1)} %collective-permute-done.4.refs_0_), channel_id=1, source_target_pairs={{0,1},{1,0},{2,3},{3,2},{4,5},{5,4},{6,7},{7,6},{8,9},{9,8},{10,11... | collective-permute-start | bytes 405512 | tf_op jit(solution)/shard_map/ppermute | solution.py:300
  15.4 4.0 %collective-permute-start.7 = (s16[528,128]{1,0:T(8,128)(2,1)S(1)}, s16[528,128]{1,0:T(8,128)(2,1)S(1)}, u32[]{:S(2)}, u32[]{:S(2)}) collective-permute-start(s16[528,128]{1,0:T(8,128)(2,1)S(1)} %collective-permute-done.6.refs_0_), channel_id=1, source_target_pairs={{0,1},{1,0},{2,3},{3,2},{4,5},{5,4},{6,7},{7,6},{8,9},{9,8},{10,11... | collective-permute-start | bytes 405512 | tf_op jit(solution)/shard_map/ppermute | solution.py:300
  15.5 4.0 %collective-permute-start.9 = (s16[528,128]{1,0:T(8,128)(2,1)S(1)}, s16[528,128]{1,0:T(8,128)(2,1)S(1)}, u32[]{:S(2)}, u32[]{:S(2)}) collective-permute-start(s16[528,128]{1,0:T(8,128)(2,1)S(1)} %collective-permute-done.8.refs_2_), channel_id=1, source_target_pairs={{0,1},{1,0},{2,3},{3,2},{4,5},{5,4},{6,7},{7,6},{8,9},{9,8},{10,11... | collective-permute-start | bytes 405512 | tf_op jit(solution)/shard_map/ppermute | solution.py:300
  18.6 1.6 %collective-permute-start.11 = (s16[528,128]{1,0:T(8,128)(2,1)S(1)}, s16[528,128]{1,0:T(8,128)(2,1)S(1)}, u32[]{:S(2)}, u32[]{:S(2)}) collective-permute-start(s16[528,128]{1,0:T(8,128)(2,1)S(1)} %collective-permute-done.10.refs_4_), channel_id=1, source_target_pairs={{0,1},{1,0},{2,3},{3,2},{4,5},{5,4},{6,7},{7,6},{8,9},{9,8},{10,11... | collective-permute-start | bytes 405512 | tf_op jit(solution)/shard_map/ppermute | solution.py:300

commit v8 on v7

--- a/solution.py
+++ b/solution.py
@@ -40,7 +40,6 @@
     chip, core = place()
     tile = tiles.shape[1]
     local = panels.shape[0] // chip_blocks - 1
-    live = live_tiles(count)
 
     def put(s, carry):
         i, j = index[0, s], index[1, s]
@@ -50,12 +49,12 @@
         def _():
             slot = jnp.where(cls == 0, local, cls // 2)
             panel = slot * chip_blocks + j % chip_blocks
-            at = pl.multiple_of((i % chip_blocks) * tile, tile)
+            at = pl.multiple_of((i % (chip_blocks // 2)) * tile, tile)
             panels[panel, pl.ds(at, tile), :] = tiles[s]
 
         return carry
 
-    lax.fori_loop(0, live, put, 0)
+    lax.fori_loop(0, live_tiles(count), put, 0)
 
 
 def fetch(sems, *pairs):
@@ -72,11 +71,11 @@
     panels[...] = jnp.zeros_like(panels)
     for copy in copies:
         copy.wait()
-    put_tiles(index, count, tiles, panels, panels.shape[1] // panels.shape[2])
+    put_tiles(index, count, tiles, panels, 2 * panels.shape[1] // panels.shape[2])
 
 
 def direct_kernel(
-    index_ref, count_ref, tiles_ref, panels, chip_q, rows_panels, direct, mirror,
+    index_ref, count_ref, tiles_ref, chip_q, rows_panels, direct,
     index, count, tiles, sems,
 ):
     copies = fetch(sems, (index_ref, index), (count_ref, count), (tiles_ref, tiles))
@@ -86,7 +85,7 @@
     tile = tiles.shape[1]
     rows = rows_panels.shape[1]
     chip_blocks = 2 * rows // tile
-    chip, core = place()
+    chip, _ = place()
 
     def put(s, carry):
         i, j = index[0, s], index[1, s]
@@ -97,12 +96,6 @@
 
     lax.fori_loop(0, live_tiles(count), put, 0)
     direct[...] = direct_sum(rows_panels, 0, split(chip_q[...], tile))
-    q_t = chip_q[...].T
-    local = panels.shape[0] - chip_blocks + core * (chip_blocks // 2)
-    for b in range(rows // tile):
-        mirror[b * tile:(b + 1) * tile, :] = jnp.dot(
-            q_t, panels[local + b], preferred_element_type=jnp.float32
-        )
 
 
 def write_message(message, blocks):
@@ -131,15 +124,20 @@
     ]
 
 
-def mirrored_blocks(q_t, panels, slot):
-    tile = panels.shape[2]
-    chip_blocks = panels.shape[1] // tile
-    blocks = []
-    for g in range(slot * chip_blocks, (slot + 1) * chip_blocks, 2):
-        pair = jnp.concatenate([panels[g], panels[g + 1]], axis=1)
-        sums = jnp.dot(q_t, pair, preferred_element_type=jnp.float32)
-        blocks += [sums[:, :tile], sums[:, tile:]]
-    return blocks
+def mirrored_blocks(parts, blocks):
+    tile = parts[0][1].shape[2]
+    sums = []
+    for b in range(0, blocks, 2):
+        pair = sum(
+            jnp.dot(
+                q_t,
+                jnp.concatenate([panels[g + b], panels[g + b + 1]], axis=1),
+                preferred_element_type=jnp.float32,
+            )
+            for q_t, panels, g in parts
+        )
+        sums += [pair[:, :tile], pair[:, tile:]]
+    return sums
 
 
 def direct_sum(panels, start, blocks):
@@ -161,10 +159,11 @@
 
 
 def far_kernel(
-    chips, slots, index_ref, count_ref, tiles, own_q, other_q, _, panels, chip_q, *refs
+    chips, k, index_ref, count_ref, tiles, own_q, other_q, own_panels,
+    chip_q, message, panels, index, count, sems,
 ):
-    *messages, index, count, sems = refs
-    rows, tile = own_q.shape[0], panels.shape[2]
+    rows, tile = own_q.shape[0], tiles.shape[1]
+    chip_blocks = 2 * rows // tile
     _, core = place()
     chip_q[pl.ds(pl.multiple_of(core * rows, rows), rows), :] = own_q[...]
     chip_q[pl.ds(pl.multiple_of((1 - core) * rows, rows), rows), :] = other_q[...]
@@ -172,47 +171,63 @@
     @pl.when(in_lower_half(chips))
     def _():
         copies = fetch(sems, (index_ref, index), (count_ref, count))
-        q_t = chip_q[...].T
+        panels[...] = jnp.zeros_like(panels)
+        own_t, other_t = own_q[...].T, other_q[...].T
         for copy in copies:
             copy.wait()
-        put_tiles(index, count, tiles, panels, panels.shape[1] // tile)
+        put_tiles(index, count, tiles, panels, chip_blocks)
+        first = k * chip_blocks
+        parts = [(own_t, own_panels, first), (other_t, panels, first)]
+        write_message(message, mirrored_blocks(parts, chip_blocks))
+
+    @pl.when(jnp.logical_not(in_lower_half(chips)))
+    def _():
+        write_message(message, split(chip_q[...].astype(jnp.float32), tile))
+
+
+def near_kernel(
+    chips, slots, index_ref, count_ref, tiles, own_panels, far_panels, chip_q, *refs
+):
+    *messages, mirror, panels, index, count, sems = refs
+    rows, tile = own_panels.shape[1:]
+    chip_blocks = 2 * rows // tile
+    chip, core = place()
+
+    def write(other_panels):
+        def transposed(at):
+            return chip_q[pl.ds(pl.multiple_of(at * rows, rows), rows), :].T
+
+        own_t, other_t = transposed(core), transposed(1 - core)
+
+        def mirrored(first, blocks):
+            return mirrored_blocks(
+                [(own_t, own_panels, first), (other_t, other_panels, first)], blocks
+            )
+
+        q = split(chip_q[...].astype(jnp.float32), tile)
         for k, message in zip(slots, messages, strict=True):
-            write_message(message, mirrored_blocks(q_t, panels, k))
+            up = chip < (chip ^ (2 * k + core))
+            blocks = mirrored(k * chip_blocks, chip_blocks)
+            write_message(
+                message, [jnp.where(up, m, x) for m, x in zip(blocks, q, strict=True)]
+            )
+        half = chip_blocks // 2
+        local = mirrored(other_panels.shape[0] - chip_blocks + core * half, half)
+        for b, m in enumerate(local):
+            mirror[b * tile:(b + 1) * tile, :] = m
+
+    @pl.when(in_lower_half(chips))
+    def _():
+        write(far_panels)
 
     @pl.when(jnp.logical_not(in_lower_half(chips)))
     def _():
-        write_message(messages[0], split(chip_q[...].astype(jnp.float32), tile))
-        for message in messages[1:]:
-            message[...] = messages[0][...]
-
-
-def near_kernel(
-    chips, slots, index_ref, count_ref, tiles, _, chip_q, panels, *refs
-):
-    *messages, index, count, sems = refs
-    tile = panels.shape[2]
-    chip, core = place()
-    q = chip_q[...]
-
-    @pl.when(jnp.logical_not(in_lower_half(chips)))
-    def _():
-        for copy in fetch(sems, (index_ref, index), (count_ref, count)):
+        copies = fetch(sems, (index_ref, index), (count_ref, count))
+        panels[...] = jnp.zeros_like(panels)
+        for copy in copies:
             copy.wait()
-        put_tiles(index, count, tiles, panels, panels.shape[1] // tile)
-
-    q_t = q.T
-    q_wide = q.astype(jnp.float32)
-    for k, message in zip(slots, messages, strict=True):
-        up = chip < (chip ^ (2 * k + core))
-        write_message(
-            message,
-            [
-                jnp.where(up, m, own)
-                for m, own in zip(
-                    mirrored_blocks(q_t, panels, k), split(q_wide, tile), strict=True
-                )
-            ],
-        )
+        put_tiles(index, count, tiles, panels, chip_blocks)
+        write(panels)
 
 
 def is_low(k, mine):
@@ -306,7 +321,7 @@
     other_count = swap(tile_count)
 
     panels_shape = jax.ShapeDtypeStruct(
-        ((slots + 1) * chip_blocks, chip_rows, tile), jnp.bfloat16
+        ((slots + 1) * chip_blocks, rows, tile), jnp.bfloat16
     )
     rows_panels_shape = jax.ShapeDtypeStruct(
         (chips * chip_blocks, rows, tile), jnp.bfloat16
@@ -338,45 +353,47 @@
     far = list(range(slots // 2, slots))
     near = list(reversed(range(slots // 2)))
     rest = near + far[1:]
-    first = far[:1]
-    panels, chip_q, *far_messages = pl.pallas_call(
-        functools.partial(far_kernel, chips, first),
-        out_shape=[panels_shape, q_shape] + [message] * len(first),
-        in_specs=[pl.BlockSpec(memory_space=pl.ANY)] * 2 + [VMEM()] * 4,
-        out_specs=[VMEM()] * (2 + len(first)),
-        scratch_shapes=own_scratch[:2] + [pltpu.SemaphoreType.DMA((2,))],
-        input_output_aliases={5: 0},
+    other = (other_index, other_count, other_tiles)
+    other_specs = [pl.BlockSpec(memory_space=pl.ANY)] * 2 + [VMEM()]
+    other_scratch = [*own_scratch[:2], pltpu.SemaphoreType.DMA((2,))]
+    chip_q, far_message, far_panels = pl.pallas_call(
+        functools.partial(far_kernel, chips, far[0]),
+        out_shape=[q_shape, message, panels_shape],
+        in_specs=other_specs + [VMEM()] * 3,
+        out_specs=[VMEM()] * 3,
+        scratch_shapes=other_scratch,
         compiler_params=params,
         name="pack_far",
-    )(other_index, other_count, other_tiles, q_block, other_q, own_panels)
-    panels, *rest_messages = pl.pallas_call(
+    )(*other, q_block, other_q, own_panels)
+    *rest_messages, mirror = pl.pallas_call(
         functools.partial(near_kernel, chips, rest),
-        out_shape=[panels_shape] + [message] * len(rest),
-        in_specs=[pl.BlockSpec(memory_space=pl.ANY)] * 2 + [VMEM()] * 3,
-        out_specs=[VMEM()] * (1 + len(rest)),
-        scratch_shapes=own_scratch[:2] + [pltpu.SemaphoreType.DMA((2,))],
-        input_output_aliases={3: 0},
+        out_shape=[message] * len(rest) + [half_shape],
+        in_specs=other_specs + [VMEM()] * 3,
+        out_specs=[VMEM()] * (len(rest) + 1),
+        scratch_shapes=[pltpu.VMEM(panels_shape.shape, jnp.bfloat16), *other_scratch],
         compiler_params=params,
         name="pack_near",
-    )(other_index, other_count, other_tiles, panels, chip_q)
-    messages = dict(zip(first + rest, far_messages + rest_messages, strict=True))
+    )(*other, own_panels, far_panels, chip_q)
+    messages = dict(zip(far[:1] + rest, [far_message, *rest_messages], strict=True))
     received = {
         k: lax.ppermute(messages[k], "row", [
             (d, d ^ (2 * (2 * k + d % 2))) for d in range(devices) if 2 * k + d % 2
         ])
-        for k in first + rest
+        for k in far[:1] + rest
     }
 
-    rows_panels, direct, mirror = pl.pallas_call(
+    rows_panels, direct = pl.pallas_call(
         direct_kernel,
-        out_shape=[rows_panels_shape, half_shape, half_shape],
-        in_specs=[hbm] * 3 + [VMEM()] * 2,
-        out_specs=[VMEM()] * 3,
+        out_shape=[rows_panels_shape, half_shape],
+        in_specs=[hbm] * 3 + [VMEM()],
+        out_specs=[VMEM()] * 2,
         scratch_shapes=own_scratch,
         compiler_params=params,
-        cost_estimate=pl.CostEstimate(flops=10000000000, bytes_accessed=0, transcendentals=0),
-            name="direct_local",
-    )(*own, panels, chip_q)
+        cost_estimate=pl.CostEstimate(
+            flops=10**10, bytes_accessed=0, transcendentals=0
+        ),
+        name="direct_local",
+    )(*own, chip_q)
 
     def gather(kernel, sources, sums, name, outs, passed=()):
         sums = list(sums)

time: 21.4 us -> 21.4 us (level)
  no operation moved by 1% of the time
where the time goes in v8:
time: 21.4 us; the launch traced here: 21 us
  starting transfers between devices  11.7 us (55%)
  Pallas kernels  6.46 us (30%)
  waiting for transfers between devices  2.75 us (13%)
    ppermute x4, starting transfers between devices, on_device(): lax.ppermute(messages[k], 'row', [(d, d ^ 2 * (2 * k + d % 2)) for d in r...  6.64 us
    ppermute x8, starting transfers between devices, swap(): return lax.ppermute(x, 'row', other_core)  5.04 us
    ppermute x4, waiting for transfers between devices, on_device(): lax.ppermute(messages[k], 'row', [(d, d ^ 2 * (2 * k + d % 2)) for d in r...  2.65 us
    pallas_call x1, Pallas kernels, on_device(): pl.pallas_call(direct_kernel, out_shape=[rows_panels_shape, half_shape],...  1.57 us
    pallas_call x1, Pallas kernels, on_device(): pl.pallas_call(own_kernel, out_shape=panels_shape, in_specs=[hbm] * 3, ou...  1.45 us
    pallas_call x1, Pallas kernels, on_device(): pl.pallas_call(functools.partial(far_kernel, chips, far[0]), out_shape=[q...  1.14 us
    pallas_call x1, Pallas kernels, on_device(): pl.pallas_call(functools.partial(final_kernel, last, 1.0 / math.sqrt(rows...  0.9 us
    pallas_call x2, Pallas kernels, gather(): pl.pallas_call(functools.partial(kernel, sources), out_shape=[half_shape]...  0.88 us
  transfers between devices with their start and end apart: 12, of which 2 were waited for; matrix products, arithmetic and copies ran while one was open for 0% of the time, Pallas kernels for 21%

profile of v8, /device:TPU:0, one launch (start us, length us, event | category | flops | bytes accessed | tf_op | source)
XLA Modules:
  0.0 21.0 jit_solution(6879193866506390636)
XLA Ops:
  0.0 0.5 %collective-permute-start.2 = (bf16[18,128,128]{2,1,0:T(8,128)(2,1)}, bf16[18,128,128]{2,1,0:T(8,128)(2,1)S(1)}, u32[]{:S(2)}, u32[]{:S(2)}) collective-permute-start(bf16[18,128,128]{2,1,0:T(8,128)(2,1)} %tiles_ref.3), channel_id=1, source_target_pairs={{0,1},{1,0},{2,3},{3,2},{4,5},{5,4},{6,7},{7,6},{8,9},{9,8},{10,11... | collective-permute-start | bytes 1769480 | tf_op jit(solution)/shard_map/ppermute | solution.py:315
  0.5 0.1 collective-permute-start.3
  0.5 0.4 %collective-permute-start.1 = (s32[2]{0:T(128)}, s32[2]{0:T(128)S(1)}, u32[]{:S(2)}, u32[]{:S(2)}) collective-permute-start(s32[2]{0:T(128)} %count_ref.3), channel_id=1, source_target_pairs={{0,1},{1,0},{2,3},{3,2},{4,5},{5,4},{6,7},{7,6},{8,9},{9,8},{10,11... | collective-permute-start | bytes 32 | tf_op jit(solution)/shard_map/ppermute | solution.py:315
  1.0 0.1 collective-permute-start
  1.0 1.4 %own_tiles.1.own_panels = bf16[20,256,128]{2,1,0:T(8,128)(2,1)S(1)} custom-call(s32[2,18]{1,0:T(2,128)} %bitcast.2, s32[2]{0:T(128)} %count_ref.3, bf16[18,128,128]{2,1,0:T(8,128)(2,1)} %tiles_ref.3), custom_call_target="tpu_custom_call" | custom-call | tf_op jit(solution)/shard_map/own_tiles/pallas_call | solution.py:344
  2.5 0.0 collective-permute-done.1.count_ref
  2.5 0.0 collective-permute-done.index_ref
  2.5 0.0 collective-permute-done.3.other_q
  2.5 0.0 collective-permute-done.2.tiles
  2.5 0.0 copy-done
  2.5 1.1 %pack_far.1 = (bf16[512,128]{1,0:T(8,128)(2,1)S(1)}, s16[528,128]{1,0:T(8,128)(2,1)S(1)}, bf16[20,256,128]{2,1,0:T(8,128)(2,1)S(1)}) custom-call(s32[2,18]{1,0:T(2,128)S(1)} %collective-permute-done.index_ref, s32[2]{0:T(128)S(1)} %collective-permute-done.1.count_ref, bf16[18,128,128]{2,1,0:T(8,128)(2,1)S(1)} %collective-permute-done.2.tiles, ...), custom_call_target="tpu_custom_call" | custom-call | tf_op jit(solution)/shard_map/pack_far/pallas_call | solution.py:359
  3.7 2.9 %collective-permute-start.4 = (s16[528,128]{1,0:T(8,128)(2,1)S(1)}, s16[528,128]{1,0:T(8,128)(2,1)S(1)}, u32[]{:S(2)}, u32[]{:S(2)}) collective-permute-start(s16[528,128]{1,0:T(8,128)(2,1)S(1)} %get-tuple-element.21), channel_id=1, source_target_pairs={{0,8},{1,11},{2,10},{3,9},{4,12},{5,15},{6,14},{7,13},{8,0},{9,3},... | collective-permute-start | bytes 405512 | tf_op jit(solution)/shard_map/ppermute | solution.py:379
  6.6 0.5 %pack_near.1 = (s16[528,128]{1,0:T(8,128)(2,1)S(1)}, s16[528,128]{1,0:T(8,128)(2,1)S(1)}, s16[528,128]{1,0:T(8,128)(2,1)S(1)}, f32[256,128]{1,0:T(8,128)S(1)}) custom-call(s32[2,18]{1,0:T(2,128)S(1)} %collective-permute-done.index_ref, s32[2]{0:T(128)S(1)} %collective-permute-done.1.count_ref, bf16[18,128,128]{2,1,0:T(8,128)(2,1)S(1)} %collective-permute-done.2.tiles, ...), custom_call_target="tpu_custom_call" | custom-call | tf_op jit(solution)/shard_map/pack_near/pallas_call | solution.py:368
  7.1 1.6 %collective-permute-start.6 = (s16[528,128]{1,0:T(8,128)(2,1)S(1)}, s16[528,128]{1,0:T(8,128)(2,1)S(1)}, u32[]{:S(2)}, u32[]{:S(2)}) collective-permute-start(s16[528,128]{1,0:T(8,128)(2,1)S(1)} %get-tuple-element.24), channel_id=1, source_target_pairs={{0,4},{1,7},{2,6},{3,5},{4,0},{5,3},{6,2},{7,1},{8,12},{9,15},{10,... | collective-permute-start | bytes 405512 | tf_op jit(solution)/shard_map/ppermute | solution.py:379
  8.7 0.7 %collective-permute-start.8 = (s16[528,128]{1,0:T(8,128)(2,1)S(1)}, s16[528,128]{1,0:T(8,128)(2,1)S(1)}, u32[]{:S(2)}, u32[]{:S(2)}) collective-permute-start(s16[528,128]{1,0:T(8,128)(2,1)S(1)} %get-tuple-element.25), channel_id=1, source_target_pairs={{1,3},{3,1},{5,7},{7,5},{9,11},{11,9},{13,15},{15,13},{17,19},{19,... | collective-permute-start | bytes 405512 | tf_op jit(solution)/shard_map/ppermute | solution.py:379
  9.4 1.5 %collective-permute-start.10 = (s16[528,128]{1,0:T(8,128)(2,1)S(1)}, s16[528,128]{1,0:T(8,128)(2,1)S(1)}, u32[]{:S(2)}, u32[]{:S(2)}) collective-permute-start(s16[528,128]{1,0:T(8,128)(2,1)S(1)} %get-tuple-element.26), channel_id=1, source_target_pairs={{0,12},{1,15},{2,14},{3,13},{4,8},{5,11},{6,10},{7,9},{8,4},{9,7},... | collective-permute-start | bytes 405512 | tf_op jit(solution)/shard_map/ppermute | solution.py:379
  10.9 0.0 collective-permute-done.4.refs_0_
  10.9 3.0 %collective-permute-start.5 = (s16[528,128]{1,0:T(8,128)(2,1)S(1)}, s16[528,128]{1,0:T(8,128)(2,1)S(1)}, u32[]{:S(2)}, u32[]{:S(2)}) collective-permute-start(s16[528,128]{1,0:T(8,128)(2,1)S(1)} %collective-permute-done.4.refs_0_), channel_id=1, source_target_pairs={{0,1},{1,0},{2,3},{3,2},{4,5},{5,4},{6,7},{7,6},{8,9},{9,8},{10,11... | collective-permute-start | bytes 405512 | tf_op jit(solution)/shard_map/ppermute | solution.py:315
  13.9 1.6 %direct_local.1 = (bf16[32,256,128]{2,1,0:T(8,128)(2,1)S(1)}, f32[256,128]{1,0:T(8,128)S(1)}) custom-call(s32[2,18]{1,0:T(2,128)} %bitcast.3, s32[2]{0:T(128)} %count_ref.3, bf16[18,128,128]{2,1,0:T(8,128)(2,1)} %tiles_ref.3, bf16[512,128]{1,0:T(8,128)(2,1)S(1)} %get-tuple-element.16.chip_q), custom_call_target="tpu_custom_call" | custom-call | flops 10000000000 | tf_op jit(solution)/shard_map/direct_local/pallas_call | solution.py:385
  15.4 0.0 collective-permute-done.6.refs_0_
  15.5 0.1 collective-permute-start.7
  15.5 0.0 collective-permute-done.8.refs_2_
  15.5 0.5 %collective-permute-start.9 = (s16[528,128]{1,0:T(8,128)(2,1)S(1)}, s16[528,128]{1,0:T(8,128)(2,1)S(1)}, u32[]{:S(2)}, u32[]{:S(2)}) collective-permute-start(s16[528,128]{1,0:T(8,128)(2,1)S(1)} %collective-permute-done.8.refs_2_), channel_id=1, source_target_pairs={{0,1},{1,0},{2,3},{3,2},{4,5},{5,4},{6,7},{7,6},{8,9},{9,8},{10,11... | collective-permute-start | bytes 405512 | tf_op jit(solution)/shard_map/ppermute | solution.py:315
  16.0 2.6 %collective-permute-done.10.refs_4_ = s16[528,128]{1,0:T(8,128)(2,1)S(1)} collective-permute-done((s16[528,128]{1,0:T(8,128)(2,1)S(1)}, s16[528,128]{1,0:T(8,128)(2,1)S(1)}, u32[]{:S(2)}, u32[]{:S(2)}) %collective-permute-start.10) | collective-permute-done | bytes 135200 | tf_op jit(solution)/shard_map/ppermute | solution.py:379
  18.7 0.5 %collective-permute-start.11 = (s16[528,128]{1,0:T(8,128)(2,1)S(1)}, s16[528,128]{1,0:T(8,128)(2,1)S(1)}, u32[]{:S(2)}, u32[]{:S(2)}) collective-permute-start(s16[528,128]{1,0:T(8,128)(2,1)S(1)} %collective-permute-done.10.refs_4_), channel_id=1, source_target_pairs={{0,1},{1,0},{2,3},{3,2},{4,5},{5,4},{6,7},{7,6},{8,9},{9,8},{10,11... | collective-permute-start | bytes 405512 | tf_op jit(solution)/shard_map/ppermute | solution.py:315
  19.1 0.0 collective-permute-done.5.refs_1_
  19.1 0.3 %gather_first.1 = (f32[256,128]{1,0:T(8,128)S(1)}, f32[256,128]{1,0:T(8,128)S(1)}) custom-call(bf16[32,256,128]{2,1,0:T(8,128)(2,1)S(1)} %get-tuple-element.17.rows_panels, f32[256,128]{1,0:T(8,128)S(1)} %get-tuple-element.18.direct, f32[256,128]{1,0:T(8,128)S(1)} %get-tuple-element.20.mirror, s16[528,128]{1,0:T(8,128)(2,1)S(1)} %collective-permute-done.4.refs_0_, ...), custom_call_target="tpu_custom_call" | custom-call | flops 10000000000 | tf_op jit(solution)/shard_map/gather_first/pallas_call | solution.py:400
  19.5 0.0 collective-permute-done.7.refs_1_
  19.5 0.0 collective-permute-done.9.refs_3_
  19.5 0.6 %gather_most.1.base = f32[256,128]{1,0:T(8,128)S(1)} custom-call(bf16[32,256,128]{2,1,0:T(8,128)(2,1)S(1)} %get-tuple-element.17.rows_panels, f32[256,128]{1,0:T(8,128)S(1)} %get-tuple-element.22.direct, f32[256,128]{1,0:T(8,128)S(1)} %get-tuple-element.23.mirror, s16[528,128]{1,0:T(8,128)(2,1)S(1)} %collective-permute-done.6.refs_0_, ...), custom_call_target="tpu_custom_call" | custom-call | flops 10000000000 | tf_op jit(solution)/shard_map/gather_most/pallas_call | solution.py:400
  20.1 0.1 collective-permute-done.11.message
  20.1 0.9 %gather_last.1 = f32[256,128]{1,0:T(8,128)} custom-call(bf16[32,256,128]{2,1,0:T(8,128)(2,1)S(1)} %get-tuple-element.17.rows_panels, f32[256,128]{1,0:T(8,128)S(1)} %gather_most.1.base, s16[528,128]{1,0:T(8,128)(2,1)S(1)} %collective-permute-done.11.message), custom_call_target="tpu_custom_call" | custom-call | tf_op jit(solution)/shard_map/gather_last/pallas_call | solution.py:427
  (1 shorter events, 0.0 us)
Async XLA Ops:
  0.0 2.5 %copy-start = (bf16[256,128]{1,0:T(8,128)(2,1)S(1)}, bf16[256,128]{1,0:T(8,128)(2,1)}, u32[]{:S(2)}) copy-start(bf16[256,128]{1,0:T(8,128)(2,1)} %own_q.1) | copy-start | bytes 196612
  0.0 2.5 %collective-permute-start.2 = (bf16[18,128,128]{2,1,0:T(8,128)(2,1)}, bf16[18,128,128]{2,1,0:T(8,128)(2,1)S(1)}, u32[]{:S(2)}, u32[]{:S(2)}) collective-permute-start(bf16[18,128,128]{2,1,0:T(8,128)(2,1)} %tiles_ref.3), channel_id=1, source_target_pairs={{0,1},{1,0},{2,3},{3,2},{4,5},{5,4},{6,7},{7,6},{8,9},{9,8},{10,11... | collective-permute-start | bytes 1769480 | tf_op jit(solution)/shard_map/ppermute | solution.py:315
  0.5 2.1 %collective-permute-start.3 = (bf16[256,128]{1,0:T(8,128)(2,1)}, bf16[256,128]{1,0:T(8,128)(2,1)S(1)}, u32[]{:S(2)}, u32[]{:S(2)}) collective-permute-start(bf16[256,128]{1,0:T(8,128)(2,1)} %own_q.1), channel_id=1, source_target_pairs={{0,1},{1,0},{2,3},{3,2},{4,5},{5,4},{6,7},{7,6},{8,9},{9,8},{10,11... | collective-permute-start | bytes 196616 | tf_op jit(solution)/shard_map/ppermute | solution.py:315
  0.5 2.0 %collective-permute-start.1 = (s32[2]{0:T(128)}, s32[2]{0:T(128)S(1)}, u32[]{:S(2)}, u32[]{:S(2)}) collective-permute-start(s32[2]{0:T(128)} %count_ref.3), channel_id=1, source_target_pairs={{0,1},{1,0},{2,3},{3,2},{4,5},{5,4},{6,7},{7,6},{8,9},{9,8},{10,11... | collective-permute-start | bytes 32 | tf_op jit(solution)/shard_map/ppermute | solution.py:315
  1.0 1.5 %collective-permute-start = (s32[2,18]{1,0:T(2,128)}, s32[2,18]{1,0:T(2,128)S(1)}, u32[]{:S(2)}, u32[]{:S(2)}) collective-permute-start(s32[2,18]{1,0:T(2,128)} %bitcast.1), channel_id=1, source_target_pairs={{0,1},{1,0},{2,3},{3,2},{4,5},{5,4},{6,7},{7,6},{8,9},{9,8},{10,11... | collective-permute-start | bytes 440 | tf_op jit(solution)/shard_map/ppermute | solution.py:315
  3.7 7.2 %collective-permute-start.4 = (s16[528,128]{1,0:T(8,128)(2,1)S(1)}, s16[528,128]{1,0:T(8,128)(2,1)S(1)}, u32[]{:S(2)}, u32[]{:S(2)}) collective-permute-start(s16[528,128]{1,0:T(8,128)(2,1)S(1)} %get-tuple-element.21), channel_id=1, source_target_pairs={{0,8},{1,11},{2,10},{3,9},{4,12},{5,15},{6,14},{7,13},{8,0},{9,3},... | collective-permute-start | bytes 405512 | tf_op jit(solution)/shard_map/ppermute | solution.py:379
  7.1 8.3 %collective-permute-start.6 = (s16[528,128]{1,0:T(8,128)(2,1)S(1)}, s16[528,128]{1,0:T(8,128)(2,1)S(1)}, u32[]{:S(2)}, u32[]{:S(2)}) collective-permute-start(s16[528,128]{1,0:T(8,128)(2,1)S(1)} %get-tuple-element.24), channel_id=1, source_target_pairs={{0,4},{1,7},{2,6},{3,5},{4,0},{5,3},{6,2},{7,1},{8,12},{9,15},{10,... | collective-permute-start | bytes 405512 | tf_op jit(solution)/shard_map/ppermute | solution.py:379
  8.7 6.8 %collective-permute-start.8 = (s16[528,128]{1,0:T(8,128)(2,1)S(1)}, s16[528,128]{1,0:T(8,128)(2,1)S(1)}, u32[]{:S(2)}, u32[]{:S(2)}) collective-permute-start(s16[528,128]{1,0:T(8,128)(2,1)S(1)} %get-tuple-element.25), channel_id=1, source_target_pairs={{1,3},{3,1},{5,7},{7,5},{9,11},{11,9},{13,15},{15,13},{17,19},{19,... | collective-permute-start | bytes 405512 | tf_op jit(solution)/shard_map/ppermute | solution.py:379
  9.4 9.3 %collective-permute-start.10 = (s16[528,128]{1,0:T(8,128)(2,1)S(1)}, s16[528,128]{1,0:T(8,128)(2,1)S(1)}, u32[]{:S(2)}, u32[]{:S(2)}) collective-permute-start(s16[528,128]{1,0:T(8,128)(2,1)S(1)} %get-tuple-element.26), channel_id=1, source_target_pairs={{0,12},{1,15},{2,14},{3,13},{4,8},{5,11},{6,10},{7,9},{8,4},{9,7},... | collective-permute-start | bytes 405512 | tf_op jit(solution)/shard_map/ppermute | solution.py:379
  10.9 8.3 %collective-permute-start.5 = (s16[528,128]{1,0:T(8,128)(2,1)S(1)}, s16[528,128]{1,0:T(8,128)(2,1)S(1)}, u32[]{:S(2)}, u32[]{:S(2)}) collective-permute-start(s16[528,128]{1,0:T(8,128)(2,1)S(1)} %collective-permute-done.4.refs_0_), channel_id=1, source_target_pairs={{0,1},{1,0},{2,3},{3,2},{4,5},{5,4},{6,7},{7,6},{8,9},{9,8},{10,11... | collective-permute-start | bytes 405512 | tf_op jit(solution)/shard_map/ppermute | solution.py:315
  15.5 4.0 %collective-permute-start.7 = (s16[528,128]{1,0:T(8,128)(2,1)S(1)}, s16[528,128]{1,0:T(8,128)(2,1)S(1)}, u32[]{:S(2)}, u32[]{:S(2)}) collective-permute-start(s16[528,128]{1,0:T(8,128)(2,1)S(1)} %collective-permute-done.6.refs_0_), channel_id=1, source_target_pairs={{0,1},{1,0},{2,3},{3,2},{4,5},{5,4},{6,7},{7,6},{8,9},{9,8},{10,11... | collective-permute-start | bytes 405512 | tf_op jit(solution)/shard_map/ppermute | solution.py:315
  15.5 3.9 %collective-permute-start.9 = (s16[528,128]{1,0:T(8,128)(2,1)S(1)}, s16[528,128]{1,0:T(8,128)(2,1)S(1)}, u32[]{:S(2)}, u32[]{:S(2)}) collective-permute-start(s16[528,128]{1,0:T(8,128)(2,1)S(1)} %collective-permute-done.8.refs_2_), channel_id=1, source_target_pairs={{0,1},{1,0},{2,3},{3,2},{4,5},{5,4},{6,7},{7,6},{8,9},{9,8},{10,11... | collective-permute-start | bytes 405512 | tf_op jit(solution)/shard_map/ppermute | solution.py:315
  18.7 1.5 %collective-permute-start.11 = (s16[528,128]{1,0:T(8,128)(2,1)S(1)}, s16[528,128]{1,0:T(8,128)(2,1)S(1)}, u32[]{:S(2)}, u32[]{:S(2)}) collective-permute-start(s16[528,128]{1,0:T(8,128)(2,1)S(1)} %collective-permute-done.10.refs_4_), channel_id=1, source_target_pairs={{0,1},{1,0},{2,3},{3,2},{4,5},{5,4},{6,7},{7,6},{8,9},{9,8},{10,11... | collective-permute-start | bytes 405512 | tf_op jit(solution)/shard_map/ppermute | solution.py:315

commit v9 on v8

--- a/solution.py
+++ b/solution.py
@@ -39,22 +39,23 @@
 def put_tiles(index, count, tiles, panels, chip_blocks):
     chip, core = place()
     tile = tiles.shape[1]
-    local = panels.shape[0] // chip_blocks - 1
-
-    def put(s, carry):
-        i, j = index[0, s], index[1, s]
-        cls = chip ^ (j // chip_blocks)
-
-        @pl.when((cls == 0) | (cls % 2 == core))
-        def _():
+    spare = panels.shape[0] - 1
+    local = spare // chip_blocks - 1
+    step = 2 if tiles.shape[0] % 2 == 0 else 1
+    live = live_tiles(count)
+
+    def put(n, carry):
+        for s in [n * step + e for e in range(step)]:
+            i, j = index[0, s], index[1, s]
+            cls = chip ^ (j // chip_blocks)
             slot = jnp.where(cls == 0, local, cls // 2)
-            panel = slot * chip_blocks + j % chip_blocks
+            wanted = (s < live) & ((cls == 0) | (cls % 2 == core))
+            panel = jnp.where(wanted, slot * chip_blocks + j % chip_blocks, spare)
             at = pl.multiple_of((i % (chip_blocks // 2)) * tile, tile)
             panels[panel, pl.ds(at, tile), :] = tiles[s]
-
         return carry
 
-    lax.fori_loop(0, live_tiles(count), put, 0)
+    lax.fori_loop(0, (live + step - 1) // step, put, 0)
 
 
 def fetch(sems, *pairs):
@@ -160,7 +161,7 @@
 
 def far_kernel(
     chips, k, index_ref, count_ref, tiles, own_q, other_q, own_panels,
-    chip_q, message, panels, index, count, sems,
+    chip_q, message, panels, sums, index, count, sems,
 ):
     rows, tile = own_q.shape[0], tiles.shape[1]
     chip_blocks = 2 * rows // tile
@@ -172,13 +173,16 @@
     def _():
         copies = fetch(sems, (index_ref, index), (count_ref, count))
         panels[...] = jnp.zeros_like(panels)
-        own_t, other_t = own_q[...].T, other_q[...].T
+        first = class_of(k, core, True, chips) // 2 * chip_blocks
+        mine = mirrored_blocks([(own_q[...].T, own_panels, first)], chip_blocks)
+        for b, m in enumerate(mine):
+            sums[b] = m
+        other_t = other_q[...].T
         for copy in copies:
             copy.wait()
         put_tiles(index, count, tiles, panels, chip_blocks)
-        first = k * chip_blocks
-        parts = [(own_t, own_panels, first), (other_t, panels, first)]
-        write_message(message, mirrored_blocks(parts, chip_blocks))
+        theirs = mirrored_blocks([(other_t, panels, first)], chip_blocks)
+        write_message(message, [sums[b] + m for b, m in enumerate(theirs)])
 
     @pl.when(jnp.logical_not(in_lower_half(chips)))
     def _():
@@ -206,13 +210,15 @@
 
         q = split(chip_q[...].astype(jnp.float32), tile)
         for k, message in zip(slots, messages, strict=True):
-            up = chip < (chip ^ (2 * k + core))
-            blocks = mirrored(k * chip_blocks, chip_blocks)
+            cls = class_of(k, core, in_lower_half(chips), chips)
+            up = chip < (chip ^ cls)
+            blocks = mirrored(cls // 2 * chip_blocks, chip_blocks)
             write_message(
                 message, [jnp.where(up, m, x) for m, x in zip(blocks, q, strict=True)]
             )
         half = chip_blocks // 2
-        local = mirrored(other_panels.shape[0] - chip_blocks + core * half, half)
+        last = other_panels.shape[0] - 1 - chip_blocks
+        local = mirrored(last + core * half, half)
         for b, m in enumerate(local):
             mirror[b * tile:(b + 1) * tile, :] = m
 
@@ -230,9 +236,19 @@
         write(panels)
 
 
-def is_low(k, mine):
+def class_of(k, core, from_lower, chips):
+    if k < chips // 4:
+        return 2 * k + core
+    other = chips // 2 + chips // 4 - 1 - k
+    if isinstance(core, int):
+        return 2 * (other if core and from_lower else k) + core
+    return 2 * jnp.where((core == 1) & from_lower, other, k) + core
+
+
+def is_low(chips, k, mine):
     chip, core = place()
-    cls = 2 * k + (core if mine else 1 - core)
+    carrier = core if mine else 1 - core
+    cls = class_of(k, carrier, jnp.logical_not(in_lower_half(chips)), chips)
     return (chip ^ cls) < chip, cls
 
 
@@ -245,11 +261,11 @@
     ]
 
 
-def gather_part(sources, rows_panels, direct, mirror, messages):
+def gather_part(chips, sources, rows_panels, direct, mirror, messages):
     total = direct[...]
     mirrored = split(mirror[...], rows_panels.shape[2])
     for (k, mine), message in zip(sources, messages, strict=True):
-        low, cls = is_low(k, mine)
+        low, cls = is_low(chips, k, mine)
         blocks = read_message(message)
         total = total + direct_sum(rows_panels, cls * len(blocks), blocks)
         mirrored = [
@@ -259,26 +275,26 @@
     return total, mirrored
 
 
-def gather_kernel(sources, rows_panels, direct, mirror, *refs):
+def gather_kernel(chips, sources, rows_panels, direct, mirror, *refs):
     *messages, direct_out, mirror_out = refs
     tile = rows_panels.shape[2]
-    total, mirrored = gather_part(sources, rows_panels, direct, mirror, messages)
+    total, mirrored = gather_part(chips, sources, rows_panels, direct, mirror, messages)
     direct_out[...] = total
     for b, m in enumerate(mirrored):
         mirror_out[b * tile:(b + 1) * tile, :] = m
 
 
-def join_kernel(sources, rows_panels, direct, mirror, *refs):
+def join_kernel(chips, sources, rows_panels, direct, mirror, *refs):
     *messages, base = refs
     tile = rows_panels.shape[2]
-    total, mirrored = gather_part(sources, rows_panels, direct, mirror, messages)
+    total, mirrored = gather_part(chips, sources, rows_panels, direct, mirror, messages)
     for b, (block, m) in enumerate(zip(split(total, tile), mirrored, strict=True)):
         base[b * tile:(b + 1) * tile, :] = block + m.T
 
 
-def final_kernel(k, factor, rows_panels, base, message, out, result, sem):
+def final_kernel(chips, k, factor, rows_panels, base, message, out, result, sem):
     tile = rows_panels.shape[2]
-    low, cls = is_low(k, False)
+    low, cls = is_low(chips, k, False)
 
     @pl.when(low)
     def _():
@@ -321,7 +337,7 @@
     other_count = swap(tile_count)
 
     panels_shape = jax.ShapeDtypeStruct(
-        ((slots + 1) * chip_blocks, rows, tile), jnp.bfloat16
+        ((slots + 1) * chip_blocks + 1, rows, tile), jnp.bfloat16
     )
     rows_panels_shape = jax.ShapeDtypeStruct(
         (chips * chip_blocks, rows, tile), jnp.bfloat16
@@ -361,7 +377,7 @@
         out_shape=[q_shape, message, panels_shape],
         in_specs=other_specs + [VMEM()] * 3,
         out_specs=[VMEM()] * 3,
-        scratch_shapes=other_scratch,
+        scratch_shapes=[pltpu.VMEM((chip_blocks, tile, columns), wide), *other_scratch],
         compiler_params=params,
         name="pack_far",
     )(*other, q_block, other_q, own_panels)
@@ -377,7 +393,9 @@
     messages = dict(zip(far[:1] + rest, [far_message, *rest_messages], strict=True))
     received = {
         k: lax.ppermute(messages[k], "row", [
-            (d, d ^ (2 * (2 * k + d % 2))) for d in range(devices) if 2 * k + d % 2
+            (d, d ^ (2 * cls))
+            for d in range(devices)
+            if (cls := class_of(k, d % 2, d < devices // 2, chips))
         ])
         for k in far[:1] + rest
     }
@@ -398,7 +416,7 @@
     def gather(kernel, sources, sums, name, outs, passed=()):
         sums = list(sums)
         return pl.pallas_call(
-            functools.partial(kernel, sources),
+            functools.partial(kernel, chips, sources),
             out_shape=[half_shape] * outs + [message] * len(passed),
             in_specs=[VMEM()] * (1 + len(sums) + len(sources) + len(passed)),
             out_specs=[VMEM()] * (outs + len(passed)),
@@ -425,7 +443,7 @@
         (direct, mirror), "gather_most", 1,
     )
     return pl.pallas_call(
-        functools.partial(final_kernel, last, 1.0 / math.sqrt(rows * devices)),
+        functools.partial(final_kernel, chips, last, 1.0 / math.sqrt(rows * devices)),
         out_shape=half_shape,
         in_specs=[VMEM()] * 3,
         out_specs=hbm,

time: 21.4 us -> 21.3 us (level)
  no operation moved by 1% of the time
where the time goes in v9:
time: 21.3 us; the launch traced here: 21 us
  starting transfers between devices  11.7 us (55%)
  Pallas kernels  6.33 us (30%)
  waiting for transfers between devices  2.79 us (13%)
    ppermute x4, starting transfers between devices, on_device(): lax.ppermute(messages[k], 'row', [(d, d ^ 2 * cls) for d in range(devices...  6.65 us
    ppermute x8, starting transfers between devices, swap(): return lax.ppermute(x, 'row', other_core)  5.08 us
    ppermute x4, waiting for transfers between devices, on_device(): lax.ppermute(messages[k], 'row', [(d, d ^ 2 * cls) for d in range(devices...  2.65 us
    pallas_call x1, Pallas kernels, on_device(): pl.pallas_call(direct_kernel, out_shape=[rows_panels_shape, half_shape],...  1.58 us
    pallas_call x1, Pallas kernels, on_device(): pl.pallas_call(own_kernel, out_shape=panels_shape, in_specs=[hbm] * 3, ou...  1.41 us
    pallas_call x1, Pallas kernels, on_device(): pl.pallas_call(functools.partial(far_kernel, chips, far[0]), out_shape=[q...  1.05 us
    pallas_call x1, Pallas kernels, on_device(): pl.pallas_call(functools.partial(final_kernel, chips, last, 1.0 / math.sq...  0.9 us
    pallas_call x2, Pallas kernels, gather(): pl.pallas_call(functools.partial(kernel, chips, sources), out_shape=[half...  0.87 us
  transfers between devices with their start and end apart: 12, of which 2 were waited for; matrix products, arithmetic and copies ran while one was open for 0% of the time, Pallas kernels for 21%

profile of v9, /device:TPU:0, one launch (start us, length us, event | category | flops | bytes accessed | tf_op | source)
XLA Modules:
  0.0 21.0 jit_solution(14768341823950757931)
XLA Ops:
  0.0 0.5 %collective-permute-start.2 = (bf16[18,128,128]{2,1,0:T(8,128)(2,1)}, bf16[18,128,128]{2,1,0:T(8,128)(2,1)S(1)}, u32[]{:S(2)}, u32[]{:S(2)}) collective-permute-start(bf16[18,128,128]{2,1,0:T(8,128)(2,1)} %tiles_ref.3), channel_id=1, source_target_pairs={{0,1},{1,0},{2,3},{3,2},{4,5},{5,4},{6,7},{7,6},{8,9},{9,8},{10,11... | collective-permute-start | bytes 1769480 | tf_op jit(solution)/shard_map/ppermute | solution.py:331
  0.5 0.1 collective-permute-start.3
  0.5 0.4 %collective-permute-start.1 = (s32[2]{0:T(128)}, s32[2]{0:T(128)S(1)}, u32[]{:S(2)}, u32[]{:S(2)}) collective-permute-start(s32[2]{0:T(128)} %count_ref.3), channel_id=1, source_target_pairs={{0,1},{1,0},{2,3},{3,2},{4,5},{5,4},{6,7},{7,6},{8,9},{9,8},{10,11... | collective-permute-start | bytes 32 | tf_op jit(solution)/shard_map/ppermute | solution.py:331
  1.0 0.1 collective-permute-start
  1.0 1.4 %own_tiles.1.own_panels = bf16[21,256,128]{2,1,0:T(8,128)(2,1)S(1)} custom-call(s32[2,18]{1,0:T(2,128)} %bitcast.2, s32[2]{0:T(128)} %count_ref.3, bf16[18,128,128]{2,1,0:T(8,128)(2,1)} %tiles_ref.3), custom_call_target="tpu_custom_call" | custom-call | tf_op jit(solution)/shard_map/own_tiles/pallas_call | solution.py:360
  2.4 0.0 collective-permute-done.1.count_ref
  2.5 0.0 collective-permute-done.index_ref
  2.5 0.0 collective-permute-done.3.other_q
  2.5 0.0 collective-permute-done.2.tiles
  2.5 0.0 copy-done
  2.5 1.0 %pack_far.1 = (bf16[512,128]{1,0:T(8,128)(2,1)S(1)}, s16[528,128]{1,0:T(8,128)(2,1)S(1)}, bf16[21,256,128]{2,1,0:T(8,128)(2,1)S(1)}) custom-call(s32[2,18]{1,0:T(2,128)S(1)} %collective-permute-done.index_ref, s32[2]{0:T(128)S(1)} %collective-permute-done.1.count_ref, bf16[18,128,128]{2,1,0:T(8,128)(2,1)S(1)} %collective-permute-done.2.tiles, ...), custom_call_target="tpu_custom_call" | custom-call | tf_op jit(solution)/shard_map/pack_far/pallas_call | solution.py:375
  3.6 3.0 %collective-permute-start.4 = (s16[528,128]{1,0:T(8,128)(2,1)S(1)}, s16[528,128]{1,0:T(8,128)(2,1)S(1)}, u32[]{:S(2)}, u32[]{:S(2)}) collective-permute-start(s16[528,128]{1,0:T(8,128)(2,1)S(1)} %get-tuple-element.21), channel_id=1, source_target_pairs={{0,8},{1,15},{2,10},{3,13},{4,12},{5,11},{6,14},{7,9},{8,0},{9,3},... | collective-permute-start | bytes 405512 | tf_op jit(solution)/shard_map/ppermute | solution.py:395
  6.6 0.5 %pack_near.1 = (s16[528,128]{1,0:T(8,128)(2,1)S(1)}, s16[528,128]{1,0:T(8,128)(2,1)S(1)}, s16[528,128]{1,0:T(8,128)(2,1)S(1)}, f32[256,128]{1,0:T(8,128)S(1)}) custom-call(s32[2,18]{1,0:T(2,128)S(1)} %collective-permute-done.index_ref, s32[2]{0:T(128)S(1)} %collective-permute-done.1.count_ref, bf16[18,128,128]{2,1,0:T(8,128)(2,1)S(1)} %collective-permute-done.2.tiles, ...), custom_call_target="tpu_custom_call" | custom-call | tf_op jit(solution)/shard_map/pack_near/pallas_call | solution.py:384
  7.1 1.6 %collective-permute-start.6 = (s16[528,128]{1,0:T(8,128)(2,1)S(1)}, s16[528,128]{1,0:T(8,128)(2,1)S(1)}, u32[]{:S(2)}, u32[]{:S(2)}) collective-permute-start(s16[528,128]{1,0:T(8,128)(2,1)S(1)} %get-tuple-element.24), channel_id=1, source_target_pairs={{0,4},{1,7},{2,6},{3,5},{4,0},{5,3},{6,2},{7,1},{8,12},{9,15},{10,... | collective-permute-start | bytes 405512 | tf_op jit(solution)/shard_map/ppermute | solution.py:395
  8.7 0.7 %collective-permute-start.8 = (s16[528,128]{1,0:T(8,128)(2,1)S(1)}, s16[528,128]{1,0:T(8,128)(2,1)S(1)}, u32[]{:S(2)}, u32[]{:S(2)}) collective-permute-start(s16[528,128]{1,0:T(8,128)(2,1)S(1)} %get-tuple-element.25), channel_id=1, source_target_pairs={{1,3},{3,1},{5,7},{7,5},{9,11},{11,9},{13,15},{15,13},{17,19},{19,... | collective-permute-start | bytes 405512 | tf_op jit(solution)/shard_map/ppermute | solution.py:395
  9.4 1.4 %collective-permute-start.10 = (s16[528,128]{1,0:T(8,128)(2,1)S(1)}, s16[528,128]{1,0:T(8,128)(2,1)S(1)}, u32[]{:S(2)}, u32[]{:S(2)}) collective-permute-start(s16[528,128]{1,0:T(8,128)(2,1)S(1)} %get-tuple-element.26), channel_id=1, source_target_pairs={{0,12},{1,11},{2,14},{3,9},{4,8},{5,15},{6,10},{7,13},{8,4},{9,7},... | collective-permute-start | bytes 405512 | tf_op jit(solution)/shard_map/ppermute | solution.py:395
  10.7 0.0 collective-permute-done.4.refs_0_
  10.8 3.2 %collective-permute-start.5 = (s16[528,128]{1,0:T(8,128)(2,1)S(1)}, s16[528,128]{1,0:T(8,128)(2,1)S(1)}, u32[]{:S(2)}, u32[]{:S(2)}) collective-permute-start(s16[528,128]{1,0:T(8,128)(2,1)S(1)} %collective-permute-done.4.refs_0_), channel_id=1, source_target_pairs={{0,1},{1,0},{2,3},{3,2},{4,5},{5,4},{6,7},{7,6},{8,9},{9,8},{10,11... | collective-permute-start | bytes 405512 | tf_op jit(solution)/shard_map/ppermute | solution.py:331
  13.9 1.6 %direct_local.1 = (bf16[32,256,128]{2,1,0:T(8,128)(2,1)S(1)}, f32[256,128]{1,0:T(8,128)S(1)}) custom-call(s32[2,18]{1,0:T(2,128)} %bitcast.3, s32[2]{0:T(128)} %count_ref.3, bf16[18,128,128]{2,1,0:T(8,128)(2,1)} %tiles_ref.3, bf16[512,128]{1,0:T(8,128)(2,1)S(1)} %get-tuple-element.16.chip_q), custom_call_target="tpu_custom_call" | custom-call | flops 10000000000 | tf_op jit(solution)/shard_map/direct_local/pallas_call | solution.py:403
  15.5 0.0 collective-permute-done.6.refs_0_
  15.5 0.3 %collective-permute-start.7 = (s16[528,128]{1,0:T(8,128)(2,1)S(1)}, s16[528,128]{1,0:T(8,128)(2,1)S(1)}, u32[]{:S(2)}, u32[]{:S(2)}) collective-permute-start(s16[528,128]{1,0:T(8,128)(2,1)S(1)} %collective-permute-done.6.refs_0_), channel_id=1, source_target_pairs={{0,1},{1,0},{2,3},{3,2},{4,5},{5,4},{6,7},{7,6},{8,9},{9,8},{10,11... | collective-permute-start | bytes 405512 | tf_op jit(solution)/shard_map/ppermute | solution.py:331
  15.8 0.0 collective-permute-done.8.refs_2_
  15.8 0.3 %collective-permute-start.9 = (s16[528,128]{1,0:T(8,128)(2,1)S(1)}, s16[528,128]{1,0:T(8,128)(2,1)S(1)}, u32[]{:S(2)}, u32[]{:S(2)}) collective-permute-start(s16[528,128]{1,0:T(8,128)(2,1)S(1)} %collective-permute-done.8.refs_2_), channel_id=1, source_target_pairs={{0,1},{1,0},{2,3},{3,2},{4,5},{5,4},{6,7},{7,6},{8,9},{9,8},{10,11... | collective-permute-start | bytes 405512 | tf_op jit(solution)/shard_map/ppermute | solution.py:331
  16.1 2.6 %collective-permute-done.10.refs_4_ = s16[528,128]{1,0:T(8,128)(2,1)S(1)} collective-permute-done((s16[528,128]{1,0:T(8,128)(2,1)S(1)}, s16[528,128]{1,0:T(8,128)(2,1)S(1)}, u32[]{:S(2)}, u32[]{:S(2)}) %collective-permute-start.10) | collective-permute-done | bytes 135200 | tf_op jit(solution)/shard_map/ppermute | solution.py:395
  18.7 0.3 %collective-permute-start.11 = (s16[528,128]{1,0:T(8,128)(2,1)S(1)}, s16[528,128]{1,0:T(8,128)(2,1)S(1)}, u32[]{:S(2)}, u32[]{:S(2)}) collective-permute-start(s16[528,128]{1,0:T(8,128)(2,1)S(1)} %collective-permute-done.10.refs_4_), channel_id=1, source_target_pairs={{0,1},{1,0},{2,3},{3,2},{4,5},{5,4},{6,7},{7,6},{8,9},{9,8},{10,11... | collective-permute-start | bytes 405512 | tf_op jit(solution)/shard_map/ppermute | solution.py:331
  19.0 0.0 collective-permute-done.5.refs_1_
  19.0 0.3 %gather_first.1 = (f32[256,128]{1,0:T(8,128)S(1)}, f32[256,128]{1,0:T(8,128)S(1)}) custom-call(bf16[32,256,128]{2,1,0:T(8,128)(2,1)S(1)} %get-tuple-element.17.rows_panels, f32[256,128]{1,0:T(8,128)S(1)} %get-tuple-element.18.direct, f32[256,128]{1,0:T(8,128)S(1)} %get-tuple-element.20.mirror, s16[528,128]{1,0:T(8,128)(2,1)S(1)} %collective-permute-done.4.refs_0_, ...), custom_call_target="tpu_custom_call" | custom-call | flops 10000000000 | tf_op jit(solution)/shard_map/gather_first/pallas_call | solution.py:418
  19.4 0.0 collective-permute-done.7.refs_1_
  19.4 0.0 collective-permute-done.9.refs_3_
  19.4 0.6 %gather_most.1.base = f32[256,128]{1,0:T(8,128)S(1)} custom-call(bf16[32,256,128]{2,1,0:T(8,128)(2,1)S(1)} %get-tuple-element.17.rows_panels, f32[256,128]{1,0:T(8,128)S(1)} %get-tuple-element.22.direct, f32[256,128]{1,0:T(8,128)S(1)} %get-tuple-element.23.mirror, s16[528,128]{1,0:T(8,128)(2,1)S(1)} %collective-permute-done.6.refs_0_, ...), custom_call_target="tpu_custom_call" | custom-call | flops 10000000000 | tf_op jit(solution)/shard_map/gather_most/pallas_call | solution.py:418
  19.9 0.1 collective-permute-done.11.message
  20.1 0.9 %gather_last.1 = f32[256,128]{1,0:T(8,128)} custom-call(bf16[32,256,128]{2,1,0:T(8,128)(2,1)S(1)} %get-tuple-element.17.rows_panels, f32[256,128]{1,0:T(8,128)S(1)} %gather_most.1.base, s16[528,128]{1,0:T(8,128)(2,1)S(1)} %collective-permute-done.11.message), custom_call_target="tpu_custom_call" | custom-call | tf_op jit(solution)/shard_map/gather_last/pallas_call | solution.py:445
  (1 shorter events, 0.0 us)
Async XLA Ops:
  0.0 2.5 %copy-start = (bf16[256,128]{1,0:T(8,128)(2,1)S(1)}, bf16[256,128]{1,0:T(8,128)(2,1)}, u32[]{:S(2)}) copy-start(bf16[256,128]{1,0:T(8,128)(2,1)} %own_q.1) | copy-start | bytes 196612
  0.0 2.5 %collective-permute-start.2 = (bf16[18,128,128]{2,1,0:T(8,128)(2,1)}, bf16[18,128,128]{2,1,0:T(8,128)(2,1)S(1)}, u32[]{:S(2)}, u32[]{:S(2)}) collective-permute-start(bf16[18,128,128]{2,1,0:T(8,128)(2,1)} %tiles_ref.3), channel_id=1, source_target_pairs={{0,1},{1,0},{2,3},{3,2},{4,5},{5,4},{6,7},{7,6},{8,9},{9,8},{10,11... | collective-permute-start | bytes 1769480 | tf_op jit(solution)/shard_map/ppermute | solution.py:331
  0.5 2.0 %collective-permute-start.3 = (bf16[256,128]{1,0:T(8,128)(2,1)}, bf16[256,128]{1,0:T(8,128)(2,1)S(1)}, u32[]{:S(2)}, u32[]{:S(2)}) collective-permute-start(bf16[256,128]{1,0:T(8,128)(2,1)} %own_q.1), channel_id=1, source_target_pairs={{0,1},{1,0},{2,3},{3,2},{4,5},{5,4},{6,7},{7,6},{8,9},{9,8},{10,11... | collective-permute-start | bytes 196616 | tf_op jit(solution)/shard_map/ppermute | solution.py:331
  0.5 1.9 %collective-permute-start.1 = (s32[2]{0:T(128)}, s32[2]{0:T(128)S(1)}, u32[]{:S(2)}, u32[]{:S(2)}) collective-permute-start(s32[2]{0:T(128)} %count_ref.3), channel_id=1, source_target_pairs={{0,1},{1,0},{2,3},{3,2},{4,5},{5,4},{6,7},{7,6},{8,9},{9,8},{10,11... | collective-permute-start | bytes 32 | tf_op jit(solution)/shard_map/ppermute | solution.py:331
  1.0 1.5 %collective-permute-start = (s32[2,18]{1,0:T(2,128)}, s32[2,18]{1,0:T(2,128)S(1)}, u32[]{:S(2)}, u32[]{:S(2)}) collective-permute-start(s32[2,18]{1,0:T(2,128)} %bitcast.1), channel_id=1, source_target_pairs={{0,1},{1,0},{2,3},{3,2},{4,5},{5,4},{6,7},{7,6},{8,9},{9,8},{10,11... | collective-permute-start | bytes 440 | tf_op jit(solution)/shard_map/ppermute | solution.py:331
  3.6 7.2 %collective-permute-start.4 = (s16[528,128]{1,0:T(8,128)(2,1)S(1)}, s16[528,128]{1,0:T(8,128)(2,1)S(1)}, u32[]{:S(2)}, u32[]{:S(2)}) collective-permute-start(s16[528,128]{1,0:T(8,128)(2,1)S(1)} %get-tuple-element.21), channel_id=1, source_target_pairs={{0,8},{1,15},{2,10},{3,13},{4,12},{5,11},{6,14},{7,9},{8,0},{9,3},... | collective-permute-start | bytes 405512 | tf_op jit(solution)/shard_map/ppermute | solution.py:395
  7.1 8.4 %collective-permute-start.6 = (s16[528,128]{1,0:T(8,128)(2,1)S(1)}, s16[528,128]{1,0:T(8,128)(2,1)S(1)}, u32[]{:S(2)}, u32[]{:S(2)}) collective-permute-start(s16[528,128]{1,0:T(8,128)(2,1)S(1)} %get-tuple-element.24), channel_id=1, source_target_pairs={{0,4},{1,7},{2,6},{3,5},{4,0},{5,3},{6,2},{7,1},{8,12},{9,15},{10,... | collective-permute-start | bytes 405512 | tf_op jit(solution)/shard_map/ppermute | solution.py:395
  8.7 7.0 %collective-permute-start.8 = (s16[528,128]{1,0:T(8,128)(2,1)S(1)}, s16[528,128]{1,0:T(8,128)(2,1)S(1)}, u32[]{:S(2)}, u32[]{:S(2)}) collective-permute-start(s16[528,128]{1,0:T(8,128)(2,1)S(1)} %get-tuple-element.25), channel_id=1, source_target_pairs={{1,3},{3,1},{5,7},{7,5},{9,11},{11,9},{13,15},{15,13},{17,19},{19,... | collective-permute-start | bytes 405512 | tf_op jit(solution)/shard_map/ppermute | solution.py:395
  9.4 9.3 %collective-permute-start.10 = (s16[528,128]{1,0:T(8,128)(2,1)S(1)}, s16[528,128]{1,0:T(8,128)(2,1)S(1)}, u32[]{:S(2)}, u32[]{:S(2)}) collective-permute-start(s16[528,128]{1,0:T(8,128)(2,1)S(1)} %get-tuple-element.26), channel_id=1, source_target_pairs={{0,12},{1,11},{2,14},{3,9},{4,8},{5,15},{6,10},{7,13},{8,4},{9,7},... | collective-permute-start | bytes 405512 | tf_op jit(solution)/shard_map/ppermute | solution.py:395
  10.8 8.3 %collective-permute-start.5 = (s16[528,128]{1,0:T(8,128)(2,1)S(1)}, s16[528,128]{1,0:T(8,128)(2,1)S(1)}, u32[]{:S(2)}, u32[]{:S(2)}) collective-permute-start(s16[528,128]{1,0:T(8,128)(2,1)S(1)} %collective-permute-done.4.refs_0_), channel_id=1, source_target_pairs={{0,1},{1,0},{2,3},{3,2},{4,5},{5,4},{6,7},{7,6},{8,9},{9,8},{10,11... | collective-permute-start | bytes 405512 | tf_op jit(solution)/shard_map/ppermute | solution.py:331
  15.5 3.9 %collective-permute-start.7 = (s16[528,128]{1,0:T(8,128)(2,1)S(1)}, s16[528,128]{1,0:T(8,128)(2,1)S(1)}, u32[]{:S(2)}, u32[]{:S(2)}) collective-permute-start(s16[528,128]{1,0:T(8,128)(2,1)S(1)} %collective-permute-done.6.refs_0_), channel_id=1, source_target_pairs={{0,1},{1,0},{2,3},{3,2},{4,5},{5,4},{6,7},{7,6},{8,9},{9,8},{10,11... | collective-permute-start | bytes 405512 | tf_op jit(solution)/shard_map/ppermute | solution.py:331
  15.8 3.6 %collective-permute-start.9 = (s16[528,128]{1,0:T(8,128)(2,1)S(1)}, s16[528,128]{1,0:T(8,128)(2,1)S(1)}, u32[]{:S(2)}, u32[]{:S(2)}) collective-permute-start(s16[528,128]{1,0:T(8,128)(2,1)S(1)} %collective-permute-done.8.refs_2_), channel_id=1, source_target_pairs={{0,1},{1,0},{2,3},{3,2},{4,5},{5,4},{6,7},{7,6},{8,9},{9,8},{10,11... | collective-permute-start | bytes 405512 | tf_op jit(solution)/shard_map/ppermute | solution.py:331
  18.7 1.4 %collective-permute-start.11 = (s16[528,128]{1,0:T(8,128)(2,1)S(1)}, s16[528,128]{1,0:T(8,128)(2,1)S(1)}, u32[]{:S(2)}, u32[]{:S(2)}) collective-permute-start(s16[528,128]{1,0:T(8,128)(2,1)S(1)} %collective-permute-done.10.refs_4_), channel_id=1, source_target_pairs={{0,1},{1,0},{2,3},{3,2},{4,5},{5,4},{6,7},{7,6},{8,9},{9,8},{10,11... | collective-permute-start | bytes 405512 | tf_op jit(solution)/shard_map/ppermute | solution.py:331

commit v10 on v9

--- a/solution.py
+++ b/solution.py
@@ -165,7 +165,7 @@
 ):
     rows, tile = own_q.shape[0], tiles.shape[1]
     chip_blocks = 2 * rows // tile
-    _, core = place()
+    chip, core = place()
     chip_q[pl.ds(pl.multiple_of(core * rows, rows), rows), :] = own_q[...]
     chip_q[pl.ds(pl.multiple_of((1 - core) * rows, rows), rows), :] = other_q[...]
 
@@ -173,7 +173,7 @@
     def _():
         copies = fetch(sems, (index_ref, index), (count_ref, count))
         panels[...] = jnp.zeros_like(panels)
-        first = class_of(k, core, True, chips) // 2 * chip_blocks
+        first = class_of(k, core, True, chip % 2, chips) // 2 * chip_blocks
         mine = mirrored_blocks([(own_q[...].T, own_panels, first)], chip_blocks)
         for b, m in enumerate(mine):
             sums[b] = m
@@ -210,7 +210,7 @@
 
         q = split(chip_q[...].astype(jnp.float32), tile)
         for k, message in zip(slots, messages, strict=True):
-            cls = class_of(k, core, in_lower_half(chips), chips)
+            cls = class_of(k, core, in_lower_half(chips), chip % 2, chips)
             up = chip < (chip ^ cls)
             blocks = mirrored(cls // 2 * chip_blocks, chip_blocks)
             write_message(
@@ -236,19 +236,22 @@
         write(panels)
 
 
-def class_of(k, core, from_lower, chips):
+def class_of(k, core, from_lower, odd, chips):
     if k < chips // 4:
         return 2 * k + core
     other = chips // 2 + chips // 4 - 1 - k
     if isinstance(core, int):
-        return 2 * (other if core and from_lower else k) + core
-    return 2 * jnp.where((core == 1) & from_lower, other, k) + core
+        turned = not odd if from_lower else odd and core == 0
+        return 2 * (other if turned else k) + core
+    turned = jnp.where(from_lower, odd == 0, (odd == 1) & (core == 0))
+    return 2 * jnp.where(turned, other, k) + core
 
 
 def is_low(chips, k, mine):
     chip, core = place()
     carrier = core if mine else 1 - core
-    cls = class_of(k, carrier, jnp.logical_not(in_lower_half(chips)), chips)
+    odd = (chip + carrier) % 2
+    cls = class_of(k, carrier, jnp.logical_not(in_lower_half(chips)), odd, chips)
     return (chip ^ cls) < chip, cls
 
 
@@ -395,7 +398,7 @@
         k: lax.ppermute(messages[k], "row", [
             (d, d ^ (2 * cls))
             for d in range(devices)
-            if (cls := class_of(k, d % 2, d < devices // 2, chips))
+            if (cls := class_of(k, d % 2, d < devices // 2, d // 2 % 2, chips))
         ])
         for k in far[:1] + rest
     }

time: 21.3 us -> 21.2 us (level)
  starting transfers between devices: 11.7 us -> 13.5 us
  waiting for transfers between devices: 2.79 us -> 1.06 us
    ppermute x4, waiting for transfers between devices: 2.65 us -> 0.95 us  [on_device(): lax.ppermute(messages[k], 'row', [(d, d ^ 2 * cls) for d in range(devices...]
    ppermute x8, starting transfers between devices: 5.08 us -> 6.19 us  [swap(): return lax.ppermute(x, 'row', other_core)]
    ppermute x4, starting transfers between devices: 6.65 us -> 7.26 us  [on_device(): lax.ppermute(messages[k], 'row', [(d, d ^ 2 * cls) for d in range(devices...]
  transfers between devices with their start and end apart: 12 -> 12, of which waited for: 2 -> 3; matrix products, arithmetic and copies ran while one was open for 0% -> 0% of each run, Pallas kernels for 21% -> 21%
where the time goes in v10:
time: 21.2 us; the launch traced here: 20.9 us
  starting transfers between devices  13.5 us (64%)
  Pallas kernels  6.29 us (30%)
  waiting for transfers between devices  1.06 us (5%)
    ppermute x4, starting transfers between devices, on_device(): lax.ppermute(messages[k], 'row', [(d, d ^ 2 * cls) for d in range(devices...  7.26 us
    ppermute x8, starting transfers between devices, swap(): return lax.ppermute(x, 'row', other_core)  6.19 us
    pallas_call x1, Pallas kernels, on_device(): pl.pallas_call(direct_kernel, out_shape=[rows_panels_shape, half_shape],...  1.58 us
    pallas_call x1, Pallas kernels, on_device(): pl.pallas_call(own_kernel, out_shape=panels_shape, in_specs=[hbm] * 3, ou...  1.41 us
    pallas_call x1, Pallas kernels, on_device(): pl.pallas_call(functools.partial(far_kernel, chips, far[0]), out_shape=[q...  1 us
    ppermute x4, waiting for transfers between devices, on_device(): lax.ppermute(messages[k], 'row', [(d, d ^ 2 * cls) for d in range(devices...  0.95 us
    pallas_call x1, Pallas kernels, on_device(): pl.pallas_call(functools.partial(final_kernel, chips, last, 1.0 / math.sq...  0.9 us
    pallas_call x2, Pallas kernels, gather(): pl.pallas_call(functools.partial(kernel, chips, sources), out_shape=[half...  0.87 us
  transfers between devices with their start and end apart: 12, of which 3 were waited for; matrix products, arithmetic and copies ran while one was open for 0% of the time, Pallas kernels for 21%

profile of v10, /device:TPU:0, one launch (start us, length us, event | category | flops | bytes accessed | tf_op | source)
XLA Modules:
  0.0 20.9 jit_solution(16474215543894814839)
XLA Ops:
  0.0 0.5 %collective-permute-start.2 = (bf16[18,128,128]{2,1,0:T(8,128)(2,1)}, bf16[18,128,128]{2,1,0:T(8,128)(2,1)S(1)}, u32[]{:S(2)}, u32[]{:S(2)}) collective-permute-start(bf16[18,128,128]{2,1,0:T(8,128)(2,1)} %tiles_ref.3), channel_id=1, source_target_pairs={{0,1},{1,0},{2,3},{3,2},{4,5},{5,4},{6,7},{7,6},{8,9},{9,8},{10,11... | collective-permute-start | bytes 1769480 | tf_op jit(solution)/shard_map/ppermute | solution.py:334
  0.5 0.1 collective-permute-start.3
  0.5 0.4 %collective-permute-start.1 = (s32[2]{0:T(128)}, s32[2]{0:T(128)S(1)}, u32[]{:S(2)}, u32[]{:S(2)}) collective-permute-start(s32[2]{0:T(128)} %count_ref.3), channel_id=1, source_target_pairs={{0,1},{1,0},{2,3},{3,2},{4,5},{5,4},{6,7},{7,6},{8,9},{9,8},{10,11... | collective-permute-start | bytes 32 | tf_op jit(solution)/shard_map/ppermute | solution.py:334
  1.0 0.1 collective-permute-start
  1.0 1.4 %own_tiles.1.own_panels = bf16[21,256,128]{2,1,0:T(8,128)(2,1)S(1)} custom-call(s32[2,18]{1,0:T(2,128)} %bitcast.2, s32[2]{0:T(128)} %count_ref.3, bf16[18,128,128]{2,1,0:T(8,128)(2,1)} %tiles_ref.3), custom_call_target="tpu_custom_call" | custom-call | tf_op jit(solution)/shard_map/own_tiles/pallas_call | solution.py:363
  2.4 0.0 collective-permute-done.1.count_ref
  2.5 0.0 collective-permute-done.index_ref
  2.5 0.0 collective-permute-done.3.other_q
  2.5 0.0 collective-permute-done.2.tiles
  2.5 0.0 copy-done
  2.5 1.0 %pack_far.1 = (bf16[512,128]{1,0:T(8,128)(2,1)S(1)}, s16[528,128]{1,0:T(8,128)(2,1)S(1)}, bf16[21,256,128]{2,1,0:T(8,128)(2,1)S(1)}) custom-call(s32[2,18]{1,0:T(2,128)S(1)} %collective-permute-done.index_ref, s32[2]{0:T(128)S(1)} %collective-permute-done.1.count_ref, bf16[18,128,128]{2,1,0:T(8,128)(2,1)S(1)} %collective-permute-done.2.tiles, ...), custom_call_target="tpu_custom_call" | custom-call | tf_op jit(solution)/shard_map/pack_far/pallas_call | solution.py:378
  3.5 4.1 %collective-permute-start.4 = (s16[528,128]{1,0:T(8,128)(2,1)S(1)}, s16[528,128]{1,0:T(8,128)(2,1)S(1)}, u32[]{:S(2)}, u32[]{:S(2)}) collective-permute-start(s16[528,128]{1,0:T(8,128)(2,1)S(1)} %get-tuple-element.21), channel_id=1, source_target_pairs={{0,12},{1,15},{2,10},{3,9},{4,8},{5,11},{6,14},{7,13},{8,0},{9,3},... | collective-permute-start | bytes 405512 | tf_op jit(solution)/shard_map/ppermute | solution.py:398
  7.6 0.5 %pack_near.1 = (s16[528,128]{1,0:T(8,128)(2,1)S(1)}, s16[528,128]{1,0:T(8,128)(2,1)S(1)}, s16[528,128]{1,0:T(8,128)(2,1)S(1)}, f32[256,128]{1,0:T(8,128)S(1)}) custom-call(s32[2,18]{1,0:T(2,128)S(1)} %collective-permute-done.index_ref, s32[2]{0:T(128)S(1)} %collective-permute-done.1.count_ref, bf16[18,128,128]{2,1,0:T(8,128)(2,1)S(1)} %collective-permute-done.2.tiles, ...), custom_call_target="tpu_custom_call" | custom-call | tf_op jit(solution)/shard_map/pack_near/pallas_call | solution.py:387
  8.1 0.1 collective-permute-start.6
  8.2 0.7 %collective-permute-start.8 = (s16[528,128]{1,0:T(8,128)(2,1)S(1)}, s16[528,128]{1,0:T(8,128)(2,1)S(1)}, u32[]{:S(2)}, u32[]{:S(2)}) collective-permute-start(s16[528,128]{1,0:T(8,128)(2,1)S(1)} %get-tuple-element.25), channel_id=1, source_target_pairs={{1,3},{3,1},{5,7},{7,5},{9,11},{11,9},{13,15},{15,13},{17,19},{19,... | collective-permute-start | bytes 405512 | tf_op jit(solution)/shard_map/ppermute | solution.py:398
  8.9 2.5 %collective-permute-start.10 = (s16[528,128]{1,0:T(8,128)(2,1)S(1)}, s16[528,128]{1,0:T(8,128)(2,1)S(1)}, u32[]{:S(2)}, u32[]{:S(2)}) collective-permute-start(s16[528,128]{1,0:T(8,128)(2,1)S(1)} %get-tuple-element.26), channel_id=1, source_target_pairs={{0,8},{1,11},{2,14},{3,13},{4,12},{5,15},{6,10},{7,9},{8,4},{9,7},... | collective-permute-start | bytes 405512 | tf_op jit(solution)/shard_map/ppermute | solution.py:398
  11.3 0.1 collective-permute-done.4.refs_0_
  11.5 2.4 %collective-permute-start.5 = (s16[528,128]{1,0:T(8,128)(2,1)S(1)}, s16[528,128]{1,0:T(8,128)(2,1)S(1)}, u32[]{:S(2)}, u32[]{:S(2)}) collective-permute-start(s16[528,128]{1,0:T(8,128)(2,1)S(1)} %collective-permute-done.4.refs_0_), channel_id=1, source_target_pairs={{0,1},{1,0},{2,3},{3,2},{4,5},{5,4},{6,7},{7,6},{8,9},{9,8},{10,11... | collective-permute-start | bytes 405512 | tf_op jit(solution)/shard_map/ppermute | solution.py:334
  13.9 1.6 %direct_local.1 = (bf16[32,256,128]{2,1,0:T(8,128)(2,1)S(1)}, f32[256,128]{1,0:T(8,128)S(1)}) custom-call(s32[2,18]{1,0:T(2,128)} %bitcast.3, s32[2]{0:T(128)} %count_ref.3, bf16[18,128,128]{2,1,0:T(8,128)(2,1)} %tiles_ref.3, bf16[512,128]{1,0:T(8,128)(2,1)S(1)} %get-tuple-element.16.chip_q), custom_call_target="tpu_custom_call" | custom-call | flops 10000000000 | tf_op jit(solution)/shard_map/direct_local/pallas_call | solution.py:406
  15.5 0.0 collective-permute-done.6.refs_0_
  15.5 2.3 %collective-permute-start.7 = (s16[528,128]{1,0:T(8,128)(2,1)S(1)}, s16[528,128]{1,0:T(8,128)(2,1)S(1)}, u32[]{:S(2)}, u32[]{:S(2)}) collective-permute-start(s16[528,128]{1,0:T(8,128)(2,1)S(1)} %collective-permute-done.6.refs_0_), channel_id=1, source_target_pairs={{0,1},{1,0},{2,3},{3,2},{4,5},{5,4},{6,7},{7,6},{8,9},{9,8},{10,11... | collective-permute-start | bytes 405512 | tf_op jit(solution)/shard_map/ppermute | solution.py:334
  17.8 0.0 collective-permute-done.8.refs_2_
  17.8 0.0 collective-permute-start.9
  17.8 0.8 %collective-permute-done.10.refs_4_ = s16[528,128]{1,0:T(8,128)(2,1)S(1)} collective-permute-done((s16[528,128]{1,0:T(8,128)(2,1)S(1)}, s16[528,128]{1,0:T(8,128)(2,1)S(1)}, u32[]{:S(2)}, u32[]{:S(2)}) %collective-permute-start.10) | collective-permute-done | bytes 135200 | tf_op jit(solution)/shard_map/ppermute | solution.py:398
  18.6 0.4 %collective-permute-start.11 = (s16[528,128]{1,0:T(8,128)(2,1)S(1)}, s16[528,128]{1,0:T(8,128)(2,1)S(1)}, u32[]{:S(2)}, u32[]{:S(2)}) collective-permute-start(s16[528,128]{1,0:T(8,128)(2,1)S(1)} %collective-permute-done.10.refs_4_), channel_id=1, source_target_pairs={{0,1},{1,0},{2,3},{3,2},{4,5},{5,4},{6,7},{7,6},{8,9},{9,8},{10,11... | collective-permute-start | bytes 405512 | tf_op jit(solution)/shard_map/ppermute | solution.py:334
  19.0 0.0 collective-permute-done.5.refs_1_
  19.0 0.3 %gather_first.1 = (f32[256,128]{1,0:T(8,128)S(1)}, f32[256,128]{1,0:T(8,128)S(1)}) custom-call(bf16[32,256,128]{2,1,0:T(8,128)(2,1)S(1)} %get-tuple-element.17.rows_panels, f32[256,128]{1,0:T(8,128)S(1)} %get-tuple-element.18.direct, f32[256,128]{1,0:T(8,128)S(1)} %get-tuple-element.20.mirror, s16[528,128]{1,0:T(8,128)(2,1)S(1)} %collective-permute-done.4.refs_0_, ...), custom_call_target="tpu_custom_call" | custom-call | flops 10000000000 | tf_op jit(solution)/shard_map/gather_first/pallas_call | solution.py:421
  19.4 0.0 collective-permute-done.7.refs_1_
  19.4 0.0 collective-permute-done.9.refs_3_
  19.4 0.6 %gather_most.1.base = f32[256,128]{1,0:T(8,128)S(1)} custom-call(bf16[32,256,128]{2,1,0:T(8,128)(2,1)S(1)} %get-tuple-element.17.rows_panels, f32[256,128]{1,0:T(8,128)S(1)} %get-tuple-element.22.direct, f32[256,128]{1,0:T(8,128)S(1)} %get-tuple-element.23.mirror, s16[528,128]{1,0:T(8,128)(2,1)S(1)} %collective-permute-done.6.refs_0_, ...), custom_call_target="tpu_custom_call" | custom-call | flops 10000000000 | tf_op jit(solution)/shard_map/gather_most/pallas_call | solution.py:421
  20.0 0.1 collective-permute-done.11.message
  20.0 0.9 %gather_last.1 = f32[256,128]{1,0:T(8,128)} custom-call(bf16[32,256,128]{2,1,0:T(8,128)(2,1)S(1)} %get-tuple-element.17.rows_panels, f32[256,128]{1,0:T(8,128)S(1)} %gather_most.1.base, s16[528,128]{1,0:T(8,128)(2,1)S(1)} %collective-permute-done.11.message), custom_call_target="tpu_custom_call" | custom-call | tf_op jit(solution)/shard_map/gather_last/pallas_call | solution.py:448
  (1 shorter events, 0.0 us)
Async XLA Ops:
  0.0 2.5 %copy-start = (bf16[256,128]{1,0:T(8,128)(2,1)S(1)}, bf16[256,128]{1,0:T(8,128)(2,1)}, u32[]{:S(2)}) copy-start(bf16[256,128]{1,0:T(8,128)(2,1)} %own_q.1) | copy-start | bytes 196612
  0.0 2.5 %collective-permute-start.2 = (bf16[18,128,128]{2,1,0:T(8,128)(2,1)}, bf16[18,128,128]{2,1,0:T(8,128)(2,1)S(1)}, u32[]{:S(2)}, u32[]{:S(2)}) collective-permute-start(bf16[18,128,128]{2,1,0:T(8,128)(2,1)} %tiles_ref.3), channel_id=1, source_target_pairs={{0,1},{1,0},{2,3},{3,2},{4,5},{5,4},{6,7},{7,6},{8,9},{9,8},{10,11... | collective-permute-start | bytes 1769480 | tf_op jit(solution)/shard_map/ppermute | solution.py:334
  0.5 2.0 %collective-permute-start.3 = (bf16[256,128]{1,0:T(8,128)(2,1)}, bf16[256,128]{1,0:T(8,128)(2,1)S(1)}, u32[]{:S(2)}, u32[]{:S(2)}) collective-permute-start(bf16[256,128]{1,0:T(8,128)(2,1)} %own_q.1), channel_id=1, source_target_pairs={{0,1},{1,0},{2,3},{3,2},{4,5},{5,4},{6,7},{7,6},{8,9},{9,8},{10,11... | collective-permute-start | bytes 196616 | tf_op jit(solution)/shard_map/ppermute | solution.py:334
  0.5 1.9 %collective-permute-start.1 = (s32[2]{0:T(128)}, s32[2]{0:T(128)S(1)}, u32[]{:S(2)}, u32[]{:S(2)}) collective-permute-start(s32[2]{0:T(128)} %count_ref.3), channel_id=1, source_target_pairs={{0,1},{1,0},{2,3},{3,2},{4,5},{5,4},{6,7},{7,6},{8,9},{9,8},{10,11... | collective-permute-start | bytes 32 | tf_op jit(solution)/shard_map/ppermute | solution.py:334
  1.0 1.5 %collective-permute-start = (s32[2,18]{1,0:T(2,128)}, s32[2,18]{1,0:T(2,128)S(1)}, u32[]{:S(2)}, u32[]{:S(2)}) collective-permute-start(s32[2,18]{1,0:T(2,128)} %bitcast.1), channel_id=1, source_target_pairs={{0,1},{1,0},{2,3},{3,2},{4,5},{5,4},{6,7},{7,6},{8,9},{9,8},{10,11... | collective-permute-start | bytes 440 | tf_op jit(solution)/shard_map/ppermute | solution.py:334
  3.5 8.0 %collective-permute-start.4 = (s16[528,128]{1,0:T(8,128)(2,1)S(1)}, s16[528,128]{1,0:T(8,128)(2,1)S(1)}, u32[]{:S(2)}, u32[]{:S(2)}) collective-permute-start(s16[528,128]{1,0:T(8,128)(2,1)S(1)} %get-tuple-element.21), channel_id=1, source_target_pairs={{0,12},{1,15},{2,10},{3,9},{4,8},{5,11},{6,14},{7,13},{8,0},{9,3},... | collective-permute-start | bytes 405512 | tf_op jit(solution)/shard_map/ppermute | solution.py:398
  8.1 7.4 %collective-permute-start.6 = (s16[528,128]{1,0:T(8,128)(2,1)S(1)}, s16[528,128]{1,0:T(8,128)(2,1)S(1)}, u32[]{:S(2)}, u32[]{:S(2)}) collective-permute-start(s16[528,128]{1,0:T(8,128)(2,1)S(1)} %get-tuple-element.24), channel_id=1, source_target_pairs={{0,4},{1,7},{2,6},{3,5},{4,0},{5,3},{6,2},{7,1},{8,12},{9,15},{10,... | collective-permute-start | bytes 405512 | tf_op jit(solution)/shard_map/ppermute | solution.py:398
  8.2 9.6 %collective-permute-start.8 = (s16[528,128]{1,0:T(8,128)(2,1)S(1)}, s16[528,128]{1,0:T(8,128)(2,1)S(1)}, u32[]{:S(2)}, u32[]{:S(2)}) collective-permute-start(s16[528,128]{1,0:T(8,128)(2,1)S(1)} %get-tuple-element.25), channel_id=1, source_target_pairs={{1,3},{3,1},{5,7},{7,5},{9,11},{11,9},{13,15},{15,13},{17,19},{19,... | collective-permute-start | bytes 405512 | tf_op jit(solution)/shard_map/ppermute | solution.py:398
  8.9 9.7 %collective-permute-start.10 = (s16[528,128]{1,0:T(8,128)(2,1)S(1)}, s16[528,128]{1,0:T(8,128)(2,1)S(1)}, u32[]{:S(2)}, u32[]{:S(2)}) collective-permute-start(s16[528,128]{1,0:T(8,128)(2,1)S(1)} %get-tuple-element.26), channel_id=1, source_target_pairs={{0,8},{1,11},{2,14},{3,13},{4,12},{5,15},{6,10},{7,9},{8,4},{9,7},... | collective-permute-start | bytes 405512 | tf_op jit(solution)/shard_map/ppermute | solution.py:398
  11.5 7.6 %collective-permute-start.5 = (s16[528,128]{1,0:T(8,128)(2,1)S(1)}, s16[528,128]{1,0:T(8,128)(2,1)S(1)}, u32[]{:S(2)}, u32[]{:S(2)}) collective-permute-start(s16[528,128]{1,0:T(8,128)(2,1)S(1)} %collective-permute-done.4.refs_0_), channel_id=1, source_target_pairs={{0,1},{1,0},{2,3},{3,2},{4,5},{5,4},{6,7},{7,6},{8,9},{9,8},{10,11... | collective-permute-start | bytes 405512 | tf_op jit(solution)/shard_map/ppermute | solution.py:334
  15.5 3.9 %collective-permute-start.7 = (s16[528,128]{1,0:T(8,128)(2,1)S(1)}, s16[528,128]{1,0:T(8,128)(2,1)S(1)}, u32[]{:S(2)}, u32[]{:S(2)}) collective-permute-start(s16[528,128]{1,0:T(8,128)(2,1)S(1)} %collective-permute-done.6.refs_0_), channel_id=1, source_target_pairs={{0,1},{1,0},{2,3},{3,2},{4,5},{5,4},{6,7},{7,6},{8,9},{9,8},{10,11... | collective-permute-start | bytes 405512 | tf_op jit(solution)/shard_map/ppermute | solution.py:334
  17.8 1.6 %collective-permute-start.9 = (s16[528,128]{1,0:T(8,128)(2,1)S(1)}, s16[528,128]{1,0:T(8,128)(2,1)S(1)}, u32[]{:S(2)}, u32[]{:S(2)}) collective-permute-start(s16[528,128]{1,0:T(8,128)(2,1)S(1)} %collective-permute-done.8.refs_2_), channel_id=1, source_target_pairs={{0,1},{1,0},{2,3},{3,2},{4,5},{5,4},{6,7},{7,6},{8,9},{9,8},{10,11... | collective-permute-start | bytes 405512 | tf_op jit(solution)/shard_map/ppermute | solution.py:334
  18.6 1.4 %collective-permute-start.11 = (s16[528,128]{1,0:T(8,128)(2,1)S(1)}, s16[528,128]{1,0:T(8,128)(2,1)S(1)}, u32[]{:S(2)}, u32[]{:S(2)}) collective-permute-start(s16[528,128]{1,0:T(8,128)(2,1)S(1)} %collective-permute-done.10.refs_4_), channel_id=1, source_target_pairs={{0,1},{1,0},{2,3},{3,2},{4,5},{5,4},{6,7},{7,6},{8,9},{9,8},{10,11... | collective-permute-start | bytes 405512 | tf_op jit(solution)/shard_map/ppermute | solution.py:334

commit v11 on v10

--- a/solution.py
+++ b/solution.py
@@ -190,14 +190,15 @@
 
 
 def near_kernel(
-    chips, slots, index_ref, count_ref, tiles, own_panels, far_panels, chip_q, *refs
+    chips, slots, index_ref, count_ref, tiles, own_panels, far_panels, chip_q,
+    far_message, *refs
 ):
     *messages, mirror, panels, index, count, sems = refs
     rows, tile = own_panels.shape[1:]
     chip_blocks = 2 * rows // tile
     chip, core = place()
 
-    def write(other_panels):
+    def write(other_panels, upper):
         def transposed(at):
             return chip_q[pl.ds(pl.multiple_of(at * rows, rows), rows), :].T
 
@@ -210,6 +211,9 @@
 
         q = split(chip_q[...].astype(jnp.float32), tile)
         for k, message in zip(slots, messages, strict=True):
+            if upper and k >= chips // 4:
+                message[...] = far_message[...]
+                continue
             cls = class_of(k, core, in_lower_half(chips), chip % 2, chips)
             up = chip < (chip ^ cls)
             blocks = mirrored(cls // 2 * chip_blocks, chip_blocks)
@@ -224,7 +228,7 @@
 
     @pl.when(in_lower_half(chips))
     def _():
-        write(far_panels)
+        write(far_panels, False)
 
     @pl.when(jnp.logical_not(in_lower_half(chips)))
     def _():
@@ -233,7 +237,7 @@
         for copy in copies:
             copy.wait()
         put_tiles(index, count, tiles, panels, chip_blocks)
-        write(panels)
+        write(panels, True)
 
 
 def class_of(k, core, from_lower, odd, chips):
@@ -387,12 +391,12 @@
     *rest_messages, mirror = pl.pallas_call(
         functools.partial(near_kernel, chips, rest),
         out_shape=[message] * len(rest) + [half_shape],
-        in_specs=other_specs + [VMEM()] * 3,
+        in_specs=other_specs + [VMEM()] * 4,
         out_specs=[VMEM()] * (len(rest) + 1),
         scratch_shapes=[pltpu.VMEM(panels_shape.shape, jnp.bfloat16), *other_scratch],
         compiler_params=params,
         name="pack_near",
-    )(*other, own_panels, far_panels, chip_q)
+    )(*other, own_panels, far_panels, chip_q, far_message)
     messages = dict(zip(far[:1] + rest, [far_message, *rest_messages], strict=True))
     received = {
         k: lax.ppermute(messages[k], "row", [

time: 21.2 us -> 21.2 us (level)
  starting transfers between devices: 13.5 us -> 13.2 us
    ppermute x4, starting transfers between devices: 7.26 us -> 7.02 us  [on_device(): lax.ppermute(messages[k], 'row', [(d, d ^ 2 * cls) for d in range(devices...]
where the time goes in v11:
time: 21.2 us; the launch traced here: 20.9 us
  starting transfers between devices  13.2 us (62%)
  Pallas kernels  6.41 us (30%)
  waiting for transfers between devices  1.23 us (6%)
    ppermute x4, starting transfers between devices, on_device(): lax.ppermute(messages[k], 'row', [(d, d ^ 2 * cls) for d in range(devices...  7.02 us
    ppermute x8, starting transfers between devices, swap(): return lax.ppermute(x, 'row', other_core)  6.13 us
    pallas_call x1, Pallas kernels, on_device(): pl.pallas_call(direct_kernel, out_shape=[rows_panels_shape, half_shape],...  1.58 us
    pallas_call x1, Pallas kernels, on_device(): pl.pallas_call(own_kernel, out_shape=panels_shape, in_specs=[hbm] * 3, ou...  1.41 us
    ppermute x4, waiting for transfers between devices, on_device(): lax.ppermute(messages[k], 'row', [(d, d ^ 2 * cls) for d in range(devices...  1.13 us
    pallas_call x1, Pallas kernels, on_device(): pl.pallas_call(functools.partial(far_kernel, chips, far[0]), out_shape=[q...  1.13 us
    pallas_call x1, Pallas kernels, on_device(): pl.pallas_call(functools.partial(final_kernel, chips, last, 1.0 / math.sq...  0.9 us
    pallas_call x2, Pallas kernels, gather(): pl.pallas_call(functools.partial(kernel, chips, sources), out_shape=[half...  0.88 us
  transfers between devices with their start and end apart: 12, of which 3 were waited for; matrix products, arithmetic and copies ran while one was open for 0% of the time, Pallas kernels for 21%

profile of v11, /device:TPU:0, one launch (start us, length us, event | category | flops | bytes accessed | tf_op | source)
XLA Modules:
  0.0 20.9 jit_solution(8356408958040134281)
XLA Ops:
  0.0 0.5 %collective-permute-start.2 = (bf16[18,128,128]{2,1,0:T(8,128)(2,1)}, bf16[18,128,128]{2,1,0:T(8,128)(2,1)S(1)}, u32[]{:S(2)}, u32[]{:S(2)}) collective-permute-start(bf16[18,128,128]{2,1,0:T(8,128)(2,1)} %tiles_ref.3), channel_id=1, source_target_pairs={{0,1},{1,0},{2,3},{3,2},{4,5},{5,4},{6,7},{7,6},{8,9},{9,8},{10,11... | collective-permute-start | bytes 1769480 | tf_op jit(solution)/shard_map/ppermute | solution.py:338
  0.5 0.1 collective-permute-start.3
  0.5 0.4 %collective-permute-start.1 = (s32[2]{0:T(128)}, s32[2]{0:T(128)S(1)}, u32[]{:S(2)}, u32[]{:S(2)}) collective-permute-start(s32[2]{0:T(128)} %count_ref.3), channel_id=1, source_target_pairs={{0,1},{1,0},{2,3},{3,2},{4,5},{5,4},{6,7},{7,6},{8,9},{9,8},{10,11... | collective-permute-start | bytes 32 | tf_op jit(solution)/shard_map/ppermute | solution.py:338
  1.0 0.1 collective-permute-start
  1.0 1.4 %own_tiles.1.own_panels = bf16[21,256,128]{2,1,0:T(8,128)(2,1)S(1)} custom-call(s32[2,18]{1,0:T(2,128)} %bitcast.2, s32[2]{0:T(128)} %count_ref.3, bf16[18,128,128]{2,1,0:T(8,128)(2,1)} %tiles_ref.3), custom_call_target="tpu_custom_call" | custom-call | tf_op jit(solution)/shard_map/own_tiles/pallas_call | solution.py:367
  2.4 0.0 collective-permute-done.1.count_ref
  2.5 0.0 collective-permute-done.index_ref
  2.5 0.0 collective-permute-done.3.other_q
  2.5 0.0 collective-permute-done.2.tiles
  2.5 0.0 copy-done
  2.5 1.1 %pack_far.1 = (bf16[512,128]{1,0:T(8,128)(2,1)S(1)}, s16[528,128]{1,0:T(8,128)(2,1)S(1)}, bf16[21,256,128]{2,1,0:T(8,128)(2,1)S(1)}) custom-call(s32[2,18]{1,0:T(2,128)S(1)} %collective-permute-done.index_ref, s32[2]{0:T(128)S(1)} %collective-permute-done.1.count_ref, bf16[18,128,128]{2,1,0:T(8,128)(2,1)S(1)} %collective-permute-done.2.tiles, ...), custom_call_target="tpu_custom_call" | custom-call | tf_op jit(solution)/shard_map/pack_far/pallas_call | solution.py:382
  3.6 3.9 %collective-permute-start.4 = (s16[528,128]{1,0:T(8,128)(2,1)S(1)}, s16[528,128]{1,0:T(8,128)(2,1)S(1)}, u32[]{:S(2)}, u32[]{:S(2)}) collective-permute-start(s16[528,128]{1,0:T(8,128)(2,1)S(1)} %get-tuple-element.20.far_message), channel_id=1, source_target_pairs={{0,12},{1,15},{2,10},{3,9},{4,8},{5,11},{6,14},{7,13},{8,0},{9,3},... | collective-permute-start | bytes 405512 | tf_op jit(solution)/shard_map/ppermute | solution.py:402
  7.6 0.5 %pack_near.1 = (s16[528,128]{1,0:T(8,128)(2,1)S(1)}, s16[528,128]{1,0:T(8,128)(2,1)S(1)}, s16[528,128]{1,0:T(8,128)(2,1)S(1)}, f32[256,128]{1,0:T(8,128)S(1)}) custom-call(s32[2,18]{1,0:T(2,128)S(1)} %collective-permute-done.index_ref, s32[2]{0:T(128)S(1)} %collective-permute-done.1.count_ref, bf16[18,128,128]{2,1,0:T(8,128)(2,1)S(1)} %collective-permute-done.2.tiles, ...), custom_call_target="tpu_custom_call" | custom-call | tf_op jit(solution)/shard_map/pack_near/pallas_call | solution.py:391
  8.1 0.1 collective-permute-start.6
  8.2 0.7 %collective-permute-start.8 = (s16[528,128]{1,0:T(8,128)(2,1)S(1)}, s16[528,128]{1,0:T(8,128)(2,1)S(1)}, u32[]{:S(2)}, u32[]{:S(2)}) collective-permute-start(s16[528,128]{1,0:T(8,128)(2,1)S(1)} %get-tuple-element.25), channel_id=1, source_target_pairs={{1,3},{3,1},{5,7},{7,5},{9,11},{11,9},{13,15},{15,13},{17,19},{19,... | collective-permute-start | bytes 405512 | tf_op jit(solution)/shard_map/ppermute | solution.py:402
  8.9 2.4 %collective-permute-start.10 = (s16[528,128]{1,0:T(8,128)(2,1)S(1)}, s16[528,128]{1,0:T(8,128)(2,1)S(1)}, u32[]{:S(2)}, u32[]{:S(2)}) collective-permute-start(s16[528,128]{1,0:T(8,128)(2,1)S(1)} %get-tuple-element.26), channel_id=1, source_target_pairs={{0,8},{1,11},{2,14},{3,13},{4,12},{5,15},{6,10},{7,9},{8,4},{9,7},... | collective-permute-start | bytes 405512 | tf_op jit(solution)/shard_map/ppermute | solution.py:402
  11.2 0.3 %collective-permute-done.4.refs_0_ = s16[528,128]{1,0:T(8,128)(2,1)S(1)} collective-permute-done((s16[528,128]{1,0:T(8,128)(2,1)S(1)}, s16[528,128]{1,0:T(8,128)(2,1)S(1)}, u32[]{:S(2)}, u32[]{:S(2)}) %collective-permute-start.4) | collective-permute-done | bytes 135200 | tf_op jit(solution)/shard_map/ppermute | solution.py:402
  11.5 2.4 %collective-permute-start.5 = (s16[528,128]{1,0:T(8,128)(2,1)S(1)}, s16[528,128]{1,0:T(8,128)(2,1)S(1)}, u32[]{:S(2)}, u32[]{:S(2)}) collective-permute-start(s16[528,128]{1,0:T(8,128)(2,1)S(1)} %collective-permute-done.4.refs_0_), channel_id=1, source_target_pairs={{0,1},{1,0},{2,3},{3,2},{4,5},{5,4},{6,7},{7,6},{8,9},{9,8},{10,11... | collective-permute-start | bytes 405512 | tf_op jit(solution)/shard_map/ppermute | solution.py:338
  13.8 1.6 %direct_local.1 = (bf16[32,256,128]{2,1,0:T(8,128)(2,1)S(1)}, f32[256,128]{1,0:T(8,128)S(1)}) custom-call(s32[2,18]{1,0:T(2,128)} %bitcast.3, s32[2]{0:T(128)} %count_ref.3, bf16[18,128,128]{2,1,0:T(8,128)(2,1)} %tiles_ref.3, bf16[512,128]{1,0:T(8,128)(2,1)S(1)} %get-tuple-element.16.chip_q), custom_call_target="tpu_custom_call" | custom-call | flops 10000000000 | tf_op jit(solution)/shard_map/direct_local/pallas_call | solution.py:410
  15.4 0.0 collective-permute-done.6.refs_0_
  15.4 2.2 %collective-permute-start.7 = (s16[528,128]{1,0:T(8,128)(2,1)S(1)}, s16[528,128]{1,0:T(8,128)(2,1)S(1)}, u32[]{:S(2)}, u32[]{:S(2)}) collective-permute-start(s16[528,128]{1,0:T(8,128)(2,1)S(1)} %collective-permute-done.6.refs_0_), channel_id=1, source_target_pairs={{0,1},{1,0},{2,3},{3,2},{4,5},{5,4},{6,7},{7,6},{8,9},{9,8},{10,11... | collective-permute-start | bytes 405512 | tf_op jit(solution)/shard_map/ppermute | solution.py:338
  17.6 0.0 collective-permute-done.8.refs_2_
  17.6 0.0 collective-permute-start.9
  17.7 0.9 %collective-permute-done.10.refs_4_ = s16[528,128]{1,0:T(8,128)(2,1)S(1)} collective-permute-done((s16[528,128]{1,0:T(8,128)(2,1)S(1)}, s16[528,128]{1,0:T(8,128)(2,1)S(1)}, u32[]{:S(2)}, u32[]{:S(2)}) %collective-permute-start.10) | collective-permute-done | bytes 135200 | tf_op jit(solution)/shard_map/ppermute | solution.py:402
  18.5 0.5 %collective-permute-start.11 = (s16[528,128]{1,0:T(8,128)(2,1)S(1)}, s16[528,128]{1,0:T(8,128)(2,1)S(1)}, u32[]{:S(2)}, u32[]{:S(2)}) collective-permute-start(s16[528,128]{1,0:T(8,128)(2,1)S(1)} %collective-permute-done.10.refs_4_), channel_id=1, source_target_pairs={{0,1},{1,0},{2,3},{3,2},{4,5},{5,4},{6,7},{7,6},{8,9},{9,8},{10,11... | collective-permute-start | bytes 405512 | tf_op jit(solution)/shard_map/ppermute | solution.py:338
  19.0 0.0 collective-permute-done.5.refs_1_
  19.0 0.3 %gather_first.1 = (f32[256,128]{1,0:T(8,128)S(1)}, f32[256,128]{1,0:T(8,128)S(1)}) custom-call(bf16[32,256,128]{2,1,0:T(8,128)(2,1)S(1)} %get-tuple-element.17.rows_panels, f32[256,128]{1,0:T(8,128)S(1)} %get-tuple-element.18.direct, f32[256,128]{1,0:T(8,128)S(1)} %get-tuple-element.21.mirror, s16[528,128]{1,0:T(8,128)(2,1)S(1)} %collective-permute-done.4.refs_0_, ...), custom_call_target="tpu_custom_call" | custom-call | flops 10000000000 | tf_op jit(solution)/shard_map/gather_first/pallas_call | solution.py:425
  19.4 0.0 collective-permute-done.7.refs_1_
  19.4 0.0 collective-permute-done.9.refs_3_
  19.4 0.6 %gather_most.1.base = f32[256,128]{1,0:T(8,128)S(1)} custom-call(bf16[32,256,128]{2,1,0:T(8,128)(2,1)S(1)} %get-tuple-element.17.rows_panels, f32[256,128]{1,0:T(8,128)S(1)} %get-tuple-element.22.direct, f32[256,128]{1,0:T(8,128)S(1)} %get-tuple-element.23.mirror, s16[528,128]{1,0:T(8,128)(2,1)S(1)} %collective-permute-done.6.refs_0_, ...), custom_call_target="tpu_custom_call" | custom-call | flops 10000000000 | tf_op jit(solution)/shard_map/gather_most/pallas_call | solution.py:425
  20.0 0.1 collective-permute-done.11.message
  20.0 0.9 %gather_last.1 = f32[256,128]{1,0:T(8,128)} custom-call(bf16[32,256,128]{2,1,0:T(8,128)(2,1)S(1)} %get-tuple-element.17.rows_panels, f32[256,128]{1,0:T(8,128)S(1)} %gather_most.1.base, s16[528,128]{1,0:T(8,128)(2,1)S(1)} %collective-permute-done.11.message), custom_call_target="tpu_custom_call" | custom-call | tf_op jit(solution)/shard_map/gather_last/pallas_call | solution.py:452
  (1 shorter events, 0.0 us)
Async XLA Ops:
  0.0 2.5 %copy-start = (bf16[256,128]{1,0:T(8,128)(2,1)S(1)}, bf16[256,128]{1,0:T(8,128)(2,1)}, u32[]{:S(2)}) copy-start(bf16[256,128]{1,0:T(8,128)(2,1)} %own_q.1) | copy-start | bytes 196612
  0.0 2.5 %collective-permute-start.2 = (bf16[18,128,128]{2,1,0:T(8,128)(2,1)}, bf16[18,128,128]{2,1,0:T(8,128)(2,1)S(1)}, u32[]{:S(2)}, u32[]{:S(2)}) collective-permute-start(bf16[18,128,128]{2,1,0:T(8,128)(2,1)} %tiles_ref.3), channel_id=1, source_target_pairs={{0,1},{1,0},{2,3},{3,2},{4,5},{5,4},{6,7},{7,6},{8,9},{9,8},{10,11... | collective-permute-start | bytes 1769480 | tf_op jit(solution)/shard_map/ppermute | solution.py:338
  0.5 2.0 %collective-permute-start.3 = (bf16[256,128]{1,0:T(8,128)(2,1)}, bf16[256,128]{1,0:T(8,128)(2,1)S(1)}, u32[]{:S(2)}, u32[]{:S(2)}) collective-permute-start(bf16[256,128]{1,0:T(8,128)(2,1)} %own_q.1), channel_id=1, source_target_pairs={{0,1},{1,0},{2,3},{3,2},{4,5},{5,4},{6,7},{7,6},{8,9},{9,8},{10,11... | collective-permute-start | bytes 196616 | tf_op jit(solution)/shard_map/ppermute | solution.py:338
  0.5 1.9 %collective-permute-start.1 = (s32[2]{0:T(128)}, s32[2]{0:T(128)S(1)}, u32[]{:S(2)}, u32[]{:S(2)}) collective-permute-start(s32[2]{0:T(128)} %count_ref.3), channel_id=1, source_target_pairs={{0,1},{1,0},{2,3},{3,2},{4,5},{5,4},{6,7},{7,6},{8,9},{9,8},{10,11... | collective-permute-start | bytes 32 | tf_op jit(solution)/shard_map/ppermute | solution.py:338
  1.0 1.5 %collective-permute-start = (s32[2,18]{1,0:T(2,128)}, s32[2,18]{1,0:T(2,128)S(1)}, u32[]{:S(2)}, u32[]{:S(2)}) collective-permute-start(s32[2,18]{1,0:T(2,128)} %bitcast.1), channel_id=1, source_target_pairs={{0,1},{1,0},{2,3},{3,2},{4,5},{5,4},{6,7},{7,6},{8,9},{9,8},{10,11... | collective-permute-start | bytes 440 | tf_op jit(solution)/shard_map/ppermute | solution.py:338
  3.6 7.8 %collective-permute-start.4 = (s16[528,128]{1,0:T(8,128)(2,1)S(1)}, s16[528,128]{1,0:T(8,128)(2,1)S(1)}, u32[]{:S(2)}, u32[]{:S(2)}) collective-permute-start(s16[528,128]{1,0:T(8,128)(2,1)S(1)} %get-tuple-element.20.far_message), channel_id=1, source_target_pairs={{0,12},{1,15},{2,10},{3,9},{4,8},{5,11},{6,14},{7,13},{8,0},{9,3},... | collective-permute-start | bytes 405512 | tf_op jit(solution)/shard_map/ppermute | solution.py:402
  8.1 7.3 %collective-permute-start.6 = (s16[528,128]{1,0:T(8,128)(2,1)S(1)}, s16[528,128]{1,0:T(8,128)(2,1)S(1)}, u32[]{:S(2)}, u32[]{:S(2)}) collective-permute-start(s16[528,128]{1,0:T(8,128)(2,1)S(1)} %get-tuple-element.24), channel_id=1, source_target_pairs={{0,4},{1,7},{2,6},{3,5},{4,0},{5,3},{6,2},{7,1},{8,12},{9,15},{10,... | collective-permute-start | bytes 405512 | tf_op jit(solution)/shard_map/ppermute | solution.py:402
  8.2 9.5 %collective-permute-start.8 = (s16[528,128]{1,0:T(8,128)(2,1)S(1)}, s16[528,128]{1,0:T(8,128)(2,1)S(1)}, u32[]{:S(2)}, u32[]{:S(2)}) collective-permute-start(s16[528,128]{1,0:T(8,128)(2,1)S(1)} %get-tuple-element.25), channel_id=1, source_target_pairs={{1,3},{3,1},{5,7},{7,5},{9,11},{11,9},{13,15},{15,13},{17,19},{19,... | collective-permute-start | bytes 405512 | tf_op jit(solution)/shard_map/ppermute | solution.py:402
  8.9 9.7 %collective-permute-start.10 = (s16[528,128]{1,0:T(8,128)(2,1)S(1)}, s16[528,128]{1,0:T(8,128)(2,1)S(1)}, u32[]{:S(2)}, u32[]{:S(2)}) collective-permute-start(s16[528,128]{1,0:T(8,128)(2,1)S(1)} %get-tuple-element.26), channel_id=1, source_target_pairs={{0,8},{1,11},{2,14},{3,13},{4,12},{5,15},{6,10},{7,9},{8,4},{9,7},... | collective-permute-start | bytes 405512 | tf_op jit(solution)/shard_map/ppermute | solution.py:402
  11.5 7.6 %collective-permute-start.5 = (s16[528,128]{1,0:T(8,128)(2,1)S(1)}, s16[528,128]{1,0:T(8,128)(2,1)S(1)}, u32[]{:S(2)}, u32[]{:S(2)}) collective-permute-start(s16[528,128]{1,0:T(8,128)(2,1)S(1)} %collective-permute-done.4.refs_0_), channel_id=1, source_target_pairs={{0,1},{1,0},{2,3},{3,2},{4,5},{5,4},{6,7},{7,6},{8,9},{9,8},{10,11... | collective-permute-start | bytes 405512 | tf_op jit(solution)/shard_map/ppermute | solution.py:338
  15.4 4.0 %collective-permute-start.7 = (s16[528,128]{1,0:T(8,128)(2,1)S(1)}, s16[528,128]{1,0:T(8,128)(2,1)S(1)}, u32[]{:S(2)}, u32[]{:S(2)}) collective-permute-start(s16[528,128]{1,0:T(8,128)(2,1)S(1)} %collective-permute-done.6.refs_0_), channel_id=1, source_target_pairs={{0,1},{1,0},{2,3},{3,2},{4,5},{5,4},{6,7},{7,6},{8,9},{9,8},{10,11... | collective-permute-start | bytes 405512 | tf_op jit(solution)/shard_map/ppermute | solution.py:338
  17.6 1.7 %collective-permute-start.9 = (s16[528,128]{1,0:T(8,128)(2,1)S(1)}, s16[528,128]{1,0:T(8,128)(2,1)S(1)}, u32[]{:S(2)}, u32[]{:S(2)}) collective-permute-start(s16[528,128]{1,0:T(8,128)(2,1)S(1)} %collective-permute-done.8.refs_2_), channel_id=1, source_target_pairs={{0,1},{1,0},{2,3},{3,2},{4,5},{5,4},{6,7},{7,6},{8,9},{9,8},{10,11... | collective-permute-start | bytes 405512 | tf_op jit(solution)/shard_map/ppermute | solution.py:338
  18.5 1.5 %collective-permute-start.11 = (s16[528,128]{1,0:T(8,128)(2,1)S(1)}, s16[528,128]{1,0:T(8,128)(2,1)S(1)}, u32[]{:S(2)}, u32[]{:S(2)}) collective-permute-start(s16[528,128]{1,0:T(8,128)(2,1)S(1)} %collective-permute-done.10.refs_4_), channel_id=1, source_target_pairs={{0,1},{1,0},{2,3},{3,2},{4,5},{5,4},{6,7},{7,6},{8,9},{9,8},{10,11... | collective-permute-start | bytes 405512 | tf_op jit(solution)/shard_map/ppermute | solution.py:338

commit v12 on v10

--- a/solution.py
+++ b/solution.py
@@ -166,12 +166,15 @@
     rows, tile = own_q.shape[0], tiles.shape[1]
     chip_blocks = 2 * rows // tile
     chip, core = place()
-    chip_q[pl.ds(pl.multiple_of(core * rows, rows), rows), :] = own_q[...]
-    chip_q[pl.ds(pl.multiple_of((1 - core) * rows, rows), rows), :] = other_q[...]
+
+    def keep_q():
+        chip_q[pl.ds(pl.multiple_of(core * rows, rows), rows), :] = own_q[...]
+        chip_q[pl.ds(pl.multiple_of((1 - core) * rows, rows), rows), :] = other_q[...]
 
     @pl.when(in_lower_half(chips))
     def _():
         copies = fetch(sems, (index_ref, index), (count_ref, count))
+        keep_q()
         panels[...] = jnp.zeros_like(panels)
         first = class_of(k, core, True, chip % 2, chips) // 2 * chip_blocks
         mine = mirrored_blocks([(own_q[...].T, own_panels, first)], chip_blocks)
@@ -186,6 +189,7 @@
 
     @pl.when(jnp.logical_not(in_lower_half(chips)))
     def _():
+        keep_q()
         write_message(message, split(chip_q[...].astype(jnp.float32), tile))
 
 
@@ -295,25 +299,37 @@
         base[b * tile:(b + 1) * tile, :] = block + m.T
 
 
-def final_kernel(chips, k, factor, rows_panels, base, message, out, result, sem):
+def final_kernel(chips, k, factor, rows_panels, base, message, out, result, sems):
     tile = rows_panels.shape[2]
     low, cls = is_low(chips, k, False)
+    parts = [pl.ds(at, tile) for at in range(0, result.shape[0], tile)]
+    copies = [
+        pltpu.make_async_copy(result.at[at], out.at[at], sems.at[n])
+        for n, at in enumerate(parts)
+    ]
 
     @pl.when(low)
     def _():
-        for b, x in enumerate(own_half(read_message(message))):
-            at = slice(b * tile, (b + 1) * tile)
+        blocks = own_half(read_message(message))
+        for at, x, copy in zip(parts, blocks, copies, strict=True):
             result[at, :] = (base[at, :] + x.T) * factor
+            copy.start()
 
     @pl.when(jnp.logical_not(low))
     def _():
         blocks = read_message(message)
-        total = direct_sum(rows_panels, cls * len(blocks), blocks)
-        result[...] = (base[...] + total) * factor
-
-    copy = pltpu.make_async_copy(result, out, sem)
-    copy.start()
-    copy.wait()
+        q = jnp.concatenate(blocks, axis=0).astype(jnp.bfloat16)
+        for at, copy in zip(parts, copies, strict=True):
+            row = jnp.concatenate(
+                [rows_panels[cls * len(blocks) + b, at, :] for b in range(len(blocks))],
+                axis=1,
+            )
+            total = jnp.dot(row, q, preferred_element_type=jnp.float32)
+            result[at, :] = (base[at, :] + total) * factor
+            copy.start()
+
+    for copy in copies:
+        copy.wait()
 
 
 VMEM = functools.partial(pl.BlockSpec, memory_space=pltpu.VMEM)
@@ -450,7 +466,10 @@
         out_shape=half_shape,
         in_specs=[VMEM()] * 3,
         out_specs=hbm,
-        scratch_shapes=[pltpu.VMEM((rows, columns), wide), pltpu.SemaphoreType.DMA(())],
+        scratch_shapes=[
+            pltpu.VMEM((rows, columns), wide),
+            pltpu.SemaphoreType.DMA((rows // tile,)),
+        ],
         compiler_params=params,
         name="gather_last",
     )(rows_panels, base, other[last])

time: 21.2 us -> 21.1 us (level)
  no operation moved by 1% of the time
where the time goes in v12:
time: 21.1 us; the launch traced here: 21 us
  starting transfers between devices  13.5 us (64%)
  Pallas kernels  6.27 us (30%)
  waiting for transfers between devices  1.01 us (5%)
    ppermute x4, starting transfers between devices, on_device(): lax.ppermute(messages[k], 'row', [(d, d ^ 2 * cls) for d in range(devices...  7.26 us
    ppermute x8, starting transfers between devices, swap(): return lax.ppermute(x, 'row', other_core)  6.27 us
    pallas_call x1, Pallas kernels, on_device(): pl.pallas_call(direct_kernel, out_shape=[rows_panels_shape, half_shape],...  1.58 us
    pallas_call x1, Pallas kernels, on_device(): pl.pallas_call(own_kernel, out_shape=panels_shape, in_specs=[hbm] * 3, ou...  1.41 us
    pallas_call x1, Pallas kernels, on_device(): pl.pallas_call(functools.partial(far_kernel, chips, far[0]), out_shape=[q...  1 us
    ppermute x4, waiting for transfers between devices, on_device(): lax.ppermute(messages[k], 'row', [(d, d ^ 2 * cls) for d in range(devices...  0.91 us
    pallas_call x1, Pallas kernels, on_device(): pl.pallas_call(functools.partial(final_kernel, chips, last, 1.0 / math.sq...  0.88 us
    pallas_call x2, Pallas kernels, gather(): pl.pallas_call(functools.partial(kernel, chips, sources), out_shape=[half...  0.87 us
  transfers between devices with their start and end apart: 12, of which 3 were waited for; matrix products, arithmetic and copies ran while one was open for 0% of the time, Pallas kernels for 21%

profile of v12, /device:TPU:0, one launch (start us, length us, event | category | flops | bytes accessed | tf_op | source)
XLA Modules:
  0.0 21.0 jit_solution(7196779442230763362)
XLA Ops:
  0.0 0.5 %collective-permute-start.2 = (bf16[18,128,128]{2,1,0:T(8,128)(2,1)}, bf16[18,128,128]{2,1,0:T(8,128)(2,1)S(1)}, u32[]{:S(2)}, u32[]{:S(2)}) collective-permute-start(bf16[18,128,128]{2,1,0:T(8,128)(2,1)} %tiles_ref.3), channel_id=1, source_target_pairs={{0,1},{1,0},{2,3},{3,2},{4,5},{5,4},{6,7},{7,6},{8,9},{9,8},{10,11... | collective-permute-start | bytes 1769480 | tf_op jit(solution)/shard_map/ppermute | solution.py:350
  0.5 0.1 collective-permute-start.3
  0.5 0.4 %collective-permute-start.1 = (s32[2]{0:T(128)}, s32[2]{0:T(128)S(1)}, u32[]{:S(2)}, u32[]{:S(2)}) collective-permute-start(s32[2]{0:T(128)} %count_ref.3), channel_id=1, source_target_pairs={{0,1},{1,0},{2,3},{3,2},{4,5},{5,4},{6,7},{7,6},{8,9},{9,8},{10,11... | collective-permute-start | bytes 32 | tf_op jit(solution)/shard_map/ppermute | solution.py:350
  1.0 0.1 collective-permute-start
  1.0 1.4 %own_tiles.1.own_panels = bf16[21,256,128]{2,1,0:T(8,128)(2,1)S(1)} custom-call(s32[2,18]{1,0:T(2,128)} %bitcast.2, s32[2]{0:T(128)} %count_ref.3, bf16[18,128,128]{2,1,0:T(8,128)(2,1)} %tiles_ref.3), custom_call_target="tpu_custom_call" | custom-call | tf_op jit(solution)/shard_map/own_tiles/pallas_call | solution.py:379
  2.4 0.0 collective-permute-done.1.count_ref
  2.5 0.0 collective-permute-done.index_ref
  2.5 0.0 collective-permute-done.3.other_q
  2.5 0.0 collective-permute-done.2.tiles
  2.5 0.0 copy-done
  2.5 1.0 %pack_far.1 = (bf16[512,128]{1,0:T(8,128)(2,1)S(1)}, s16[528,128]{1,0:T(8,128)(2,1)S(1)}, bf16[21,256,128]{2,1,0:T(8,128)(2,1)S(1)}) custom-call(s32[2,18]{1,0:T(2,128)S(1)} %collective-permute-done.index_ref, s32[2]{0:T(128)S(1)} %collective-permute-done.1.count_ref, bf16[18,128,128]{2,1,0:T(8,128)(2,1)S(1)} %collective-permute-done.2.tiles, ...), custom_call_target="tpu_custom_call" | custom-call | tf_op jit(solution)/shard_map/pack_far/pallas_call | solution.py:394
  3.5 4.1 %collective-permute-start.4 = (s16[528,128]{1,0:T(8,128)(2,1)S(1)}, s16[528,128]{1,0:T(8,128)(2,1)S(1)}, u32[]{:S(2)}, u32[]{:S(2)}) collective-permute-start(s16[528,128]{1,0:T(8,128)(2,1)S(1)} %get-tuple-element.21), channel_id=1, source_target_pairs={{0,12},{1,15},{2,10},{3,9},{4,8},{5,11},{6,14},{7,13},{8,0},{9,3},... | collective-permute-start | bytes 405512 | tf_op jit(solution)/shard_map/ppermute | solution.py:414
  7.6 0.5 %pack_near.1 = (s16[528,128]{1,0:T(8,128)(2,1)S(1)}, s16[528,128]{1,0:T(8,128)(2,1)S(1)}, s16[528,128]{1,0:T(8,128)(2,1)S(1)}, f32[256,128]{1,0:T(8,128)S(1)}) custom-call(s32[2,18]{1,0:T(2,128)S(1)} %collective-permute-done.index_ref, s32[2]{0:T(128)S(1)} %collective-permute-done.1.count_ref, bf16[18,128,128]{2,1,0:T(8,128)(2,1)S(1)} %collective-permute-done.2.tiles, ...), custom_call_target="tpu_custom_call" | custom-call | tf_op jit(solution)/shard_map/pack_near/pallas_call | solution.py:403
  8.1 0.1 collective-permute-start.6
  8.2 0.7 %collective-permute-start.8 = (s16[528,128]{1,0:T(8,128)(2,1)S(1)}, s16[528,128]{1,0:T(8,128)(2,1)S(1)}, u32[]{:S(2)}, u32[]{:S(2)}) collective-permute-start(s16[528,128]{1,0:T(8,128)(2,1)S(1)} %get-tuple-element.25), channel_id=1, source_target_pairs={{1,3},{3,1},{5,7},{7,5},{9,11},{11,9},{13,15},{15,13},{17,19},{19,... | collective-permute-start | bytes 405512 | tf_op jit(solution)/shard_map/ppermute | solution.py:414
  8.9 2.5 %collective-permute-start.10 = (s16[528,128]{1,0:T(8,128)(2,1)S(1)}, s16[528,128]{1,0:T(8,128)(2,1)S(1)}, u32[]{:S(2)}, u32[]{:S(2)}) collective-permute-start(s16[528,128]{1,0:T(8,128)(2,1)S(1)} %get-tuple-element.26), channel_id=1, source_target_pairs={{0,8},{1,11},{2,14},{3,13},{4,12},{5,15},{6,10},{7,9},{8,4},{9,7},... | collective-permute-start | bytes 405512 | tf_op jit(solution)/shard_map/ppermute | solution.py:414
  11.3 0.2 collective-permute-done.4.refs_0_
  11.5 2.5 %collective-permute-start.5 = (s16[528,128]{1,0:T(8,128)(2,1)S(1)}, s16[528,128]{1,0:T(8,128)(2,1)S(1)}, u32[]{:S(2)}, u32[]{:S(2)}) collective-permute-start(s16[528,128]{1,0:T(8,128)(2,1)S(1)} %collective-permute-done.4.refs_0_), channel_id=1, source_target_pairs={{0,1},{1,0},{2,3},{3,2},{4,5},{5,4},{6,7},{7,6},{8,9},{9,8},{10,11... | collective-permute-start | bytes 405512 | tf_op jit(solution)/shard_map/ppermute | solution.py:350
  13.9 1.6 %direct_local.1 = (bf16[32,256,128]{2,1,0:T(8,128)(2,1)S(1)}, f32[256,128]{1,0:T(8,128)S(1)}) custom-call(s32[2,18]{1,0:T(2,128)} %bitcast.3, s32[2]{0:T(128)} %count_ref.3, bf16[18,128,128]{2,1,0:T(8,128)(2,1)} %tiles_ref.3, bf16[512,128]{1,0:T(8,128)(2,1)S(1)} %get-tuple-element.16.chip_q), custom_call_target="tpu_custom_call" | custom-call | flops 10000000000 | tf_op jit(solution)/shard_map/direct_local/pallas_call | solution.py:422
  15.5 0.0 collective-permute-done.6.refs_0_
  15.5 2.3 %collective-permute-start.7 = (s16[528,128]{1,0:T(8,128)(2,1)S(1)}, s16[528,128]{1,0:T(8,128)(2,1)S(1)}, u32[]{:S(2)}, u32[]{:S(2)}) collective-permute-start(s16[528,128]{1,0:T(8,128)(2,1)S(1)} %collective-permute-done.6.refs_0_), channel_id=1, source_target_pairs={{0,1},{1,0},{2,3},{3,2},{4,5},{5,4},{6,7},{7,6},{8,9},{9,8},{10,11... | collective-permute-start | bytes 405512 | tf_op jit(solution)/shard_map/ppermute | solution.py:350
  17.8 0.0 collective-permute-done.8.refs_2_
  17.8 0.0 collective-permute-start.9
  17.8 0.8 %collective-permute-done.10.refs_4_ = s16[528,128]{1,0:T(8,128)(2,1)S(1)} collective-permute-done((s16[528,128]{1,0:T(8,128)(2,1)S(1)}, s16[528,128]{1,0:T(8,128)(2,1)S(1)}, u32[]{:S(2)}, u32[]{:S(2)}) %collective-permute-start.10) | collective-permute-done | bytes 135200 | tf_op jit(solution)/shard_map/ppermute | solution.py:414
  18.6 0.5 %collective-permute-start.11 = (s16[528,128]{1,0:T(8,128)(2,1)S(1)}, s16[528,128]{1,0:T(8,128)(2,1)S(1)}, u32[]{:S(2)}, u32[]{:S(2)}) collective-permute-start(s16[528,128]{1,0:T(8,128)(2,1)S(1)} %collective-permute-done.10.refs_4_), channel_id=1, source_target_pairs={{0,1},{1,0},{2,3},{3,2},{4,5},{5,4},{6,7},{7,6},{8,9},{9,8},{10,11... | collective-permute-start | bytes 405512 | tf_op jit(solution)/shard_map/ppermute | solution.py:350
  19.1 0.0 collective-permute-done.5.refs_1_
  19.1 0.3 %gather_first.1 = (f32[256,128]{1,0:T(8,128)S(1)}, f32[256,128]{1,0:T(8,128)S(1)}) custom-call(bf16[32,256,128]{2,1,0:T(8,128)(2,1)S(1)} %get-tuple-element.17.rows_panels, f32[256,128]{1,0:T(8,128)S(1)} %get-tuple-element.18.direct, f32[256,128]{1,0:T(8,128)S(1)} %get-tuple-element.20.mirror, s16[528,128]{1,0:T(8,128)(2,1)S(1)} %collective-permute-done.4.refs_0_, ...), custom_call_target="tpu_custom_call" | custom-call | flops 10000000000 | tf_op jit(solution)/shard_map/gather_first/pallas_call | solution.py:437
  19.4 0.0 collective-permute-done.7.refs_1_
  19.4 0.0 collective-permute-done.9.refs_3_
  19.4 0.6 %gather_most.1.base = f32[256,128]{1,0:T(8,128)S(1)} custom-call(bf16[32,256,128]{2,1,0:T(8,128)(2,1)S(1)} %get-tuple-element.17.rows_panels, f32[256,128]{1,0:T(8,128)S(1)} %get-tuple-element.22.direct, f32[256,128]{1,0:T(8,128)S(1)} %get-tuple-element.23.mirror, s16[528,128]{1,0:T(8,128)(2,1)S(1)} %collective-permute-done.6.refs_0_, ...), custom_call_target="tpu_custom_call" | custom-call | flops 10000000000 | tf_op jit(solution)/shard_map/gather_most/pallas_call | solution.py:437
  20.0 0.1 collective-permute-done.11.message
  20.1 0.9 %gather_last.1 = f32[256,128]{1,0:T(8,128)} custom-call(bf16[32,256,128]{2,1,0:T(8,128)(2,1)S(1)} %get-tuple-element.17.rows_panels, f32[256,128]{1,0:T(8,128)S(1)} %gather_most.1.base, s16[528,128]{1,0:T(8,128)(2,1)S(1)} %collective-permute-done.11.message), custom_call_target="tpu_custom_call" | custom-call | tf_op jit(solution)/shard_map/gather_last/pallas_call | solution.py:464
  (1 shorter events, 0.0 us)
Async XLA Ops:
  0.0 2.5 %copy-start = (bf16[256,128]{1,0:T(8,128)(2,1)S(1)}, bf16[256,128]{1,0:T(8,128)(2,1)}, u32[]{:S(2)}) copy-start(bf16[256,128]{1,0:T(8,128)(2,1)} %own_q.1) | copy-start | bytes 196612
  0.0 2.5 %collective-permute-start.2 = (bf16[18,128,128]{2,1,0:T(8,128)(2,1)}, bf16[18,128,128]{2,1,0:T(8,128)(2,1)S(1)}, u32[]{:S(2)}, u32[]{:S(2)}) collective-permute-start(bf16[18,128,128]{2,1,0:T(8,128)(2,1)} %tiles_ref.3), channel_id=1, source_target_pairs={{0,1},{1,0},{2,3},{3,2},{4,5},{5,4},{6,7},{7,6},{8,9},{9,8},{10,11... | collective-permute-start | bytes 1769480 | tf_op jit(solution)/shard_map/ppermute | solution.py:350
  0.5 2.0 %collective-permute-start.3 = (bf16[256,128]{1,0:T(8,128)(2,1)}, bf16[256,128]{1,0:T(8,128)(2,1)S(1)}, u32[]{:S(2)}, u32[]{:S(2)}) collective-permute-start(bf16[256,128]{1,0:T(8,128)(2,1)} %own_q.1), channel_id=1, source_target_pairs={{0,1},{1,0},{2,3},{3,2},{4,5},{5,4},{6,7},{7,6},{8,9},{9,8},{10,11... | collective-permute-start | bytes 196616 | tf_op jit(solution)/shard_map/ppermute | solution.py:350
  0.5 1.9 %collective-permute-start.1 = (s32[2]{0:T(128)}, s32[2]{0:T(128)S(1)}, u32[]{:S(2)}, u32[]{:S(2)}) collective-permute-start(s32[2]{0:T(128)} %count_ref.3), channel_id=1, source_target_pairs={{0,1},{1,0},{2,3},{3,2},{4,5},{5,4},{6,7},{7,6},{8,9},{9,8},{10,11... | collective-permute-start | bytes 32 | tf_op jit(solution)/shard_map/ppermute | solution.py:350
  1.0 1.5 %collective-permute-start = (s32[2,18]{1,0:T(2,128)}, s32[2,18]{1,0:T(2,128)S(1)}, u32[]{:S(2)}, u32[]{:S(2)}) collective-permute-start(s32[2,18]{1,0:T(2,128)} %bitcast.1), channel_id=1, source_target_pairs={{0,1},{1,0},{2,3},{3,2},{4,5},{5,4},{6,7},{7,6},{8,9},{9,8},{10,11... | collective-permute-start | bytes 440 | tf_op jit(solution)/shard_map/ppermute | solution.py:350
  3.5 8.0 %collective-permute-start.4 = (s16[528,128]{1,0:T(8,128)(2,1)S(1)}, s16[528,128]{1,0:T(8,128)(2,1)S(1)}, u32[]{:S(2)}, u32[]{:S(2)}) collective-permute-start(s16[528,128]{1,0:T(8,128)(2,1)S(1)} %get-tuple-element.21), channel_id=1, source_target_pairs={{0,12},{1,15},{2,10},{3,9},{4,8},{5,11},{6,14},{7,13},{8,0},{9,3},... | collective-permute-start | bytes 405512 | tf_op jit(solution)/shard_map/ppermute | solution.py:414
  8.1 7.4 %collective-permute-start.6 = (s16[528,128]{1,0:T(8,128)(2,1)S(1)}, s16[528,128]{1,0:T(8,128)(2,1)S(1)}, u32[]{:S(2)}, u32[]{:S(2)}) collective-permute-start(s16[528,128]{1,0:T(8,128)(2,1)S(1)} %get-tuple-element.24), channel_id=1, source_target_pairs={{0,4},{1,7},{2,6},{3,5},{4,0},{5,3},{6,2},{7,1},{8,12},{9,15},{10,... | collective-permute-start | bytes 405512 | tf_op jit(solution)/shard_map/ppermute | solution.py:414
  8.2 9.6 %collective-permute-start.8 = (s16[528,128]{1,0:T(8,128)(2,1)S(1)}, s16[528,128]{1,0:T(8,128)(2,1)S(1)}, u32[]{:S(2)}, u32[]{:S(2)}) collective-permute-start(s16[528,128]{1,0:T(8,128)(2,1)S(1)} %get-tuple-element.25), channel_id=1, source_target_pairs={{1,3},{3,1},{5,7},{7,5},{9,11},{11,9},{13,15},{15,13},{17,19},{19,... | collective-permute-start | bytes 405512 | tf_op jit(solution)/shard_map/ppermute | solution.py:414
  8.9 9.7 %collective-permute-start.10 = (s16[528,128]{1,0:T(8,128)(2,1)S(1)}, s16[528,128]{1,0:T(8,128)(2,1)S(1)}, u32[]{:S(2)}, u32[]{:S(2)}) collective-permute-start(s16[528,128]{1,0:T(8,128)(2,1)S(1)} %get-tuple-element.26), channel_id=1, source_target_pairs={{0,8},{1,11},{2,14},{3,13},{4,12},{5,15},{6,10},{7,9},{8,4},{9,7},... | collective-permute-start | bytes 405512 | tf_op jit(solution)/shard_map/ppermute | solution.py:414
  11.5 7.6 %collective-permute-start.5 = (s16[528,128]{1,0:T(8,128)(2,1)S(1)}, s16[528,128]{1,0:T(8,128)(2,1)S(1)}, u32[]{:S(2)}, u32[]{:S(2)}) collective-permute-start(s16[528,128]{1,0:T(8,128)(2,1)S(1)} %collective-permute-done.4.refs_0_), channel_id=1, source_target_pairs={{0,1},{1,0},{2,3},{3,2},{4,5},{5,4},{6,7},{7,6},{8,9},{9,8},{10,11... | collective-permute-start | bytes 405512 | tf_op jit(solution)/shard_map/ppermute | solution.py:350
  15.5 3.9 %collective-permute-start.7 = (s16[528,128]{1,0:T(8,128)(2,1)S(1)}, s16[528,128]{1,0:T(8,128)(2,1)S(1)}, u32[]{:S(2)}, u32[]{:S(2)}) collective-permute-start(s16[528,128]{1,0:T(8,128)(2,1)S(1)} %collective-permute-done.6.refs_0_), channel_id=1, source_target_pairs={{0,1},{1,0},{2,3},{3,2},{4,5},{5,4},{6,7},{7,6},{8,9},{9,8},{10,11... | collective-permute-start | bytes 405512 | tf_op jit(solution)/shard_map/ppermute | solution.py:350
  17.8 1.6 %collective-permute-start.9 = (s16[528,128]{1,0:T(8,128)(2,1)S(1)}, s16[528,128]{1,0:T(8,128)(2,1)S(1)}, u32[]{:S(2)}, u32[]{:S(2)}) collective-permute-start(s16[528,128]{1,0:T(8,128)(2,1)S(1)} %collective-permute-done.8.refs_2_), channel_id=1, source_target_pairs={{0,1},{1,0},{2,3},{3,2},{4,5},{5,4},{6,7},{7,6},{8,9},{9,8},{10,11... | collective-permute-start | bytes 405512 | tf_op jit(solution)/shard_map/ppermute | solution.py:350
  18.6 1.5 %collective-permute-start.11 = (s16[528,128]{1,0:T(8,128)(2,1)S(1)}, s16[528,128]{1,0:T(8,128)(2,1)S(1)}, u32[]{:S(2)}, u32[]{:S(2)}) collective-permute-start(s16[528,128]{1,0:T(8,128)(2,1)S(1)} %collective-permute-done.10.refs_4_), channel_id=1, source_target_pairs={{0,1},{1,0},{2,3},{3,2},{4,5},{5,4},{6,7},{7,6},{8,9},{9,8},{10,11... | collective-permute-start | bytes 405512 | tf_op jit(solution)/shard_map/ppermute | solution.py:350
